TPU v7x, 256 devices: a whole 4x4x8 slice. The times are simulated.
256 devices in a mesh: rows: 16 (over z_lo, y, core), near: 4 (over z_hi), far: 4 (over x).
Axes of the slice: x: 4, y: 4, z: 8 (z_hi: 4, z_lo: 2; z = z_hi * 2 + z_lo), core: 2. Of those that a mesh axis runs over, the one named last changes fastest.
Arguments:
- diag_block: float32 [512, 512], replicated, as said below
- history_rows: float32 [512, 24576], P('rows', ('near', 'far'))
- panel_below: float32 [16384, 512], P(('rows', 'near', 'far')), may hold values from -6 to 6
- history_below: float32 [16384, 24576], P('rows', ('near', 'far')), may hold values from -6 to 6
Outputs:
- panel_factor: float32 [16384, 512], P(('rows', 'near', 'far'))
- diag_factor: float32 [512, 512], replicated
Inputs may be any that keep to these rules, and one draw needn't show every extreme that they name: diag_block minus history_rows history_rows^T is symmetric with a dominant positive diagonal.
All inputs are finite; a program needn't handle non-finite values.
Results may differ from a plain program's by a relative error of at most 0.000067.
Values sent between devices are 32-bit elements; how exact they have to be, the bound alone decides.
No kernel may reach another device: no remote copies, remote signals or barrier semaphores. Data moves between devices by JAX's collectives and lax.ppermute only.
A program may use at most 64 MiB of HBM per device.

v0:
```python
import functools

import jax
import jax.numpy as jnp
from jax import lax
from jax.experimental import pallas as pl
from jax.experimental.pallas import tpu as pltpu
from jax.sharding import PartitionSpec as P

F32, BF16 = jnp.float32, jnp.bfloat16
NT = (((1,), (1,)), ((), ()))
NN = (((1,), (0,)), ((), ()))
VMEM = pl.BlockSpec(memory_space=pltpu.VMEM)
SMEM = pl.BlockSpec(memory_space=pltpu.SMEM)


def split(x):
    hi = x.astype(BF16)
    return hi, (x - hi.astype(F32)).astype(BF16)


def dot3(a, b, dims):
    d = lambda x, y: lax.dot_general(x, y, dims, preferred_element_type=F32)
    return d(a[0], b[1]) + d(a[1], b[0]) + d(a[0], b[0])


def call(kernel, out_shape, in_specs, args, scratch=(), flops=0, moved=0, vmem=16, aliases=()):
    outs = jax.tree.map(lambda _: VMEM, out_shape)
    return pl.pallas_call(
        kernel,
        out_shape=out_shape,
        in_specs=in_specs,
        out_specs=outs,
        scratch_shapes=list(scratch),
        input_output_aliases=dict(aliases),
        cost_estimate=pl.CostEstimate(flops=flops, bytes_accessed=moved, transcendentals=0),
        compiler_params=pltpu.CompilerParams(vmem_limit_bytes=vmem * 2**20),
    )(*args)


def at_rows(me, z, y_step, core_step, size):
    place = z * 8 + lax.rem(me ^ (y_step * 2 + core_step), 8)
    return pl.ds(pl.multiple_of(place * size, size), size)


def slot_of(shape, size):
    return lax.rem(lax.broadcasted_iota(jnp.int32, shape, 1) // (2 * size), 4)


def schur_kernel(me_ref, *refs):
    pieces, (out_ref, hi_ref, lo_ref) = refs[:6], refs[6:]
    me = me_ref[0]
    size = pieces[0].shape[0] // 2
    for core_step in range(2):
        for i, y_step in enumerate((0, 1, 3)):
            hi, lo = split(pieces[core_step * 3 + i][...])
            for z in range(2):
                part = slice(z * size, (z + 1) * size)
                for slot in (y_step, 2) if y_step == 3 else (y_step,):
                    at = at_rows(me, z, slot, core_step, size)
                    hi_ref[at, :] = hi[part]
                    lo_ref[at, :] = lo[part]
    left = split(jnp.concatenate([pieces[0][...], pieces[1][...]], 0))
    both = dot3(left, (hi_ref[...], lo_ref[...]), NT)
    here, near = both[:2 * size], both[2 * size:]
    y = lax.rem(me // 2, 4)
    out_ref[...] = jnp.where(slot_of(here.shape, size) == (y ^ 2), near, here)


def complete_kernel(me_ref, *refs):
    pieces, (hi_ref, lo_ref) = refs[:4], refs[6:]
    me = me_ref[0]
    size = pieces[0].shape[0]
    for core_step in range(2):
        for z in range(2):
            at = at_rows(me, z, 2, core_step, size)
            hi_ref[at, :], lo_ref[at, :] = split(pieces[core_step * 2 + z][...])


def product_kernel(step, at_ref, below_ref, hi_ref, lo_ref, out_ref):
    near, far = at_ref[0], at_ref[1] ^ step
    rows = jnp.concatenate([below_ref[near ^ j, far] for j in range(below_ref.shape[0])], 0)
    out_ref[...] = dot3(split(rows), (hi_ref[...], lo_ref[...]), NT)


def product(at, step, below, hi, lo):
    near_n, far_n, share, depth = below.shape
    panel = hi.shape[0]
    return call(
        functools.partial(product_kernel, step),
        jax.ShapeDtypeStruct((near_n * share, panel), F32),
        [SMEM] + [VMEM] * 3,
        [at, below, hi, lo],
        flops=11 * near_n * share * depth * panel,
        moved=6 * 2**20,
    )


def recip(x):
    r = pl.reciprocal(x, approx=True)
    return r * (2.0 - x * r)


def factor_block(rows, nb, sc):
    groups = len(rows)
    lane = lax.broadcasted_iota(jnp.int32, (8, nb), 1)
    sub = lax.broadcasted_iota(jnp.int32, (8, nb), 0)
    rows = list(rows)
    inv = [jnp.where(lane == sub + 8 * g, 1.0, 0.0) for g in range(groups)]
    bc = lambda x, k: jnp.broadcast_to(x[k:k + 1, :], (8, nb))
    col = lambda g, t, k: jnp.broadcast_to(rows[g][:, 8 * t + k:8 * t + k + 1], (8, nb))

    def stack(parts):
        out = parts[7]
        for k in range(7):
            out = jnp.where(sub == k, parts[k], out)
        return out

    for t in range(groups):
        own = [col(t, t, k) for k in range(8)]
        p = t % 2
        for m in range(8):
            sc[p, m] = own[m]
        sc[p, 8] = rows[t]
        sc[p, 9] = inv[t]
        lb = lambda m, s: jnp.broadcast_to(sc[p, m, s:s + 1, :], (8, nb))
        e = [[lb(m, s) for m in range(s + 1)] for s in range(8)]
        u = [lb(8, k) for k in range(8)]
        v = [lb(9, k) for k in range(8)]
        diag, pairs = [], []
        for k in range(0, 8, 2):
            a, b, c = e[k][k], e[k + 1][k], e[k + 1][k + 1]
            det = a * c - b * b
            ra, rd = recip(a), recip(det)
            r1 = a * rd
            diag += [a, det * ra]
            low = b * ra
            u[k + 1] = u[k + 1] - low * u[k]
            v[k + 1] = v[k + 1] - low * v[k]
            for s in range(k + 2, 8):
                l0 = e[s][k] * ra
                e[s][k + 1] = e[s][k + 1] - l0 * b
                l1 = e[s][k + 1] * r1
                for m in range(k + 2, s + 1):
                    e[s][m] = (e[s][m] - l0 * e[m][k]) - l1 * e[m][k + 1]
                u[s] = (u[s] - l0 * u[k]) - l1 * u[k + 1]
                v[s] = (v[s] - l0 * v[k]) - l1 * v[k + 1]
            pairs.append((ra, r1))
        for g in range(t + 1, min(t + 1 + 3, groups)):
            f = [col(g, t, k) for k in range(8)]
            for k in range(0, 8, 2):
                ra, r1 = pairs[k // 2]
                f0 = f[k] * ra
                f1 = (f[k + 1] - f0 * e[k + 1][k]) * r1
                for m in range(k + 2, 8):
                    f[m] = (f[m] - f0 * e[m][k]) - f1 * e[m][k + 1]
                rows[g] = (rows[g] - f0 * u[k]) - f1 * u[k + 1]
                inv[g] = (inv[g] - f0 * v[k]) - f1 * v[k + 1]
        scale = lax.rsqrt(stack(diag))
        rows[t] = jnp.where(lane >= sub + 8 * t, stack(u) * scale, 0.0)
        inv[t] = stack(v) * scale
        if t + 1 + 3 < groups:
            both = jnp.concatenate([rows[t], inv[t]], 1)
            hi = both.astype(BF16).astype(F32)
            lo = both - hi
            left = jnp.concatenate([hi[:, :nb], lo[:, :nb], hi[:, :nb], lo[:, :nb]], 0).astype(BF16)
            right = jnp.concatenate([hi, hi, lo, lo], 0).astype(BF16)
            step = lax.dot_general(left, right, (((0,), (0,)), ((), ())), preferred_element_type=F32)
            for g in range(t + 1 + 3, groups):
                rows[g] = rows[g] - step[8 * g:8 * g + 8, :nb]
                inv[g] = inv[g] - step[8 * g:8 * g + 8, nb:]
    return rows, inv


def factor_columns(first, count, w_ref, l_ref, x_ref, sc_ref):
    n = w_ref.shape[0]
    nb = 128
    blk = lambda i: slice(i * nb, (i + 1) * nb)
    for b in range(first, first + count):
        rows = [w_ref[b * nb + 8 * g:b * nb + 8 * g + 8, blk(b)] for g in range(nb // 8)]
        up, inv = factor_block(rows, nb, sc_ref)
        x11 = jnp.concatenate(inv, 0)
        l_ref[blk(b), blk(b)] = jnp.concatenate(up, 0).T
        x_ref[blk(b), blk(b)] = x11
        if (b + 1) * nb < n:
            rest = slice((b + 1) * nb, n)
            l21 = dot3(split(w_ref[rest, blk(b)]), split(x11), NT)
            l_ref[rest, blk(b)] = l21
            ls = split(l21)
            w_ref[rest, rest] = w_ref[rest, rest] - dot3(ls, ls, NT)
        if b > 0:
            done = slice(0, b * nb)
            t = dot3(split(l_ref[blk(b), done]), split(x_ref[done, done]), NN)
            x_ref[blk(b), done] = -dot3(split(x11), split(t), NN)


def leading_kernel(me_ref, diag_ref, *refs):
    pieces, (w_ref, l_ref, x_ref, sc_ref) = refs[:8], refs[8:]
    me = me_ref[0]
    size = pieces[0].shape[0] // 2
    y = lax.rem(me // 2, 4)
    for core_step in range(2):
        for y_step in range(4):
            own = pieces[core_step * 4 + y_step][...]
            other = pieces[core_step * 4 + (y_step ^ 1)][...]
            tiles = [other[:, i:i + 128] for i in range(0, other.shape[1], 128)]
            other = jnp.concatenate([pltpu.roll(t, 64, 1) for t in tiles], 1)
            whole = jnp.where(slot_of(own.shape, size) == (y ^ y_step ^ 2), other, own)
            for z in range(2):
                at = at_rows(me, z, y_step, core_step, size)
                w_ref[at, :] = diag_ref[at, :] - whole[z * size:(z + 1) * size]
    l_ref[...] = jnp.zeros_like(l_ref)
    x_ref[...] = jnp.zeros_like(x_ref)
    factor_columns(0, w_ref.shape[0] // 128 - 1, w_ref, l_ref, x_ref, sc_ref)


def last_kernel(w_in, l_in, x_in, l_ref, x_ref, w_ref, sc_ref):
    w_ref[...] = w_in[...]
    l_ref[...] = l_in[...]
    x_ref[...] = x_in[...]
    factor_columns(w_ref.shape[0] // 128 - 1, 1, w_ref, l_ref, x_ref, sc_ref)


def final_kernel(below_ref, p0, p1, p2, p3, x_ref, out_ref):
    updated = below_ref[...] - ((p0[...] + p1[...]) + (p2[...] + p3[...]))
    out_ref[...] = dot3(split(updated), split(x_ref[...]), NT)


def swap(x, axis, size, step):
    return lax.ppermute(x, axis, [(i, i ^ step) for i in range(size)])


def tree(a, b, c, d):
    return (a + b) + (c + d)


def sum_near(x, rows_n, near_n):
    half = rows_n // 2

    def move(source):
        pairs = []
        for r in range(rows_n):
            z, rest = divmod(r, half)
            for n in range(near_n):
                m, w = source(n, z)
                pairs.append(((w * half + rest) * near_n + m % near_n, r * near_n + n))
        return lax.ppermute(x, ("rows", "near"), pairs)

    far_off = move(lambda n, z: (n + 2, 1 - z))
    next_1 = move(lambda n, z: (n + 2 * z - 1, 1 - z))
    next_2 = move(lambda n, z: (n + 1 - 2 * z, z))
    return (x + far_off) + (next_1 + next_2)


def body(sizes, diag_block, history_rows, panel_below, history_below):
    rows_n, near_n, far_n = sizes
    panel = diag_block.shape[0]
    mine, depth = history_rows.shape
    share = panel_below.shape[0]
    place = lax.axis_index("rows")
    me = place.reshape(1)
    at = jnp.stack([lax.axis_index("near"), lax.axis_index("far")])
    core = lambda x: swap(x, "rows", rows_n, 1)
    along_y = lambda x, k: swap(x, "rows", rows_n, 2 * k)
    other_z = swap(history_rows, "rows", rows_n, 8)
    low = place < rows_n // 2
    pair = jnp.concatenate([jnp.where(low, history_rows, other_z), jnp.where(low, other_z, history_rows)], 0)
    y1, y3 = along_y(pair, 1), along_y(pair, 3)
    close = [pair, y1, y3]
    close_other = [core(x) for x in close]
    gathered = jax.ShapeDtypeStruct((panel, depth), BF16)
    schur_part, hi, lo = call(
        schur_kernel,
        (jax.ShapeDtypeStruct((2 * mine, panel), F32), gathered, gathered),
        [SMEM] + [VMEM] * 6,
        [me] + close + close_other,
        flops=24 * mine * depth * panel,
        moved=8 * panel * depth,
    )
    y2 = [along_y(y3[:mine], 1), along_y(y1[mine:], 3)]
    *y2_late, _ = lax.optimization_barrier((*y2, schur_part))
    by_far = [swap(schur_part, "far", far_n, k) for k in (1, 2, 3)]
    hi, lo = call(
        complete_kernel,
        (gathered, gathered),
        [SMEM] + [VMEM] * 6,
        [me] + y2_late + [core(x) for x in y2_late] + [hi, lo],
        moved=2 * panel * depth,
        aliases=((5, 0), (6, 1)),
    )
    below = history_below.reshape(near_n, far_n, share, depth)
    parts = [product(at, k, below, hi, lo) for k in (0, 1, 2, 3)]
    schur_part = tree(schur_part, *by_far)
    schur_part = sum_near(schur_part, rows_n, near_n)
    schur_pieces = [schur_part] + [along_y(schur_part, k) for k in (1, 2, 3)]
    schur_pieces = schur_pieces + [core(x) for x in schur_pieces]
    parts = [parts[0]] + [swap(parts[k], "far", far_n, k) for k in (1, 2, 3)]
    quarter = lambda p, j: p[j * share:(j + 1) * share]
    sums = [tree(*[quarter(p, j) for p in parts]) for j in range(near_n)]
    square = jax.ShapeDtypeStruct((panel, panel), F32)
    broadcasts = pltpu.VMEM((2, 10, 8, 128), F32)
    leading = call(
        leading_kernel,
        (square,) * 3,
        [SMEM] + [VMEM] * 9,
        [me, diag_block] + schur_pieces,
        scratch=[broadcasts],
        flops=96 * panel**3,
        moved=16 * panel * panel,
    )
    *leading, sums[1], sums[2], sums[3] = lax.optimization_barrier((*leading, *sums[1:]))
    sums = [sums[0]] + [swap(sums[j], "near", near_n, j) for j in (1, 2, 3)]
    diag_factor, inverse = call(
        last_kernel,
        (square,) * 2,
        [VMEM] * 3,
        leading,
        scratch=[pltpu.VMEM((panel, panel), F32), broadcasts],
        flops=24 * panel**3,
        moved=16 * panel * panel,
    )
    panel_factor = call(
        final_kernel,
        jax.ShapeDtypeStruct((share, panel), F32),
        [VMEM] * 6,
        [panel_below] + sums + [inverse],
        flops=6 * share * panel * panel,
        moved=8 * panel * panel,
    )
    return (panel_factor, diag_factor)


def solution(mesh):
    sizes = tuple(mesh.shape[name] for name in ("rows", "near", "far"))
    return jax.shard_map(
        functools.partial(body, sizes),
        mesh=mesh,
        in_specs=(
            P(),
            P("rows", ("near", "far")),
            P(("rows", "near", "far"), None),
            P("rows", ("near", "far")),
        ),
        out_specs=(P(("rows", "near", "far"), None), P()),
        check_vma=False,
    )
```

profile of v0, /device:TPU:1, one launch (start us, length us, event | category | flops | bytes accessed | tf_op | source)
XLA Modules:
  0.0 115.2 jit_solution(12482072500468617329)
XLA Ops:
  0.6 2.6 %collective-permute-start = (f32[32,1536]{1,0:T(8,128)}, f32[32,1536]{1,0:T(8,128)S(1)}, u32[]{:S(2)}, u32[]{:S(2)}) collective-permute-start(f32[32,1536]{1,0:T(8,128)} %param.5), channel_id=1, source_target_pairs={{0,128},{16,144},{32,160},{48,176},{64,192},{80,208},{96,224},{112... | collective-permute-start | bytes 589832 | tf_op jit(solution)/shard_map/ppermute | solution.py:230
  3.2 3.9 %collective-permute-done = f32[32,1536]{1,0:T(8,128)S(1)} collective-permute-done((f32[32,1536]{1,0:T(8,128)}, f32[32,1536]{1,0:T(8,128)S(1)}, u32[]{:S(2)}, u32[]{:S(2)}) %collective-permute-start) | collective-permute-done | bytes 196640 | tf_op jit(solution)/shard_map/ppermute | solution.py:230
  7.1 1.0 broadcast_select_fusion.1
  8.1 2.2 %collective-permute-start.3 = (f32[64,1536]{1,0:T(8,128)S(1)}, f32[64,1536]{1,0:T(8,128)S(1)}, u32[]{:S(2)}, u32[]{:S(2)}) collective-permute-start(f32[64,1536]{1,0:T(8,128)S(1)} %pad_maximum_fusion.refs_0_), channel_id=1, source_target_pairs={{0,32},{16,48},{32,0},{48,16},{64,96},{80,112},{96,64},{112,80},{1... | collective-permute-start | bytes 1179656 | tf_op jit(solution)/shard_map/ppermute | solution.py:230
  10.3 1.9 %collective-permute-start.1 = (f32[64,1536]{1,0:T(8,128)S(1)}, f32[64,1536]{1,0:T(8,128)S(1)}, u32[]{:S(2)}, u32[]{:S(2)}) collective-permute-start(f32[64,1536]{1,0:T(8,128)S(1)} %pad_maximum_fusion.refs_0_), channel_id=1, source_target_pairs={{0,96},{16,112},{32,64},{48,80},{64,32},{80,48},{96,0},{112,16},{1... | collective-permute-start | bytes 1179656 | tf_op jit(solution)/shard_map/ppermute | solution.py:230
  12.2 1.9 %collective-permute-start.5 = (f32[64,1536]{1,0:T(8,128)S(1)}, f32[64,1536]{1,0:T(8,128)S(1)}, u32[]{:S(2)}, u32[]{:S(2)}) collective-permute-start(f32[64,1536]{1,0:T(8,128)S(1)} %pad_maximum_fusion.refs_0_), channel_id=1, source_target_pairs={{0,16},{16,0},{32,48},{48,32},{64,80},{80,64},{96,112},{112,96},{1... | collective-permute-start | bytes 1179656 | tf_op jit(solution)/shard_map/ppermute | solution.py:230
  14.1 3.2 %collective-permute-done.3.refs_1_ = f32[64,1536]{1,0:T(8,128)S(1)} collective-permute-done((f32[64,1536]{1,0:T(8,128)S(1)}, f32[64,1536]{1,0:T(8,128)S(1)}, u32[]{:S(2)}, u32[]{:S(2)}) %collective-permute-start.3) | collective-permute-done | bytes 393248 | tf_op jit(solution)/shard_map/ppermute | solution.py:230
  17.3 3.0 %collective-permute-start.6 = (f32[64,1536]{1,0:T(8,128)S(1)}, f32[64,1536]{1,0:T(8,128)S(1)}, u32[]{:S(2)}, u32[]{:S(2)}) collective-permute-start(f32[64,1536]{1,0:T(8,128)S(1)} %collective-permute-done.3.refs_1_), channel_id=1, source_target_pairs={{0,16},{16,0},{32,48},{48,32},{64,80},{80,64},{96,112},{112,96},{1... | collective-permute-start | bytes 1179656 | tf_op jit(solution)/shard_map/ppermute | solution.py:230
  20.4 0.1 collective-permute-done.1.refs_2_
  20.5 2.6 %collective-permute-start.7 = (f32[64,1536]{1,0:T(8,128)S(1)}, f32[64,1536]{1,0:T(8,128)S(1)}, u32[]{:S(2)}, u32[]{:S(2)}) collective-permute-start(f32[64,1536]{1,0:T(8,128)S(1)} %collective-permute-done.1.refs_2_), channel_id=1, source_target_pairs={{0,16},{16,0},{32,48},{48,32},{64,80},{80,64},{96,112},{112,96},{1... | collective-permute-start | bytes 1179656 | tf_op jit(solution)/shard_map/ppermute | solution.py:230
  23.0 0.7 slice.72
  23.7 0.0 collective-permute-start.2
  23.7 0.7 slice.73
  24.4 1.9 %collective-permute-start.4 = (f32[32,1536]{1,0:T(8,128)}, f32[32,1536]{1,0:T(8,128)S(1)}, u32[]{:S(2)}, u32[]{:S(2)}) collective-permute-start(f32[32,1536]{1,0:T(8,128)} %slice.73), channel_id=1, source_target_pairs={{0,96},{16,112},{32,64},{48,80},{64,32},{80,48},{96,0},{112,16},{1... | collective-permute-start | bytes 589832 | tf_op jit(solution)/shard_map/ppermute | solution.py:230
  26.3 0.0 collective-permute-done.5.refs_3_
  26.3 0.0 collective-permute-done.6.refs_4_
  26.3 0.0 collective-permute-done.7.refs_5_
  26.3 2.8 %shard_map.59 = (f32[64,512]{1,0:T(8,128)}, bf16[512,1536]{1,0:T(8,128)(2,1)S(1)}, bf16[512,1536]{1,0:T(8,128)(2,1)S(1)}) custom-call(s32[1]{0:T(128)} %bitcast.3.me_ref, f32[64,1536]{1,0:T(8,128)S(1)} %pad_maximum_fusion.refs_0_, f32[64,1536]{1,0:T(8,128)S(1)} %collective-permute-done.3.refs_1_, f32[64,1536]{1,0:T(8,128)S(1)} %collective-permute-done.1.refs_2_, ...), custom_call_target="tpu_custom_call" | custom-call | flops 603979776 | bytes 6291456 | tf_op jit(solution)/shard_map/pallas_call | solution.py:29
  29.1 2.7 %collective-permute-start.14 = (f32[64,512]{1,0:T(8,128)}, f32[64,512]{1,0:T(8,128)}, u32[]{:S(2)}, u32[]{:S(2)}) collective-permute-start(f32[64,512]{1,0:T(8,128)} %get-tuple-element.20), channel_id=1, source_target_pairs={{0,2},{1,3},{2,0},{3,1},{4,6},{5,7},{6,4},{7,5},{8,10},{9,11},{10,... | collective-permute-start | bytes 393224 | tf_op jit(solution)/shard_map/ppermute | solution.py:230
  31.9 0.9 collective-permute-start.15
  32.7 0.0 collective-permute-start.13
  32.8 0.1 pad_add_fusion.at_ref
  32.8 0.0 collective-permute-done.2.refs_0_
  32.8 0.0 collective-permute-done.4.refs_1_
  32.8 1.0 collective-permute-start.8
  33.8 0.1 collective-permute-start.9
  33.9 1.8 %collective-permute-done.14 = f32[64,512]{1,0:T(8,128)} collective-permute-done((f32[64,512]{1,0:T(8,128)}, f32[64,512]{1,0:T(8,128)}, u32[]{:S(2)}, u32[]{:S(2)}) %collective-permute-start.14) | collective-permute-done | bytes 131104 | tf_op jit(solution)/shard_map/ppermute | solution.py:230
  35.7 2.9 %collective-permute-done.15 = f32[64,512]{1,0:T(8,128)} collective-permute-done((f32[64,512]{1,0:T(8,128)}, f32[64,512]{1,0:T(8,128)}, u32[]{:S(2)}, u32[]{:S(2)}) %collective-permute-start.15) | collective-permute-done | bytes 131104 | tf_op jit(solution)/shard_map/ppermute | solution.py:230
  38.5 0.0 collective-permute-done.13
  38.6 1.1 add_add_fusion.1
  39.7 5.3 %collective-permute-start.17 = (f32[64,512]{1,0:T(8,128)S(1)}, f32[64,512]{1,0:T(8,128)S(1)}, u32[]{:S(2)}, u32[]{:S(2)}) collective-permute-start(f32[64,512]{1,0:T(8,128)S(1)} %add_add_fusion.1), channel_id=1, source_target_pairs={{140,0},{128,4},{132,8},{136,12},{156,16},{144,20},{148,24},{152,2... | collective-permute-start | bytes 393224 | tf_op jit(solution)/shard_map/ppermute | solution.py:247
  45.0 1.2 %collective-permute-start.18 = (f32[64,512]{1,0:T(8,128)S(1)}, f32[64,512]{1,0:T(8,128)S(1)}, u32[]{:S(2)}, u32[]{:S(2)}) collective-permute-start(f32[64,512]{1,0:T(8,128)S(1)} %add_add_fusion.1), channel_id=1, source_target_pairs={{4,0},{8,4},{12,8},{0,12},{20,16},{24,20},{28,24},{16,28},{36,32},... | collective-permute-start | bytes 393224 | tf_op jit(solution)/shard_map/ppermute | solution.py:247
  46.2 1.0 collective-permute-start.16
  47.2 0.1 shard_map.60
  47.3 0.0 copy-start
  47.3 2.8 %copy-done = f32[1024,1536]{1,0:T(8,128)S(1)} copy-done((f32[1024,1536]{1,0:T(8,128)S(1)}, f32[1024,1536]{1,0:T(8,128)}, u32[]{:S(2)}) %copy-start) | copy-done | bytes 6291480
  50.1 2.0 %shard_map.64 = f32[256,512]{1,0:T(8,128)S(1)} custom-call(s32[2]{0:T(128)S(1)} %pad_add_fusion.at_ref, f32[4,4,64,1536]{3,2,1,0:T(8,128)S(1)} %bitcast.4, bf16[512,1536]{1,0:T(8,128)(2,1)S(1)} %get-tuple-element.25.hi_ref, bf16[512,1536]{1,0:T(8,128)(2,1)S(1)} %get-tuple-element.26.lo_ref), custom_call_target="tpu_custom_call" | custom-call | flops 2214592512 | bytes 6291456 | tf_op jit(solution)/shard_map/pallas_call | solution.py:29
  52.1 3.3 %collective-permute-start.12 = (f32[256,512]{1,0:T(8,128)S(1)}, f32[256,512]{1,0:T(8,128)S(1)}, u32[]{:S(2)}, u32[]{:S(2)}) collective-permute-start(f32[256,512]{1,0:T(8,128)S(1)} %shard_map.64), channel_id=1, source_target_pairs={{0,3},{1,2},{2,1},{3,0},{4,7},{5,6},{6,5},{7,4},{8,11},{9,10},{10,... | collective-permute-start | bytes 1572872 | tf_op jit(solution)/shard_map/ppermute | solution.py:230
  55.5 2.0 %shard_map.63 = f32[256,512]{1,0:T(8,128)S(1)} custom-call(s32[2]{0:T(128)S(1)} %pad_add_fusion.at_ref, f32[4,4,64,1536]{3,2,1,0:T(8,128)S(1)} %bitcast.5, bf16[512,1536]{1,0:T(8,128)(2,1)S(1)} %get-tuple-element.25.hi_ref, bf16[512,1536]{1,0:T(8,128)(2,1)S(1)} %get-tuple-element.26.lo_ref), custom_call_target="tpu_custom_call" | custom-call | flops 2214592512 | bytes 6291456 | tf_op jit(solution)/shard_map/pallas_call | solution.py:29
  57.6 1.0 collective-permute-start.19
  58.5 1.1 collective-permute-start.20
  59.6 1.9 %collective-permute-start.21 = (f32[64,512]{1,0:T(8,128)S(1)}, f32[64,512]{1,0:T(8,128)S(1)}, u32[]{:S(2)}, u32[]{:S(2)}) collective-permute-start(f32[64,512]{1,0:T(8,128)S(1)} %add_add_fusion.refs_0_), channel_id=1, source_target_pairs={{0,96},{16,112},{32,64},{48,80},{64,32},{80,48},{96,0},{112,16},{1... | collective-permute-start | bytes 393224 | tf_op jit(solution)/shard_map/ppermute | solution.py:230
  61.5 2.0 %shard_map.62 = f32[256,512]{1,0:T(8,128)S(1)} custom-call(s32[2]{0:T(128)S(1)} %pad_add_fusion.at_ref, f32[4,4,64,1536]{3,2,1,0:T(8,128)S(1)} %bitcast.6, bf16[512,1536]{1,0:T(8,128)(2,1)S(1)} %get-tuple-element.25.hi_ref, bf16[512,1536]{1,0:T(8,128)(2,1)S(1)} %get-tuple-element.26.lo_ref), custom_call_target="tpu_custom_call" | custom-call | flops 2214592512 | bytes 6291456 | tf_op jit(solution)/shard_map/pallas_call | solution.py:29
  63.5 0.0 copy-start.2
  63.5 2.3 %collective-permute-start.22 = (f32[64,512]{1,0:T(8,128)S(1)}, f32[64,512]{1,0:T(8,128)S(1)}, u32[]{:S(2)}, u32[]{:S(2)}) collective-permute-start(f32[64,512]{1,0:T(8,128)S(1)} %add_add_fusion.refs_0_), channel_id=1, source_target_pairs={{0,16},{16,0},{32,48},{48,32},{64,80},{80,64},{96,112},{112,96},{1... | collective-permute-start | bytes 393224 | tf_op jit(solution)/shard_map/ppermute | solution.py:230
  65.8 0.1 collective-permute-start.23
  65.9 1.5 %collective-permute-start.24 = (f32[64,512]{1,0:T(8,128)S(1)}, f32[64,512]{1,0:T(8,128)S(1)}, u32[]{:S(2)}, u32[]{:S(2)}) collective-permute-start(f32[64,512]{1,0:T(8,128)S(1)} %collective-permute-done.20.refs_2_), channel_id=1, source_target_pairs={{0,16},{16,0},{32,48},{48,32},{64,80},{80,64},{96,112},{112,96},{1... | collective-permute-start | bytes 393224 | tf_op jit(solution)/shard_map/ppermute | solution.py:230
  67.4 0.3 collective-permute-done.21.refs_3_
  67.6 1.5 %collective-permute-start.25 = (f32[64,512]{1,0:T(8,128)S(1)}, f32[64,512]{1,0:T(8,128)S(1)}, u32[]{:S(2)}, u32[]{:S(2)}) collective-permute-start(f32[64,512]{1,0:T(8,128)S(1)} %collective-permute-done.21.refs_3_), channel_id=1, source_target_pairs={{0,16},{16,0},{32,48},{48,32},{64,80},{80,64},{96,112},{112,96},{1... | collective-permute-start | bytes 393224 | tf_op jit(solution)/shard_map/ppermute | solution.py:230
  69.1 2.0 %shard_map.61 = f32[256,512]{1,0:T(8,128)S(1)} custom-call(s32[2]{0:T(128)S(1)} %pad_add_fusion.at_ref, f32[4,4,64,1536]{3,2,1,0:T(8,128)S(1)} %bitcast.7, bf16[512,1536]{1,0:T(8,128)(2,1)S(1)} %get-tuple-element.25.hi_ref, bf16[512,1536]{1,0:T(8,128)(2,1)S(1)} %get-tuple-element.26.lo_ref), custom_call_target="tpu_custom_call" | custom-call | flops 2214592512 | bytes 6291456 | tf_op jit(solution)/shard_map/pallas_call | solution.py:29
  71.2 0.6 collective-permute-start.11
  71.8 1.2 %collective-permute-start.10 = (f32[256,512]{1,0:T(8,128)S(1)}, f32[256,512]{1,0:T(8,128)S(1)}, u32[]{:S(2)}, u32[]{:S(2)}) collective-permute-start(f32[256,512]{1,0:T(8,128)S(1)} %shard_map.62), channel_id=1, source_target_pairs={{0,1},{1,0},{2,3},{3,2},{4,5},{5,4},{6,7},{7,6},{8,9},{9,8},{10,11... | collective-permute-start | bytes 1572872 | tf_op jit(solution)/shard_map/ppermute | solution.py:230
  73.0 10.8 %shard_map.65 = (f32[512,512]{1,0:T(8,128)S(1)}, f32[512,512]{1,0:T(8,128)S(1)}, f32[512,512]{1,0:T(8,128)S(1)}) custom-call(s32[1]{0:T(128)} %bitcast.3.me_ref, f32[512,512]{1,0:T(8,128)S(1)} %copy-done.2, f32[64,512]{1,0:T(8,128)S(1)} %add_add_fusion.refs_0_, f32[64,512]{1,0:T(8,128)S(1)} %collective-permute-done.19.refs_1_, ...), custom_call_target="tpu_custom_call" | custom-call | flops 12884901888 | bytes 4194304 | tf_op jit(solution)/shard_map/pallas_call | solution.py:29
  83.9 2.4 %collective-permute-done.11 = f32[256,512]{1,0:T(8,128)S(1)} collective-permute-done((f32[256,512]{1,0:T(8,128)S(1)}, f32[256,512]{1,0:T(8,128)S(1)}, u32[]{:S(2)}, u32[]{:S(2)}) %collective-permute-start.11) | collective-permute-done | bytes 524320 | tf_op jit(solution)/shard_map/ppermute | solution.py:230
  86.3 10.0 %collective-permute-done.10 = f32[256,512]{1,0:T(8,128)S(1)} collective-permute-done((f32[256,512]{1,0:T(8,128)S(1)}, f32[256,512]{1,0:T(8,128)S(1)}, u32[]{:S(2)}, u32[]{:S(2)}) %collective-permute-start.10) | collective-permute-done | bytes 524320 | tf_op jit(solution)/shard_map/ppermute | solution.py:230
  96.3 0.2 fusion
  96.6 0.0 copy-start.1
  96.6 3.3 %collective-permute-start.26 = (f32[64,512]{1,0:T(8,128)S(1)}, f32[64,512]{1,0:T(8,128)S(1)}, u32[]{:S(2)}, u32[]{:S(2)}) collective-permute-start(f32[64,512]{1,0:T(8,128)S(1)} %get-tuple-element.30), channel_id=1, source_target_pairs={{0,4},{4,0},{8,12},{12,8},{1,5},{5,1},{9,13},{13,9},{2,6},{6,2},{1... | collective-permute-start | bytes 393224 | tf_op jit(solution)/shard_map/ppermute | solution.py:230
  99.9 3.8 %collective-permute-start.27 = (f32[64,512]{1,0:T(8,128)S(1)}, f32[64,512]{1,0:T(8,128)S(1)}, u32[]{:S(2)}, u32[]{:S(2)}) collective-permute-start(f32[64,512]{1,0:T(8,128)S(1)} %get-tuple-element.31), channel_id=1, source_target_pairs={{0,8},{4,12},{8,0},{12,4},{1,9},{5,13},{9,1},{13,5},{2,10},{6,14},... | collective-permute-start | bytes 393224 | tf_op jit(solution)/shard_map/ppermute | solution.py:230
  103.7 0.0 collective-permute-start.28
  103.7 4.0 %shard_map.66 = (f32[512,512]{1,0:T(8,128)}, f32[512,512]{1,0:T(8,128)S(1)}) custom-call(f32[512,512]{1,0:T(8,128)S(1)} %get-tuple-element.33.w_in, f32[512,512]{1,0:T(8,128)S(1)} %get-tuple-element.34.l_in, f32[512,512]{1,0:T(8,128)S(1)} %get-tuple-element.35.x_in), custom_call_target="tpu_custom_call" | custom-call | flops 3221225472 | bytes 4194304 | tf_op jit(solution)/shard_map/pallas_call | solution.py:29
  107.8 4.8 %collective-permute-done.27.p2 = f32[64,512]{1,0:T(8,128)S(1)} collective-permute-done((f32[64,512]{1,0:T(8,128)S(1)}, f32[64,512]{1,0:T(8,128)S(1)}, u32[]{:S(2)}, u32[]{:S(2)}) %collective-permute-start.27) | collective-permute-done | bytes 131104 | tf_op jit(solution)/shard_map/ppermute | solution.py:230
  112.5 1.4 %collective-permute-done.28.p3 = f32[64,512]{1,0:T(8,128)S(1)} collective-permute-done((f32[64,512]{1,0:T(8,128)S(1)}, f32[64,512]{1,0:T(8,128)S(1)}, u32[]{:S(2)}, u32[]{:S(2)}) %collective-permute-start.28) | collective-permute-done | bytes 131104 | tf_op jit(solution)/shard_map/ppermute | solution.py:230
  113.9 1.3 %shard_map.67 = f32[64,512]{1,0:T(8,128)} custom-call(f32[64,512]{1,0:T(8,128)S(1)} %copy-done.1, f32[64,512]{1,0:T(8,128)S(1)} %get-tuple-element.41.p0, f32[64,512]{1,0:T(8,128)S(1)} %collective-permute-done.26.p1, f32[64,512]{1,0:T(8,128)S(1)} %collective-permute-done.27.p2, f32[64,512]{1,0:T(8,128)S(1)} %collective-permute-done.28.p3, ...), custom_call_target="tpu_custom_call" | custom-call | flops 100663296 | bytes 2097152 | tf_op jit(solution)/shard_map/pallas_call | solution.py:29
  (17 shorter events, 0.1 us)
Async XLA Ops:
  0.6 6.4 %collective-permute-start = (f32[32,1536]{1,0:T(8,128)}, f32[32,1536]{1,0:T(8,128)S(1)}, u32[]{:S(2)}, u32[]{:S(2)}) collective-permute-start(f32[32,1536]{1,0:T(8,128)} %param.5), channel_id=1, source_target_pairs={{0,128},{16,144},{32,160},{48,176},{64,192},{80,208},{96,224},{112... | collective-permute-start | bytes 589832 | tf_op jit(solution)/shard_map/ppermute | solution.py:230
  8.1 9.3 %collective-permute-start.3 = (f32[64,1536]{1,0:T(8,128)S(1)}, f32[64,1536]{1,0:T(8,128)S(1)}, u32[]{:S(2)}, u32[]{:S(2)}) collective-permute-start(f32[64,1536]{1,0:T(8,128)S(1)} %pad_maximum_fusion.refs_0_), channel_id=1, source_target_pairs={{0,32},{16,48},{32,0},{48,16},{64,96},{80,112},{96,64},{112,80},{1... | collective-permute-start | bytes 1179656 | tf_op jit(solution)/shard_map/ppermute | solution.py:230
  10.3 10.2 %collective-permute-start.1 = (f32[64,1536]{1,0:T(8,128)S(1)}, f32[64,1536]{1,0:T(8,128)S(1)}, u32[]{:S(2)}, u32[]{:S(2)}) collective-permute-start(f32[64,1536]{1,0:T(8,128)S(1)} %pad_maximum_fusion.refs_0_), channel_id=1, source_target_pairs={{0,96},{16,112},{32,64},{48,80},{64,32},{80,48},{96,0},{112,16},{1... | collective-permute-start | bytes 1179656 | tf_op jit(solution)/shard_map/ppermute | solution.py:230
  12.2 14.1 %collective-permute-start.5 = (f32[64,1536]{1,0:T(8,128)S(1)}, f32[64,1536]{1,0:T(8,128)S(1)}, u32[]{:S(2)}, u32[]{:S(2)}) collective-permute-start(f32[64,1536]{1,0:T(8,128)S(1)} %pad_maximum_fusion.refs_0_), channel_id=1, source_target_pairs={{0,16},{16,0},{32,48},{48,32},{64,80},{80,64},{96,112},{112,96},{1... | collective-permute-start | bytes 1179656 | tf_op jit(solution)/shard_map/ppermute | solution.py:230
  17.3 9.0 %collective-permute-start.6 = (f32[64,1536]{1,0:T(8,128)S(1)}, f32[64,1536]{1,0:T(8,128)S(1)}, u32[]{:S(2)}, u32[]{:S(2)}) collective-permute-start(f32[64,1536]{1,0:T(8,128)S(1)} %collective-permute-done.3.refs_1_), channel_id=1, source_target_pairs={{0,16},{16,0},{32,48},{48,32},{64,80},{80,64},{96,112},{112,96},{1... | collective-permute-start | bytes 1179656 | tf_op jit(solution)/shard_map/ppermute | solution.py:230
  20.5 5.8 %collective-permute-start.7 = (f32[64,1536]{1,0:T(8,128)S(1)}, f32[64,1536]{1,0:T(8,128)S(1)}, u32[]{:S(2)}, u32[]{:S(2)}) collective-permute-start(f32[64,1536]{1,0:T(8,128)S(1)} %collective-permute-done.1.refs_2_), channel_id=1, source_target_pairs={{0,16},{16,0},{32,48},{48,32},{64,80},{80,64},{96,112},{112,96},{1... | collective-permute-start | bytes 1179656 | tf_op jit(solution)/shard_map/ppermute | solution.py:230
  23.7 9.1 %collective-permute-start.2 = (f32[32,1536]{1,0:T(8,128)}, f32[32,1536]{1,0:T(8,128)S(1)}, u32[]{:S(2)}, u32[]{:S(2)}) collective-permute-start(f32[32,1536]{1,0:T(8,128)} %slice.72), channel_id=1, source_target_pairs={{0,32},{16,48},{32,0},{48,16},{64,96},{80,112},{96,64},{112,80},{1... | collective-permute-start | bytes 589832 | tf_op jit(solution)/shard_map/ppermute | solution.py:230
  24.4 8.4 %collective-permute-start.4 = (f32[32,1536]{1,0:T(8,128)}, f32[32,1536]{1,0:T(8,128)S(1)}, u32[]{:S(2)}, u32[]{:S(2)}) collective-permute-start(f32[32,1536]{1,0:T(8,128)} %slice.73), channel_id=1, source_target_pairs={{0,96},{16,112},{32,64},{48,80},{64,32},{80,48},{96,0},{112,16},{1... | collective-permute-start | bytes 589832 | tf_op jit(solution)/shard_map/ppermute | solution.py:230
  29.1 6.5 %collective-permute-start.14 = (f32[64,512]{1,0:T(8,128)}, f32[64,512]{1,0:T(8,128)}, u32[]{:S(2)}, u32[]{:S(2)}) collective-permute-start(f32[64,512]{1,0:T(8,128)} %get-tuple-element.20), channel_id=1, source_target_pairs={{0,2},{1,3},{2,0},{3,1},{4,6},{5,7},{6,4},{7,5},{8,10},{9,11},{10,... | collective-permute-start | bytes 393224 | tf_op jit(solution)/shard_map/ppermute | solution.py:230
  31.9 6.7 %collective-permute-start.15 = (f32[64,512]{1,0:T(8,128)}, f32[64,512]{1,0:T(8,128)}, u32[]{:S(2)}, u32[]{:S(2)}) collective-permute-start(f32[64,512]{1,0:T(8,128)} %get-tuple-element.20), channel_id=1, source_target_pairs={{0,3},{1,2},{2,1},{3,0},{4,7},{5,6},{6,5},{7,4},{8,11},{9,10},{10,... | collective-permute-start | bytes 393224 | tf_op jit(solution)/shard_map/ppermute | solution.py:230
  32.7 5.8 %collective-permute-start.13 = (f32[64,512]{1,0:T(8,128)}, f32[64,512]{1,0:T(8,128)}, u32[]{:S(2)}, u32[]{:S(2)}) collective-permute-start(f32[64,512]{1,0:T(8,128)} %get-tuple-element.20), channel_id=1, source_target_pairs={{0,1},{1,0},{2,3},{3,2},{4,5},{5,4},{6,7},{7,6},{8,9},{9,8},{10,11... | collective-permute-start | bytes 393224 | tf_op jit(solution)/shard_map/ppermute | solution.py:230
  32.8 14.4 %collective-permute-start.8 = (f32[32,1536]{1,0:T(8,128)S(1)}, f32[32,1536]{1,0:T(8,128)S(1)}, u32[]{:S(2)}, u32[]{:S(2)}) collective-permute-start(f32[32,1536]{1,0:T(8,128)S(1)} %collective-permute-done.2.refs_0_), channel_id=1, source_target_pairs={{0,16},{16,0},{32,48},{48,32},{64,80},{80,64},{96,112},{112,96},{1... | collective-permute-start | bytes 589832 | tf_op jit(solution)/shard_map/ppermute | solution.py:230
  33.8 13.4 %collective-permute-start.9 = (f32[32,1536]{1,0:T(8,128)S(1)}, f32[32,1536]{1,0:T(8,128)S(1)}, u32[]{:S(2)}, u32[]{:S(2)}) collective-permute-start(f32[32,1536]{1,0:T(8,128)S(1)} %collective-permute-done.4.refs_1_), channel_id=1, source_target_pairs={{0,16},{16,0},{32,48},{48,32},{64,80},{80,64},{96,112},{112,96},{1... | collective-permute-start | bytes 589832 | tf_op jit(solution)/shard_map/ppermute | solution.py:230
  39.7 17.8 %collective-permute-start.17 = (f32[64,512]{1,0:T(8,128)S(1)}, f32[64,512]{1,0:T(8,128)S(1)}, u32[]{:S(2)}, u32[]{:S(2)}) collective-permute-start(f32[64,512]{1,0:T(8,128)S(1)} %add_add_fusion.1), channel_id=1, source_target_pairs={{140,0},{128,4},{132,8},{136,12},{156,16},{144,20},{148,24},{152,2... | collective-permute-start | bytes 393224 | tf_op jit(solution)/shard_map/ppermute | solution.py:247
  45.0 12.5 %collective-permute-start.18 = (f32[64,512]{1,0:T(8,128)S(1)}, f32[64,512]{1,0:T(8,128)S(1)}, u32[]{:S(2)}, u32[]{:S(2)}) collective-permute-start(f32[64,512]{1,0:T(8,128)S(1)} %add_add_fusion.1), channel_id=1, source_target_pairs={{4,0},{8,4},{12,8},{0,12},{20,16},{24,20},{28,24},{16,28},{36,32},... | collective-permute-start | bytes 393224 | tf_op jit(solution)/shard_map/ppermute | solution.py:247
  46.2 11.3 %collective-permute-start.16 = (f32[64,512]{1,0:T(8,128)S(1)}, f32[64,512]{1,0:T(8,128)S(1)}, u32[]{:S(2)}, u32[]{:S(2)}) collective-permute-start(f32[64,512]{1,0:T(8,128)S(1)} %add_add_fusion.1), channel_id=1, source_target_pairs={{136,0},{140,4},{128,8},{132,12},{152,16},{156,20},{144,24},{148,2... | collective-permute-start | bytes 393224 | tf_op jit(solution)/shard_map/ppermute | solution.py:247
  47.3 2.8 %copy-start = (f32[1024,1536]{1,0:T(8,128)S(1)}, f32[1024,1536]{1,0:T(8,128)}, u32[]{:S(2)}) copy-start(f32[1024,1536]{1,0:T(8,128)} %param.7) | copy-start | bytes 18874372
  52.1 31.7 %collective-permute-start.12 = (f32[256,512]{1,0:T(8,128)S(1)}, f32[256,512]{1,0:T(8,128)S(1)}, u32[]{:S(2)}, u32[]{:S(2)}) collective-permute-start(f32[256,512]{1,0:T(8,128)S(1)} %shard_map.64), channel_id=1, source_target_pairs={{0,3},{1,2},{2,1},{3,0},{4,7},{5,6},{6,5},{7,4},{8,11},{9,10},{10,... | collective-permute-start | bytes 1572872 | tf_op jit(solution)/shard_map/ppermute | solution.py:230
  57.6 8.2 %collective-permute-start.19 = (f32[64,512]{1,0:T(8,128)S(1)}, f32[64,512]{1,0:T(8,128)S(1)}, u32[]{:S(2)}, u32[]{:S(2)}) collective-permute-start(f32[64,512]{1,0:T(8,128)S(1)} %add_add_fusion.refs_0_), channel_id=1, source_target_pairs={{0,32},{16,48},{32,0},{48,16},{64,96},{80,112},{96,64},{112,80},{1... | collective-permute-start | bytes 393224 | tf_op jit(solution)/shard_map/ppermute | solution.py:230
  58.5 7.4 %collective-permute-start.20 = (f32[64,512]{1,0:T(8,128)S(1)}, f32[64,512]{1,0:T(8,128)S(1)}, u32[]{:S(2)}, u32[]{:S(2)}) collective-permute-start(f32[64,512]{1,0:T(8,128)S(1)} %add_add_fusion.refs_0_), channel_id=1, source_target_pairs={{0,64},{16,80},{32,96},{48,112},{64,0},{80,16},{96,32},{112,48},{1... | collective-permute-start | bytes 393224 | tf_op jit(solution)/shard_map/ppermute | solution.py:230
  59.6 8.0 %collective-permute-start.21 = (f32[64,512]{1,0:T(8,128)S(1)}, f32[64,512]{1,0:T(8,128)S(1)}, u32[]{:S(2)}, u32[]{:S(2)}) collective-permute-start(f32[64,512]{1,0:T(8,128)S(1)} %add_add_fusion.refs_0_), channel_id=1, source_target_pairs={{0,96},{16,112},{32,64},{48,80},{64,32},{80,48},{96,0},{112,16},{1... | collective-permute-start | bytes 393224 | tf_op jit(solution)/shard_map/ppermute | solution.py:230
  63.5 9.5 %copy-start.2 = (f32[512,512]{1,0:T(8,128)S(1)}, f32[512,512]{1,0:T(8,128)}, u32[]{:S(2)}) copy-start(f32[512,512]{1,0:T(8,128)} %diag_ref.1) | copy-start | bytes 3145732
  63.5 7.6 %collective-permute-start.22 = (f32[64,512]{1,0:T(8,128)S(1)}, f32[64,512]{1,0:T(8,128)S(1)}, u32[]{:S(2)}, u32[]{:S(2)}) collective-permute-start(f32[64,512]{1,0:T(8,128)S(1)} %add_add_fusion.refs_0_), channel_id=1, source_target_pairs={{0,16},{16,0},{32,48},{48,32},{64,80},{80,64},{96,112},{112,96},{1... | collective-permute-start | bytes 393224 | tf_op jit(solution)/shard_map/ppermute | solution.py:230
  65.8 6.0 %collective-permute-start.23 = (f32[64,512]{1,0:T(8,128)S(1)}, f32[64,512]{1,0:T(8,128)S(1)}, u32[]{:S(2)}, u32[]{:S(2)}) collective-permute-start(f32[64,512]{1,0:T(8,128)S(1)} %collective-permute-done.19.refs_1_), channel_id=1, source_target_pairs={{0,16},{16,0},{32,48},{48,32},{64,80},{80,64},{96,112},{112,96},{1... | collective-permute-start | bytes 393224 | tf_op jit(solution)/shard_map/ppermute | solution.py:230
  65.9 7.1 %collective-permute-start.24 = (f32[64,512]{1,0:T(8,128)S(1)}, f32[64,512]{1,0:T(8,128)S(1)}, u32[]{:S(2)}, u32[]{:S(2)}) collective-permute-start(f32[64,512]{1,0:T(8,128)S(1)} %collective-permute-done.20.refs_2_), channel_id=1, source_target_pairs={{0,16},{16,0},{32,48},{48,32},{64,80},{80,64},{96,112},{112,96},{1... | collective-permute-start | bytes 393224 | tf_op jit(solution)/shard_map/ppermute | solution.py:230
  67.6 5.4 %collective-permute-start.25 = (f32[64,512]{1,0:T(8,128)S(1)}, f32[64,512]{1,0:T(8,128)S(1)}, u32[]{:S(2)}, u32[]{:S(2)}) collective-permute-start(f32[64,512]{1,0:T(8,128)S(1)} %collective-permute-done.21.refs_3_), channel_id=1, source_target_pairs={{0,16},{16,0},{32,48},{48,32},{64,80},{80,64},{96,112},{112,96},{1... | collective-permute-start | bytes 393224 | tf_op jit(solution)/shard_map/ppermute | solution.py:230
  71.2 15.1 %collective-permute-start.11 = (f32[256,512]{1,0:T(8,128)S(1)}, f32[256,512]{1,0:T(8,128)S(1)}, u32[]{:S(2)}, u32[]{:S(2)}) collective-permute-start(f32[256,512]{1,0:T(8,128)S(1)} %shard_map.63), channel_id=1, source_target_pairs={{0,2},{1,3},{2,0},{3,1},{4,6},{5,7},{6,4},{7,5},{8,10},{9,11},{10,... | collective-permute-start | bytes 1572872 | tf_op jit(solution)/shard_map/ppermute | solution.py:230
  71.8 24.6 %collective-permute-start.10 = (f32[256,512]{1,0:T(8,128)S(1)}, f32[256,512]{1,0:T(8,128)S(1)}, u32[]{:S(2)}, u32[]{:S(2)}) collective-permute-start(f32[256,512]{1,0:T(8,128)S(1)} %shard_map.62), channel_id=1, source_target_pairs={{0,1},{1,0},{2,3},{3,2},{4,5},{5,4},{6,7},{7,6},{8,9},{9,8},{10,11... | collective-permute-start | bytes 1572872 | tf_op jit(solution)/shard_map/ppermute | solution.py:230
  96.6 17.3 %copy-start.1 = (f32[64,512]{1,0:T(8,128)S(1)}, f32[64,512]{1,0:T(8,128)}, u32[]{:S(2)}) copy-start(f32[64,512]{1,0:T(8,128)} %below_ref.1) | copy-start | bytes 393220
  96.6 11.2 %collective-permute-start.26 = (f32[64,512]{1,0:T(8,128)S(1)}, f32[64,512]{1,0:T(8,128)S(1)}, u32[]{:S(2)}, u32[]{:S(2)}) collective-permute-start(f32[64,512]{1,0:T(8,128)S(1)} %get-tuple-element.30), channel_id=1, source_target_pairs={{0,4},{4,0},{8,12},{12,8},{1,5},{5,1},{9,13},{13,9},{2,6},{6,2},{1... | collective-permute-start | bytes 393224 | tf_op jit(solution)/shard_map/ppermute | solution.py:230
  99.9 12.6 %collective-permute-start.27 = (f32[64,512]{1,0:T(8,128)S(1)}, f32[64,512]{1,0:T(8,128)S(1)}, u32[]{:S(2)}, u32[]{:S(2)}) collective-permute-start(f32[64,512]{1,0:T(8,128)S(1)} %get-tuple-element.31), channel_id=1, source_target_pairs={{0,8},{4,12},{8,0},{12,4},{1,9},{5,13},{9,1},{13,5},{2,10},{6,14},... | collective-permute-start | bytes 393224 | tf_op jit(solution)/shard_map/ppermute | solution.py:230
  103.7 10.2 %collective-permute-start.28 = (f32[64,512]{1,0:T(8,128)S(1)}, f32[64,512]{1,0:T(8,128)S(1)}, u32[]{:S(2)}, u32[]{:S(2)}) collective-permute-start(f32[64,512]{1,0:T(8,128)S(1)} %get-tuple-element.32), channel_id=1, source_target_pairs={{0,12},{4,8},{8,4},{12,0},{1,13},{5,9},{9,5},{13,1},{2,14},{6,10},... | collective-permute-start | bytes 393224 | tf_op jit(solution)/shard_map/ppermute | solution.py:230
where the time goes:
time: 116 us; the launch traced here: 115 us
  starting transfers between devices  49.7 us (43%)
  waiting for transfers between devices  30.9 us (27%)
  Pallas kernels  27.1 us (23%)
  local copies, waits for them, and re-layouts  4.16 us (4%)
  other arithmetic  2.46 us (2%)
    ppermute x26, starting transfers between devices, swap(): return lax.ppermute(x, axis, [(i, i ^ step) for i in range(size)])  42.3 us
    ppermute x26, waiting for transfers between devices, swap(): return lax.ppermute(x, axis, [(i, i ^ step) for i in range(size)])  30.9 us
    pallas_call x9, Pallas kernels, call(): pl.pallas_call(kernel, out_shape=out_shape, in_specs=in_specs, out_specs=...  27.1 us
    ppermute x3, starting transfers between devices, move(): return lax.ppermute(x, ('rows', 'near'), pairs)  7.48 us
    unnamed x6, local copies, waits for them, and re-layouts  2.79 us
  transfers between devices with their start and end apart: 29, of which 10 were waited for; matrix products, arithmetic and copies ran while one was open for 2% of the time, Pallas kernels for 22%

commit v1 on v0

--- a/solution.py
+++ b/solution.py
@@ -12,6 +12,7 @@
 NN = (((1,), (0,)), ((), ()))
 VMEM = pl.BlockSpec(memory_space=pltpu.VMEM)
 SMEM = pl.BlockSpec(memory_space=pltpu.SMEM)
+PRODUCT_VMEM = 45
 
 
 def split(x):
@@ -67,33 +68,76 @@
     out_ref[...] = jnp.where(slot_of(here.shape, size) == (y ^ 2), near, here)
 
 
-def complete_kernel(me_ref, *refs):
-    pieces, (hi_ref, lo_ref) = refs[:4], refs[6:]
+def complete_kernel(me_ref, p0, p1, q0, q1, _, __, hi_ref, lo_ref):
     me = me_ref[0]
-    size = pieces[0].shape[0]
-    for core_step in range(2):
+    size = p0.shape[0] // 2
+    first = lax.rem(me, 2) == 0
+    for core_step, (even, odd) in enumerate(((p0, p1), (q1, q0))):
         for z in range(2):
+            part = slice(z * size, (z + 1) * size)
             at = at_rows(me, z, 2, core_step, size)
-            hi_ref[at, :], lo_ref[at, :] = split(pieces[core_step * 2 + z][...])
-
-
-def product_kernel(step, at_ref, below_ref, hi_ref, lo_ref, out_ref):
-    near, far = at_ref[0], at_ref[1] ^ step
-    rows = jnp.concatenate([below_ref[near ^ j, far] for j in range(below_ref.shape[0])], 0)
-    out_ref[...] = dot3(split(rows), (hi_ref[...], lo_ref[...]), NT)
-
-
-def product(at, step, below, hi, lo):
+            hi_ref[at, :], lo_ref[at, :] = split(jnp.where(first, even[part, :], odd[part, :]))
+
+
+def long_dot(rows, hi, lo):
+    left_hi, left_lo = split(rows)
+    left = jnp.concatenate([left_hi, left_lo, left_hi], 1)
+    right = jnp.concatenate([lo, hi, hi], 1)
+    return lax.dot_general(left, right, NT, preferred_element_type=F32)
+
+
+def product_kernel(at_ref, below_ref, hi_ref, lo_ref, a_send, b_send, a_keep, b_keep, held, sems):
+    near, far = at_ref[0], at_ref[1]
+    near_n, _, share, _ = below_ref.shape
+    half = a_send.shape[2]
+    groups = ((1, 2), (3, 0))
+    copies = {}
+    for k in (1, 2, 3, 0):
+        for j in range(near_n):
+            to = held.at[k, pl.ds(j * share, share)]
+            copies[k, j] = pltpu.make_async_copy(below_ref.at[near ^ j, far ^ k], to, sems.at[k, j])
+            copies[k, j].start()
+    places = {1: ((a_send, 0), (b_keep, 1)), 2: ((a_send, 1), (b_send, 1)),
+              3: ((a_keep, 1), (b_send, 0)), 0: ((a_keep, 0), (b_keep, 0))}
+    for group in groups:
+        for k in group:
+            for j in range(near_n):
+                copies[k, j].wait()
+        out = long_dot(jnp.concatenate([held[k] for k in group], 0), hi_ref[...], lo_ref[...])
+        size = out.shape[0] // 2
+        for i, k in enumerate(group):
+            (a, at_a), (b, at_b) = places[k]
+            a[at_a] = out[i * size:(i + 1) * size, :half]
+            b[at_b] = out[i * size:(i + 1) * size, half:]
+
+
+def products(at, below, hi, lo):
     near_n, far_n, share, depth = below.shape
     panel = hi.shape[0]
+    rows = near_n * share
     return call(
-        functools.partial(product_kernel, step),
-        jax.ShapeDtypeStruct((near_n * share, panel), F32),
-        [SMEM] + [VMEM] * 3,
+        product_kernel,
+        (jax.ShapeDtypeStruct((2, rows, panel // 2), F32),) * 4,
+        [SMEM, pl.BlockSpec(memory_space=pl.ANY), VMEM, VMEM],
         [at, below, hi, lo],
-        flops=11 * near_n * share * depth * panel,
+        scratch=[pltpu.VMEM((far_n, rows, depth), F32), pltpu.SemaphoreType.DMA((far_n, near_n))],
+        flops=9 * far_n * rows * depth * panel,
         moved=6 * 2**20,
-    )
+        vmem=PRODUCT_VMEM,
+    )
+
+
+def middle_kernel(a_keep, a_got, b_keep, b_got, a_out, b_out):
+    a_out[...] = a_keep[1] + a_got[1]
+    b_out[...] = b_keep[1] + b_got[1]
+
+
+def combine_kernel(a_keep, a_got, a_last, b_keep, b_got, b_last, *outs):
+    share, panel = outs[0].shape
+    for j, out in enumerate(outs):
+        rows = slice(j * share, (j + 1) * share)
+        out[:, :panel // 2] = a_keep[0, rows] + a_got[0, rows] + a_last[rows]
+        out[:, panel // 2:] = b_keep[0, rows] + b_got[0, rows] + b_last[rows]
 
 
 def recip(x):
@@ -172,11 +216,11 @@
     return rows, inv
 
 
-def factor_columns(first, count, w_ref, l_ref, x_ref, sc_ref):
+def factor_columns(w_ref, l_ref, x_ref, sc_ref):
     n = w_ref.shape[0]
     nb = 128
     blk = lambda i: slice(i * nb, (i + 1) * nb)
-    for b in range(first, first + count):
+    for b in range(n // nb):
         rows = [w_ref[b * nb + 8 * g:b * nb + 8 * g + 8, blk(b)] for g in range(nb // 8)]
         up, inv = factor_block(rows, nb, sc_ref)
         x11 = jnp.concatenate(inv, 0)
@@ -194,8 +238,8 @@
             x_ref[blk(b), done] = -dot3(split(x11), split(t), NN)
 
 
-def leading_kernel(me_ref, diag_ref, *refs):
-    pieces, (w_ref, l_ref, x_ref, sc_ref) = refs[:8], refs[8:]
+def cholesky_kernel(me_ref, diag_ref, *refs):
+    pieces, (l_ref, x_ref, w_ref, sc_ref) = refs[:8], refs[8:]
     me = me_ref[0]
     size = pieces[0].shape[0] // 2
     y = lax.rem(me // 2, 4)
@@ -211,14 +255,7 @@
                 w_ref[at, :] = diag_ref[at, :] - whole[z * size:(z + 1) * size]
     l_ref[...] = jnp.zeros_like(l_ref)
     x_ref[...] = jnp.zeros_like(x_ref)
-    factor_columns(0, w_ref.shape[0] // 128 - 1, w_ref, l_ref, x_ref, sc_ref)
-
-
-def last_kernel(w_in, l_in, x_in, l_ref, x_ref, w_ref, sc_ref):
-    w_ref[...] = w_in[...]
-    l_ref[...] = l_in[...]
-    x_ref[...] = x_in[...]
-    factor_columns(w_ref.shape[0] // 128 - 1, 1, w_ref, l_ref, x_ref, sc_ref)
+    factor_columns(w_ref, l_ref, x_ref, sc_ref)
 
 
 def final_kernel(below_ref, p0, p1, p2, p3, x_ref, out_ref):
@@ -277,46 +314,49 @@
         flops=24 * mine * depth * panel,
         moved=8 * panel * depth,
     )
-    y2 = [along_y(y3[:mine], 1), along_y(y1[mine:], 3)]
+    def some(x, core_at, step):
+        pairs = [(i, i ^ step) for i in range(rows_n) if i % 2 == core_at]
+        return lax.ppermute(x, "rows", pairs)
+
+    y2 = [some(y3, 0, 2), some(y1, 1, 6)]
     *y2_late, _ = lax.optimization_barrier((*y2, schur_part))
     by_far = [swap(schur_part, "far", far_n, k) for k in (1, 2, 3)]
     hi, lo = call(
         complete_kernel,
         (gathered, gathered),
         [SMEM] + [VMEM] * 6,
-        [me] + y2_late + [core(x) for x in y2_late] + [hi, lo],
+        [me] + y2_late + [some(y2_late[0], 0, 1), some(y2_late[1], 1, 1), hi, lo],
         moved=2 * panel * depth,
         aliases=((5, 0), (6, 1)),
     )
     below = history_below.reshape(near_n, far_n, share, depth)
-    parts = [product(at, k, below, hi, lo) for k in (0, 1, 2, 3)]
+    a_send, b_send, a_keep, b_keep = products(at, below, hi, lo)
+    *by_far, a_send, b_send = lax.optimization_barrier((*by_far, a_send, b_send))
     schur_part = tree(schur_part, *by_far)
     schur_part = sum_near(schur_part, rows_n, near_n)
     schur_pieces = [schur_part] + [along_y(schur_part, k) for k in (1, 2, 3)]
     schur_pieces = schur_pieces + [core(x) for x in schur_pieces]
-    parts = [parts[0]] + [swap(parts[k], "far", far_n, k) for k in (1, 2, 3)]
-    quarter = lambda p, j: p[j * share:(j + 1) * share]
-    sums = [tree(*[quarter(p, j) for p in parts]) for j in range(near_n)]
+    a_got, b_got = swap(a_send, "far", far_n, 1), swap(b_send, "far", far_n, 3)
+    a_got, b_got, _ = lax.optimization_barrier((a_got, b_got, schur_part))
+    block = jax.ShapeDtypeStruct(a_send.shape[1:], F32)
+    a_next, b_next = call(middle_kernel, (block, block), [VMEM] * 4, [a_keep, a_got, b_keep, b_got], moved=2**20)
+    a_last, b_last = swap(a_next, "far", far_n, 3), swap(b_next, "far", far_n, 1)
+    sums = call(
+        combine_kernel,
+        (jax.ShapeDtypeStruct((share, panel), F32),) * near_n,
+        [VMEM] * 6,
+        [a_keep, a_got, a_last, b_keep, b_got, b_last],
+        moved=2**20,
+    )
+    sums = [sums[0]] + [swap(sums[j], "near", near_n, j) for j in (1, 2, 3)]
     square = jax.ShapeDtypeStruct((panel, panel), F32)
-    broadcasts = pltpu.VMEM((2, 10, 8, 128), F32)
-    leading = call(
-        leading_kernel,
-        (square,) * 3,
+    diag_factor, inverse = call(
+        cholesky_kernel,
+        (square,) * 2,
         [SMEM] + [VMEM] * 9,
         [me, diag_block] + schur_pieces,
-        scratch=[broadcasts],
-        flops=96 * panel**3,
-        moved=16 * panel * panel,
-    )
-    *leading, sums[1], sums[2], sums[3] = lax.optimization_barrier((*leading, *sums[1:]))
-    sums = [sums[0]] + [swap(sums[j], "near", near_n, j) for j in (1, 2, 3)]
-    diag_factor, inverse = call(
-        last_kernel,
-        (square,) * 2,
-        [VMEM] * 3,
-        leading,
-        scratch=[pltpu.VMEM((panel, panel), F32), broadcasts],
-        flops=24 * panel**3,
+        scratch=[pltpu.VMEM((panel, panel), F32), pltpu.VMEM((2, 10, 8, 128), F32)],
+        flops=120 * panel**3,
         moved=16 * panel * panel,
     )
     panel_factor = call(

time: 116 us -> 110 us (0.948)
  waiting for transfers between devices: 30.9 us -> 25.2 us
  starting transfers between devices: 49.7 us -> 54.4 us
  local copies, waits for them, and re-layouts: 4.16 us -> 0.67 us
  other arithmetic: 2.46 us -> 1.13 us
    ppermute x26 -> x23, waiting for transfers between devices: 30.9 us -> 9.52 us  [swap(): return lax.ppermute(x, axis, [(i, i ^ step) for i in range(size)])]
    ppermute x3, waiting for transfers between devices: 0.01 us -> 12.5 us  [move(): return lax.ppermute(x, ('rows', 'near'), pairs)]
    ppermute x0 -> x4, starting transfers between devices: none -> 10.3 us  [some(): return lax.ppermute(x, 'rows', pairs)]
    ppermute x26 -> x23, starting transfers between devices: 42.3 us -> 37.5 us  [swap(): return lax.ppermute(x, axis, [(i, i ^ step) for i in range(size)])]
    ppermute x0 -> x4, waiting for transfers between devices: none -> 3.21 us  [some(): return lax.ppermute(x, 'rows', pairs)]
    unnamed x6 -> x8, local copies, waits for them, and re-layouts: 2.79 us -> 0.67 us
    slice x2 -> x0, local copies, waits for them, and re-layouts: 1.37 us -> none  [body(): y2 = [along_y(y3[:mine], 1), along_y(y1[mine:], 3)]]
    add x2 -> x1, other arithmetic: 1.37 us -> 0.04 us  [tree(): return a + b + (c + d)]
  transfers between devices with their start and end apart: 29 -> 30, of which waited for: 10 -> 10; matrix products, arithmetic and copies ran while one was open for 2% -> 0% of each run, Pallas kernels for 22% -> 24%
where the time goes in v1:
time: 110 us
  starting transfers between devices  54.4 us (49%)
  Pallas kernels  27.3 us (25%)
  waiting for transfers between devices  25.2 us (23%)
  other arithmetic  1.13 us (1%)
    ppermute x23, starting transfers between devices, swap(): return lax.ppermute(x, axis, [(i, i ^ step) for i in range(size)])  37.5 us
    pallas_call x7, Pallas kernels, call(): pl.pallas_call(kernel, out_shape=out_shape, in_specs=in_specs, out_specs=...  27.3 us
    ppermute x3, waiting for transfers between devices, move(): return lax.ppermute(x, ('rows', 'near'), pairs)  12.5 us
    ppermute x4, starting transfers between devices, some(): return lax.ppermute(x, 'rows', pairs)  10.3 us
    ppermute x23, waiting for transfers between devices, swap(): return lax.ppermute(x, axis, [(i, i ^ step) for i in range(size)])  9.52 us
    ppermute x3, starting transfers between devices, move(): return lax.ppermute(x, ('rows', 'near'), pairs)  6.58 us
    ppermute x4, waiting for transfers between devices, some(): return lax.ppermute(x, 'rows', pairs)  3.21 us
  transfers between devices with their start and end apart: 30, of which 10 were waited for; matrix products, arithmetic and copies ran while one was open for 0% of the time, Pallas kernels for 24%

profile of v1, /device:TPU:1, one launch (start us, length us, event | category | flops | bytes accessed | tf_op | source)
XLA Modules:
  0.0 109.6 jit_solution(4882420603474441194)
XLA Ops:
  0.6 2.6 %collective-permute-start = (f32[32,1536]{1,0:T(8,128)}, f32[32,1536]{1,0:T(8,128)S(1)}, u32[]{:S(2)}, u32[]{:S(2)}) collective-permute-start(f32[32,1536]{1,0:T(8,128)} %param.5), channel_id=1, source_target_pairs={{0,128},{16,144},{32,160},{48,176},{64,192},{80,208},{96,224},{112... | collective-permute-start | bytes 589832 | tf_op jit(solution)/shard_map/ppermute | solution.py:267
  3.2 3.9 %collective-permute-done = f32[32,1536]{1,0:T(8,128)S(1)} collective-permute-done((f32[32,1536]{1,0:T(8,128)}, f32[32,1536]{1,0:T(8,128)S(1)}, u32[]{:S(2)}, u32[]{:S(2)}) %collective-permute-start) | collective-permute-done | bytes 196640 | tf_op jit(solution)/shard_map/ppermute | solution.py:267
  7.1 1.0 broadcast_select_fusion.1
  8.1 2.2 %collective-permute-start.3 = (f32[64,1536]{1,0:T(8,128)S(1)}, f32[64,1536]{1,0:T(8,128)S(1)}, u32[]{:S(2)}, u32[]{:S(2)}) collective-permute-start(f32[64,1536]{1,0:T(8,128)S(1)} %pad_maximum_fusion.refs_0_), channel_id=1, source_target_pairs={{0,32},{16,48},{32,0},{48,16},{64,96},{80,112},{96,64},{112,80},{1... | collective-permute-start | bytes 1179656 | tf_op jit(solution)/shard_map/ppermute | solution.py:267
  10.3 1.9 %collective-permute-start.1 = (f32[64,1536]{1,0:T(8,128)S(1)}, f32[64,1536]{1,0:T(8,128)S(1)}, u32[]{:S(2)}, u32[]{:S(2)}) collective-permute-start(f32[64,1536]{1,0:T(8,128)S(1)} %pad_maximum_fusion.refs_0_), channel_id=1, source_target_pairs={{0,96},{16,112},{32,64},{48,80},{64,32},{80,48},{96,0},{112,16},{1... | collective-permute-start | bytes 1179656 | tf_op jit(solution)/shard_map/ppermute | solution.py:267
  12.2 1.9 %collective-permute-start.5 = (f32[64,1536]{1,0:T(8,128)S(1)}, f32[64,1536]{1,0:T(8,128)S(1)}, u32[]{:S(2)}, u32[]{:S(2)}) collective-permute-start(f32[64,1536]{1,0:T(8,128)S(1)} %pad_maximum_fusion.refs_0_), channel_id=1, source_target_pairs={{0,16},{16,0},{32,48},{48,32},{64,80},{80,64},{96,112},{112,96},{1... | collective-permute-start | bytes 1179656 | tf_op jit(solution)/shard_map/ppermute | solution.py:267
  14.1 3.2 %collective-permute-done.3.refs_1_ = f32[64,1536]{1,0:T(8,128)S(1)} collective-permute-done((f32[64,1536]{1,0:T(8,128)S(1)}, f32[64,1536]{1,0:T(8,128)S(1)}, u32[]{:S(2)}, u32[]{:S(2)}) %collective-permute-start.3) | collective-permute-done | bytes 393248 | tf_op jit(solution)/shard_map/ppermute | solution.py:267
  17.3 3.0 %collective-permute-start.6 = (f32[64,1536]{1,0:T(8,128)S(1)}, f32[64,1536]{1,0:T(8,128)S(1)}, u32[]{:S(2)}, u32[]{:S(2)}) collective-permute-start(f32[64,1536]{1,0:T(8,128)S(1)} %collective-permute-done.3.refs_1_), channel_id=1, source_target_pairs={{0,16},{16,0},{32,48},{48,32},{64,80},{80,64},{96,112},{112,96},{1... | collective-permute-start | bytes 1179656 | tf_op jit(solution)/shard_map/ppermute | solution.py:267
  20.4 0.1 collective-permute-done.1.refs_2_
  20.5 2.6 %collective-permute-start.7 = (f32[64,1536]{1,0:T(8,128)S(1)}, f32[64,1536]{1,0:T(8,128)S(1)}, u32[]{:S(2)}, u32[]{:S(2)}) collective-permute-start(f32[64,1536]{1,0:T(8,128)S(1)} %collective-permute-done.1.refs_2_), channel_id=1, source_target_pairs={{0,16},{16,0},{32,48},{48,32},{64,80},{80,64},{96,112},{112,96},{1... | collective-permute-start | bytes 1179656 | tf_op jit(solution)/shard_map/ppermute | solution.py:267
  23.0 0.7 collective-permute-start.2
  23.7 3.8 %collective-permute-start.4 = (f32[64,1536]{1,0:T(8,128)S(1)}, f32[64,1536]{1,0:T(8,128)}, u32[]{:S(2)}, u32[]{:S(2)}) collective-permute-start(f32[64,1536]{1,0:T(8,128)S(1)} %collective-permute-done.3.refs_1_), channel_id=1, source_target_pairs={{16,112},{48,80},{80,48},{112,16},{144,240},{176,208},{208,176},{2... | collective-permute-start | bytes 1179656 | tf_op jit(solution)/shard_map/ppermute | solution.py:319
  27.5 0.0 collective-permute-done.7.refs_5_
  27.6 2.1 %shard_map.59 = (f32[64,512]{1,0:T(8,128)S(1)}, bf16[512,1536]{1,0:T(8,128)(2,1)S(1)}, bf16[512,1536]{1,0:T(8,128)(2,1)S(1)}) custom-call(s32[1]{0:T(128)} %bitcast.3.me_ref, f32[64,1536]{1,0:T(8,128)S(1)} %pad_maximum_fusion.refs_0_, f32[64,1536]{1,0:T(8,128)S(1)} %collective-permute-done.3.refs_1_, f32[64,1536]{1,0:T(8,128)S(1)} %collective-permute-done.1.refs_2_, ...), custom_call_target="tpu_custom_call" | custom-call | flops 603979776 | bytes 6291456 | tf_op jit(solution)/shard_map/pallas_call | solution.py:30
  29.7 0.0 copy-start.1
  29.7 0.6 copy-done.1
  30.3 0.0 collective-permute-done.2.p0
  30.3 3.2 %collective-permute-done.4.p1 = f32[64,1536]{1,0:T(8,128)} collective-permute-done((f32[64,1536]{1,0:T(8,128)S(1)}, f32[64,1536]{1,0:T(8,128)}, u32[]{:S(2)}, u32[]{:S(2)}) %collective-permute-start.4) | collective-permute-done | bytes 393248 | tf_op jit(solution)/shard_map/ppermute | solution.py:319
  33.5 1.3 %collective-permute-start.8 = (f32[64,1536]{1,0:T(8,128)S(1)}, f32[64,1536]{1,0:T(8,128)}, u32[]{:S(2)}, u32[]{:S(2)}) collective-permute-start(f32[64,1536]{1,0:T(8,128)S(1)} %collective-permute-done.2.p0), channel_id=1, source_target_pairs={{0,16},{32,48},{64,80},{96,112},{128,144},{160,176},{192,208},{224... | collective-permute-start | bytes 1179656 | tf_op jit(solution)/shard_map/ppermute | solution.py:319
  34.8 4.5 %collective-permute-start.9 = (f32[64,1536]{1,0:T(8,128)}, f32[64,1536]{1,0:T(8,128)}, u32[]{:S(2)}, u32[]{:S(2)}) collective-permute-start(f32[64,1536]{1,0:T(8,128)} %collective-permute-done.4.p1), channel_id=1, source_target_pairs={{16,0},{48,32},{80,64},{112,96},{144,128},{176,160},{208,192},{240... | collective-permute-start | bytes 1179656 | tf_op jit(solution)/shard_map/ppermute | solution.py:319
  39.4 0.1 pad_add_fusion.at_ref
  39.5 1.2 %collective-permute-start.10 = (f32[64,512]{1,0:T(8,128)}, f32[64,512]{1,0:T(8,128)S(1)}, u32[]{:S(2)}, u32[]{:S(2)}) collective-permute-start(f32[64,512]{1,0:T(8,128)} %copy-done.1), channel_id=1, source_target_pairs={{0,1},{1,0},{2,3},{3,2},{4,5},{5,4},{6,7},{7,6},{8,9},{9,8},{10,11... | collective-permute-start | bytes 393224 | tf_op jit(solution)/shard_map/ppermute | solution.py:267
  40.7 2.5 %collective-permute-start.11 = (f32[64,512]{1,0:T(8,128)}, f32[64,512]{1,0:T(8,128)S(1)}, u32[]{:S(2)}, u32[]{:S(2)}) collective-permute-start(f32[64,512]{1,0:T(8,128)} %copy-done.1), channel_id=1, source_target_pairs={{0,2},{1,3},{2,0},{3,1},{4,6},{5,7},{6,4},{7,5},{8,10},{9,11},{10,... | collective-permute-start | bytes 393224 | tf_op jit(solution)/shard_map/ppermute | solution.py:267
  43.1 0.2 collective-permute-start.12
  43.3 0.0 collective-permute-done.8.q0
  43.3 0.0 collective-permute-done.9.q1
  43.3 1.4 %shard_map.60 = (bf16[512,1536]{1,0:T(8,128)(2,1)S(1)}, bf16[512,1536]{1,0:T(8,128)(2,1)S(1)}) custom-call(s32[1]{0:T(128)} %bitcast.3.me_ref, f32[64,1536]{1,0:T(8,128)S(1)} %collective-permute-done.2.p0, f32[64,1536]{1,0:T(8,128)} %collective-permute-done.4.p1, ...), custom_call_target="tpu_custom_call", output_to_operand_aliasing={{0}: (5, {}), {1}: (6, {})} | custom-call | bytes 1572864 | tf_op jit(solution)/shard_map/pallas_call | solution.py:30
  44.7 0.0 copy-start.2
  44.7 7.8 %shard_map.61 = (f32[2,256,256]{2,1,0:T(8,128)S(1)}, f32[2,256,256]{2,1,0:T(8,128)S(1)}, f32[2,256,256]{2,1,0:T(8,128)S(1)}, f32[2,256,256]{2,1,0:T(8,128)S(1)}) custom-call(s32[2]{0:T(128)S(1)} %pad_add_fusion.at_ref, f32[4,4,64,1536]{3,2,1,0:T(8,128)} %bitcast.4, bf16[512,1536]{1,0:T(8,128)(2,1)S(1)} %get-tuple-element.33.hi_ref, ...), custom_call_target="tpu_custom_call" | custom-call | flops 7247757312 | bytes 6291456 | tf_op jit(solution)/shard_map/pallas_call | solution.py:30
  52.5 0.0 collective-permute-done.10
  52.5 0.0 collective-permute-done.11
  52.5 0.1 collective-permute-start.13
  52.6 2.7 %collective-permute-start.14 = (f32[2,256,256]{2,1,0:T(8,128)S(1)}, f32[2,256,256]{2,1,0:T(8,128)S(1)}, u32[]{:S(2)}, u32[]{:S(2)}) collective-permute-start(f32[2,256,256]{2,1,0:T(8,128)S(1)} %get-tuple-element.39), channel_id=1, source_target_pairs={{0,3},{1,2},{2,1},{3,0},{4,7},{5,6},{6,5},{7,4},{8,11},{9,10},{10,... | collective-permute-start | bytes 1572872 | tf_op jit(solution)/shard_map/ppermute | solution.py:267
  55.4 6.2 %collective-permute-start.15 = (f32[64,512]{1,0:T(8,128)S(1)}, f32[64,512]{1,0:T(8,128)S(1)}, u32[]{:S(2)}, u32[]{:S(2)}) collective-permute-start(f32[64,512]{1,0:T(8,128)S(1)} %add_add_fusion.1), channel_id=1, source_target_pairs={{136,0},{140,4},{128,8},{132,12},{152,16},{156,20},{144,24},{148,2... | collective-permute-start | bytes 393224 | tf_op jit(solution)/shard_map/ppermute | solution.py:284
  61.6 0.0 collective-permute-start.16
  61.6 0.4 collective-permute-start.17
  62.0 5.4 %collective-permute-done.15 = f32[64,512]{1,0:T(8,128)S(1)} collective-permute-done((f32[64,512]{1,0:T(8,128)S(1)}, f32[64,512]{1,0:T(8,128)S(1)}, u32[]{:S(2)}, u32[]{:S(2)}) %collective-permute-start.15) | collective-permute-done | bytes 131104 | tf_op jit(solution)/shard_map/ppermute | solution.py:284
  67.4 3.0 %collective-permute-done.16 = f32[64,512]{1,0:T(8,128)S(1)} collective-permute-done((f32[64,512]{1,0:T(8,128)S(1)}, f32[64,512]{1,0:T(8,128)S(1)}, u32[]{:S(2)}, u32[]{:S(2)}) %collective-permute-start.16) | collective-permute-done | bytes 131104 | tf_op jit(solution)/shard_map/ppermute | solution.py:284
  70.3 4.1 %collective-permute-done.17 = f32[64,512]{1,0:T(8,128)S(1)} collective-permute-done((f32[64,512]{1,0:T(8,128)S(1)}, f32[64,512]{1,0:T(8,128)S(1)}, u32[]{:S(2)}, u32[]{:S(2)}) %collective-permute-start.17) | collective-permute-done | bytes 131104 | tf_op jit(solution)/shard_map/ppermute | solution.py:284
  74.5 0.0 collective-permute-done.14.b_got
  74.5 0.1 shard_map.62
  74.6 0.0 copy-start.3
  74.6 0.3 collective-permute-start.18
  74.9 0.5 collective-permute-start.19
  75.4 0.0 collective-permute-start.23
  75.4 3.1 %collective-permute-start.24 = (f32[64,512]{1,0:T(8,128)S(1)}, f32[64,512]{1,0:T(8,128)S(1)}, u32[]{:S(2)}, u32[]{:S(2)}) collective-permute-start(f32[64,512]{1,0:T(8,128)S(1)} %add_add_fusion.refs_0_), channel_id=1, source_target_pairs={{0,64},{16,80},{32,96},{48,112},{64,0},{80,16},{96,32},{112,48},{1... | collective-permute-start | bytes 393224 | tf_op jit(solution)/shard_map/ppermute | solution.py:267
  78.5 0.8 collective-permute-start.25
  79.2 0.3 collective-permute-done.23.refs_1_
  79.5 3.1 %collective-permute-start.26 = (f32[64,512]{1,0:T(8,128)S(1)}, f32[64,512]{1,0:T(8,128)S(1)}, u32[]{:S(2)}, u32[]{:S(2)}) collective-permute-start(f32[64,512]{1,0:T(8,128)S(1)} %add_add_fusion.refs_0_), channel_id=1, source_target_pairs={{0,16},{16,0},{32,48},{48,32},{64,80},{80,64},{96,112},{112,96},{1... | collective-permute-start | bytes 393224 | tf_op jit(solution)/shard_map/ppermute | solution.py:267
  82.7 1.3 %collective-permute-done.24.refs_2_ = f32[64,512]{1,0:T(8,128)S(1)} collective-permute-done((f32[64,512]{1,0:T(8,128)S(1)}, f32[64,512]{1,0:T(8,128)S(1)}, u32[]{:S(2)}, u32[]{:S(2)}) %collective-permute-start.24) | collective-permute-done | bytes 131104 | tf_op jit(solution)/shard_map/ppermute | solution.py:267
  84.0 1.9 %collective-permute-start.27 = (f32[64,512]{1,0:T(8,128)S(1)}, f32[64,512]{1,0:T(8,128)S(1)}, u32[]{:S(2)}, u32[]{:S(2)}) collective-permute-start(f32[64,512]{1,0:T(8,128)S(1)} %collective-permute-done.23.refs_1_), channel_id=1, source_target_pairs={{0,16},{16,0},{32,48},{48,32},{64,80},{80,64},{96,112},{112,96},{1... | collective-permute-start | bytes 393224 | tf_op jit(solution)/shard_map/ppermute | solution.py:267
  85.8 0.6 collective-permute-done.25.refs_3_
  86.5 1.3 %collective-permute-start.28 = (f32[64,512]{1,0:T(8,128)S(1)}, f32[64,512]{1,0:T(8,128)S(1)}, u32[]{:S(2)}, u32[]{:S(2)}) collective-permute-start(f32[64,512]{1,0:T(8,128)S(1)} %collective-permute-done.24.refs_2_), channel_id=1, source_target_pairs={{0,16},{16,0},{32,48},{48,32},{64,80},{80,64},{96,112},{112,96},{1... | collective-permute-start | bytes 393224 | tf_op jit(solution)/shard_map/ppermute | solution.py:267
  87.8 0.0 collective-permute-done.18.a_last
  87.8 0.0 collective-permute-start.29
  87.8 0.1 shard_map.63
  87.9 0.2 collective-permute-start.20
  88.1 0.0 collective-permute-done.26.refs_4_
  88.1 4.6 %collective-permute-start.21 = (f32[64,512]{1,0:T(8,128)S(1)}, f32[64,512]{1,0:T(8,128)S(1)}, u32[]{:S(2)}, u32[]{:S(2)}) collective-permute-start(f32[64,512]{1,0:T(8,128)S(1)} %get-tuple-element.50), channel_id=1, source_target_pairs={{0,8},{4,12},{8,0},{12,4},{1,9},{5,13},{9,1},{13,5},{2,10},{6,14},... | collective-permute-start | bytes 393224 | tf_op jit(solution)/shard_map/ppermute | solution.py:267
  92.7 0.9 collective-permute-start.22
  93.6 14.7 %shard_map.64 = (f32[512,512]{1,0:T(8,128)}, f32[512,512]{1,0:T(8,128)S(1)}) custom-call(s32[1]{0:T(128)} %bitcast.3.me_ref, f32[512,512]{1,0:T(8,128)S(1)} %copy-done.3, f32[64,512]{1,0:T(8,128)S(1)} %add_add_fusion.refs_0_, f32[64,512]{1,0:T(8,128)S(1)} %collective-permute-done.23.refs_1_, f32[64,512]{1,0:T(8,128)S(1)} %collective-permute-done.24.refs_2_, ...), custom_call_target="tpu_custom_call" | custom-call | flops 16106127360 | bytes 4194304 | tf_op jit(solution)/shard_map/pallas_call | solution.py:30
  108.3 0.0 collective-permute-done.20.p1
  108.3 0.0 collective-permute-done.21.p2
  108.3 1.3 %shard_map.65 = f32[64,512]{1,0:T(8,128)} custom-call(f32[64,512]{1,0:T(8,128)S(1)} %copy-done, f32[64,512]{1,0:T(8,128)S(1)} %get-tuple-element.48.p0, f32[64,512]{1,0:T(8,128)S(1)} %collective-permute-done.20.p1, f32[64,512]{1,0:T(8,128)S(1)} %collective-permute-done.21.p2, f32[64,512]{1,0:T(8,128)S(1)} %collective-permute-done.22.p3, ...), custom_call_target="tpu_custom_call" | custom-call | flops 100663296 | bytes 2097152 | tf_op jit(solution)/shard_map/pallas_call | solution.py:30
  (16 shorter events, 0.1 us)
Async XLA Ops:
  0.6 6.4 %collective-permute-start = (f32[32,1536]{1,0:T(8,128)}, f32[32,1536]{1,0:T(8,128)S(1)}, u32[]{:S(2)}, u32[]{:S(2)}) collective-permute-start(f32[32,1536]{1,0:T(8,128)} %param.5), channel_id=1, source_target_pairs={{0,128},{16,144},{32,160},{48,176},{64,192},{80,208},{96,224},{112... | collective-permute-start | bytes 589832 | tf_op jit(solution)/shard_map/ppermute | solution.py:267
  8.1 9.3 %collective-permute-start.3 = (f32[64,1536]{1,0:T(8,128)S(1)}, f32[64,1536]{1,0:T(8,128)S(1)}, u32[]{:S(2)}, u32[]{:S(2)}) collective-permute-start(f32[64,1536]{1,0:T(8,128)S(1)} %pad_maximum_fusion.refs_0_), channel_id=1, source_target_pairs={{0,32},{16,48},{32,0},{48,16},{64,96},{80,112},{96,64},{112,80},{1... | collective-permute-start | bytes 1179656 | tf_op jit(solution)/shard_map/ppermute | solution.py:267
  10.3 10.2 %collective-permute-start.1 = (f32[64,1536]{1,0:T(8,128)S(1)}, f32[64,1536]{1,0:T(8,128)S(1)}, u32[]{:S(2)}, u32[]{:S(2)}) collective-permute-start(f32[64,1536]{1,0:T(8,128)S(1)} %pad_maximum_fusion.refs_0_), channel_id=1, source_target_pairs={{0,96},{16,112},{32,64},{48,80},{64,32},{80,48},{96,0},{112,16},{1... | collective-permute-start | bytes 1179656 | tf_op jit(solution)/shard_map/ppermute | solution.py:267
  12.2 15.3 %collective-permute-start.5 = (f32[64,1536]{1,0:T(8,128)S(1)}, f32[64,1536]{1,0:T(8,128)S(1)}, u32[]{:S(2)}, u32[]{:S(2)}) collective-permute-start(f32[64,1536]{1,0:T(8,128)S(1)} %pad_maximum_fusion.refs_0_), channel_id=1, source_target_pairs={{0,16},{16,0},{32,48},{48,32},{64,80},{80,64},{96,112},{112,96},{1... | collective-permute-start | bytes 1179656 | tf_op jit(solution)/shard_map/ppermute | solution.py:267
  17.3 10.2 %collective-permute-start.6 = (f32[64,1536]{1,0:T(8,128)S(1)}, f32[64,1536]{1,0:T(8,128)S(1)}, u32[]{:S(2)}, u32[]{:S(2)}) collective-permute-start(f32[64,1536]{1,0:T(8,128)S(1)} %collective-permute-done.3.refs_1_), channel_id=1, source_target_pairs={{0,16},{16,0},{32,48},{48,32},{64,80},{80,64},{96,112},{112,96},{1... | collective-permute-start | bytes 1179656 | tf_op jit(solution)/shard_map/ppermute | solution.py:267
  20.5 7.1 %collective-permute-start.7 = (f32[64,1536]{1,0:T(8,128)S(1)}, f32[64,1536]{1,0:T(8,128)S(1)}, u32[]{:S(2)}, u32[]{:S(2)}) collective-permute-start(f32[64,1536]{1,0:T(8,128)S(1)} %collective-permute-done.1.refs_2_), channel_id=1, source_target_pairs={{0,16},{16,0},{32,48},{48,32},{64,80},{80,64},{96,112},{112,96},{1... | collective-permute-start | bytes 1179656 | tf_op jit(solution)/shard_map/ppermute | solution.py:267
  23.0 7.3 %collective-permute-start.2 = (f32[64,1536]{1,0:T(8,128)S(1)}, f32[64,1536]{1,0:T(8,128)S(1)}, u32[]{:S(2)}, u32[]{:S(2)}) collective-permute-start(f32[64,1536]{1,0:T(8,128)S(1)} %collective-permute-done.1.refs_2_), channel_id=1, source_target_pairs={{0,32},{32,0},{64,96},{96,64},{128,160},{160,128},{192,224},{224,1... | collective-permute-start | bytes 1179656 | tf_op jit(solution)/shard_map/ppermute | solution.py:319
  23.7 9.8 %collective-permute-start.4 = (f32[64,1536]{1,0:T(8,128)S(1)}, f32[64,1536]{1,0:T(8,128)}, u32[]{:S(2)}, u32[]{:S(2)}) collective-permute-start(f32[64,1536]{1,0:T(8,128)S(1)} %collective-permute-done.3.refs_1_), channel_id=1, source_target_pairs={{16,112},{48,80},{80,48},{112,16},{144,240},{176,208},{208,176},{2... | collective-permute-start | bytes 1179656 | tf_op jit(solution)/shard_map/ppermute | solution.py:319
  29.7 0.7 copy-start.1
  33.5 9.8 %collective-permute-start.8 = (f32[64,1536]{1,0:T(8,128)S(1)}, f32[64,1536]{1,0:T(8,128)}, u32[]{:S(2)}, u32[]{:S(2)}) collective-permute-start(f32[64,1536]{1,0:T(8,128)S(1)} %collective-permute-done.2.p0), channel_id=1, source_target_pairs={{0,16},{32,48},{64,80},{96,112},{128,144},{160,176},{192,208},{224... | collective-permute-start | bytes 1179656 | tf_op jit(solution)/shard_map/ppermute | solution.py:319
  34.8 8.5 %collective-permute-start.9 = (f32[64,1536]{1,0:T(8,128)}, f32[64,1536]{1,0:T(8,128)}, u32[]{:S(2)}, u32[]{:S(2)}) collective-permute-start(f32[64,1536]{1,0:T(8,128)} %collective-permute-done.4.p1), channel_id=1, source_target_pairs={{16,0},{48,32},{80,64},{112,96},{144,128},{176,160},{208,192},{240... | collective-permute-start | bytes 1179656 | tf_op jit(solution)/shard_map/ppermute | solution.py:319
  39.5 13.0 %collective-permute-start.10 = (f32[64,512]{1,0:T(8,128)}, f32[64,512]{1,0:T(8,128)S(1)}, u32[]{:S(2)}, u32[]{:S(2)}) collective-permute-start(f32[64,512]{1,0:T(8,128)} %copy-done.1), channel_id=1, source_target_pairs={{0,1},{1,0},{2,3},{3,2},{4,5},{5,4},{6,7},{7,6},{8,9},{9,8},{10,11... | collective-permute-start | bytes 393224 | tf_op jit(solution)/shard_map/ppermute | solution.py:267
  40.7 11.8 %collective-permute-start.11 = (f32[64,512]{1,0:T(8,128)}, f32[64,512]{1,0:T(8,128)S(1)}, u32[]{:S(2)}, u32[]{:S(2)}) collective-permute-start(f32[64,512]{1,0:T(8,128)} %copy-done.1), channel_id=1, source_target_pairs={{0,2},{1,3},{2,0},{3,1},{4,6},{5,7},{6,4},{7,5},{8,10},{9,11},{10,... | collective-permute-start | bytes 393224 | tf_op jit(solution)/shard_map/ppermute | solution.py:267
  43.1 9.4 %collective-permute-start.12 = (f32[64,512]{1,0:T(8,128)}, f32[64,512]{1,0:T(8,128)S(1)}, u32[]{:S(2)}, u32[]{:S(2)}) collective-permute-start(f32[64,512]{1,0:T(8,128)} %copy-done.1), channel_id=1, source_target_pairs={{0,3},{1,2},{2,1},{3,0},{4,7},{5,6},{6,5},{7,4},{8,11},{9,10},{10,... | collective-permute-start | bytes 393224 | tf_op jit(solution)/shard_map/ppermute | solution.py:267
  44.7 10.7 %copy-start.2 = (f32[64,512]{1,0:T(8,128)S(1)}, f32[64,512]{1,0:T(8,128)}, u32[]{:S(2)}) copy-start(f32[64,512]{1,0:T(8,128)} %copy-done.1) | copy-start | bytes 393220
  52.5 22.0 %collective-permute-start.13 = (f32[2,256,256]{2,1,0:T(8,128)S(1)}, f32[2,256,256]{2,1,0:T(8,128)S(1)}, u32[]{:S(2)}, u32[]{:S(2)}) collective-permute-start(f32[2,256,256]{2,1,0:T(8,128)S(1)} %get-tuple-element.38), channel_id=1, source_target_pairs={{0,1},{1,0},{2,3},{3,2},{4,5},{5,4},{6,7},{7,6},{8,9},{9,8},{10,11... | collective-permute-start | bytes 1572872 | tf_op jit(solution)/shard_map/ppermute | solution.py:267
  52.6 21.9 %collective-permute-start.14 = (f32[2,256,256]{2,1,0:T(8,128)S(1)}, f32[2,256,256]{2,1,0:T(8,128)S(1)}, u32[]{:S(2)}, u32[]{:S(2)}) collective-permute-start(f32[2,256,256]{2,1,0:T(8,128)S(1)} %get-tuple-element.39), channel_id=1, source_target_pairs={{0,3},{1,2},{2,1},{3,0},{4,7},{5,6},{6,5},{7,4},{8,11},{9,10},{10,... | collective-permute-start | bytes 1572872 | tf_op jit(solution)/shard_map/ppermute | solution.py:267
  55.4 11.9 %collective-permute-start.15 = (f32[64,512]{1,0:T(8,128)S(1)}, f32[64,512]{1,0:T(8,128)S(1)}, u32[]{:S(2)}, u32[]{:S(2)}) collective-permute-start(f32[64,512]{1,0:T(8,128)S(1)} %add_add_fusion.1), channel_id=1, source_target_pairs={{136,0},{140,4},{128,8},{132,12},{152,16},{156,20},{144,24},{148,2... | collective-permute-start | bytes 393224 | tf_op jit(solution)/shard_map/ppermute | solution.py:284
  61.6 8.7 %collective-permute-start.16 = (f32[64,512]{1,0:T(8,128)S(1)}, f32[64,512]{1,0:T(8,128)S(1)}, u32[]{:S(2)}, u32[]{:S(2)}) collective-permute-start(f32[64,512]{1,0:T(8,128)S(1)} %add_add_fusion.1), channel_id=1, source_target_pairs={{140,0},{128,4},{132,8},{136,12},{156,16},{144,20},{148,24},{152,2... | collective-permute-start | bytes 393224 | tf_op jit(solution)/shard_map/ppermute | solution.py:284
  61.6 12.8 %collective-permute-start.17 = (f32[64,512]{1,0:T(8,128)S(1)}, f32[64,512]{1,0:T(8,128)S(1)}, u32[]{:S(2)}, u32[]{:S(2)}) collective-permute-start(f32[64,512]{1,0:T(8,128)S(1)} %add_add_fusion.1), channel_id=1, source_target_pairs={{4,0},{8,4},{12,8},{0,12},{20,16},{24,20},{28,24},{16,28},{36,32},... | collective-permute-start | bytes 393224 | tf_op jit(solution)/shard_map/ppermute | solution.py:284
  74.6 19.1 %copy-start.3 = (f32[512,512]{1,0:T(8,128)S(1)}, f32[512,512]{1,0:T(8,128)}, u32[]{:S(2)}) copy-start(f32[512,512]{1,0:T(8,128)} %diag_ref.1) | copy-start | bytes 3145732
  74.6 13.2 %collective-permute-start.18 = (f32[256,256]{1,0:T(8,128)S(1)}, f32[256,256]{1,0:T(8,128)S(1)}, u32[]{:S(2)}, u32[]{:S(2)}) collective-permute-start(f32[256,256]{1,0:T(8,128)S(1)} %get-tuple-element.46), channel_id=1, source_target_pairs={{0,3},{1,2},{2,1},{3,0},{4,7},{5,6},{6,5},{7,4},{8,11},{9,10},{10,... | collective-permute-start | bytes 786440 | tf_op jit(solution)/shard_map/ppermute | solution.py:267
  74.9 12.9 %collective-permute-start.19 = (f32[256,256]{1,0:T(8,128)S(1)}, f32[256,256]{1,0:T(8,128)S(1)}, u32[]{:S(2)}, u32[]{:S(2)}) collective-permute-start(f32[256,256]{1,0:T(8,128)S(1)} %get-tuple-element.47), channel_id=1, source_target_pairs={{0,1},{1,0},{2,3},{3,2},{4,5},{5,4},{6,7},{7,6},{8,9},{9,8},{10,11... | collective-permute-start | bytes 786440 | tf_op jit(solution)/shard_map/ppermute | solution.py:267
  75.4 4.1 %collective-permute-start.23 = (f32[64,512]{1,0:T(8,128)S(1)}, f32[64,512]{1,0:T(8,128)S(1)}, u32[]{:S(2)}, u32[]{:S(2)}) collective-permute-start(f32[64,512]{1,0:T(8,128)S(1)} %add_add_fusion.refs_0_), channel_id=1, source_target_pairs={{0,32},{16,48},{32,0},{48,16},{64,96},{80,112},{96,64},{112,80},{1... | collective-permute-start | bytes 393224 | tf_op jit(solution)/shard_map/ppermute | solution.py:267
  75.4 8.6 %collective-permute-start.24 = (f32[64,512]{1,0:T(8,128)S(1)}, f32[64,512]{1,0:T(8,128)S(1)}, u32[]{:S(2)}, u32[]{:S(2)}) collective-permute-start(f32[64,512]{1,0:T(8,128)S(1)} %add_add_fusion.refs_0_), channel_id=1, source_target_pairs={{0,64},{16,80},{32,96},{48,112},{64,0},{80,16},{96,32},{112,48},{1... | collective-permute-start | bytes 393224 | tf_op jit(solution)/shard_map/ppermute | solution.py:267
  78.5 8.0 %collective-permute-start.25 = (f32[64,512]{1,0:T(8,128)S(1)}, f32[64,512]{1,0:T(8,128)S(1)}, u32[]{:S(2)}, u32[]{:S(2)}) collective-permute-start(f32[64,512]{1,0:T(8,128)S(1)} %add_add_fusion.refs_0_), channel_id=1, source_target_pairs={{0,96},{16,112},{32,64},{48,80},{64,32},{80,48},{96,0},{112,16},{1... | collective-permute-start | bytes 393224 | tf_op jit(solution)/shard_map/ppermute | solution.py:267
  79.5 8.5 %collective-permute-start.26 = (f32[64,512]{1,0:T(8,128)S(1)}, f32[64,512]{1,0:T(8,128)S(1)}, u32[]{:S(2)}, u32[]{:S(2)}) collective-permute-start(f32[64,512]{1,0:T(8,128)S(1)} %add_add_fusion.refs_0_), channel_id=1, source_target_pairs={{0,16},{16,0},{32,48},{48,32},{64,80},{80,64},{96,112},{112,96},{1... | collective-permute-start | bytes 393224 | tf_op jit(solution)/shard_map/ppermute | solution.py:267
  84.0 8.7 %collective-permute-start.27 = (f32[64,512]{1,0:T(8,128)S(1)}, f32[64,512]{1,0:T(8,128)S(1)}, u32[]{:S(2)}, u32[]{:S(2)}) collective-permute-start(f32[64,512]{1,0:T(8,128)S(1)} %collective-permute-done.23.refs_1_), channel_id=1, source_target_pairs={{0,16},{16,0},{32,48},{48,32},{64,80},{80,64},{96,112},{112,96},{1... | collective-permute-start | bytes 393224 | tf_op jit(solution)/shard_map/ppermute | solution.py:267
  86.5 7.2 %collective-permute-start.28 = (f32[64,512]{1,0:T(8,128)S(1)}, f32[64,512]{1,0:T(8,128)S(1)}, u32[]{:S(2)}, u32[]{:S(2)}) collective-permute-start(f32[64,512]{1,0:T(8,128)S(1)} %collective-permute-done.24.refs_2_), channel_id=1, source_target_pairs={{0,16},{16,0},{32,48},{48,32},{64,80},{80,64},{96,112},{112,96},{1... | collective-permute-start | bytes 393224 | tf_op jit(solution)/shard_map/ppermute | solution.py:267
  87.8 5.9 %collective-permute-start.29 = (f32[64,512]{1,0:T(8,128)S(1)}, f32[64,512]{1,0:T(8,128)S(1)}, u32[]{:S(2)}, u32[]{:S(2)}) collective-permute-start(f32[64,512]{1,0:T(8,128)S(1)} %collective-permute-done.25.refs_3_), channel_id=1, source_target_pairs={{0,16},{16,0},{32,48},{48,32},{64,80},{80,64},{96,112},{112,96},{1... | collective-permute-start | bytes 393224 | tf_op jit(solution)/shard_map/ppermute | solution.py:267
  87.9 20.4 %collective-permute-start.20 = (f32[64,512]{1,0:T(8,128)S(1)}, f32[64,512]{1,0:T(8,128)S(1)}, u32[]{:S(2)}, u32[]{:S(2)}) collective-permute-start(f32[64,512]{1,0:T(8,128)S(1)} %get-tuple-element.49), channel_id=1, source_target_pairs={{0,4},{4,0},{8,12},{12,8},{1,5},{5,1},{9,13},{13,9},{2,6},{6,2},{1... | collective-permute-start | bytes 393224 | tf_op jit(solution)/shard_map/ppermute | solution.py:267
  88.1 20.3 %collective-permute-start.21 = (f32[64,512]{1,0:T(8,128)S(1)}, f32[64,512]{1,0:T(8,128)S(1)}, u32[]{:S(2)}, u32[]{:S(2)}) collective-permute-start(f32[64,512]{1,0:T(8,128)S(1)} %get-tuple-element.50), channel_id=1, source_target_pairs={{0,8},{4,12},{8,0},{12,4},{1,9},{5,13},{9,1},{13,5},{2,10},{6,14},... | collective-permute-start | bytes 393224 | tf_op jit(solution)/shard_map/ppermute | solution.py:267
  92.7 15.7 %copy-start = (f32[64,512]{1,0:T(8,128)S(1)}, f32[64,512]{1,0:T(8,128)}, u32[]{:S(2)}) copy-start(f32[64,512]{1,0:T(8,128)} %below_ref.1) | copy-start | bytes 393220
  92.7 15.6 %collective-permute-start.22 = (f32[64,512]{1,0:T(8,128)S(1)}, f32[64,512]{1,0:T(8,128)S(1)}, u32[]{:S(2)}, u32[]{:S(2)}) collective-permute-start(f32[64,512]{1,0:T(8,128)S(1)} %get-tuple-element.51), channel_id=1, source_target_pairs={{0,12},{4,8},{8,4},{12,0},{1,13},{5,9},{9,5},{13,1},{2,14},{6,10},... | collective-permute-start | bytes 393224 | tf_op jit(solution)/shard_map/ppermute | solution.py:267

commit v2 on v1

--- a/solution.py
+++ b/solution.py
@@ -68,15 +68,14 @@
     out_ref[...] = jnp.where(slot_of(here.shape, size) == (y ^ 2), near, here)
 
 
-def complete_kernel(me_ref, p0, p1, q0, q1, _, __, hi_ref, lo_ref):
+def complete_kernel(me_ref, *refs):
+    pieces, (hi_ref, lo_ref) = refs[:4], refs[6:]
     me = me_ref[0]
-    size = p0.shape[0] // 2
-    first = lax.rem(me, 2) == 0
-    for core_step, (even, odd) in enumerate(((p0, p1), (q1, q0))):
+    size = pieces[0].shape[0]
+    for core_step in range(2):
         for z in range(2):
-            part = slice(z * size, (z + 1) * size)
             at = at_rows(me, z, 2, core_step, size)
-            hi_ref[at, :], lo_ref[at, :] = split(jnp.where(first, even[part, :], odd[part, :]))
+            hi_ref[at, :], lo_ref[at, :] = split(pieces[core_step * 2 + z][...])
 
 
 def long_dot(rows, hi, lo):
@@ -314,18 +313,14 @@
         flops=24 * mine * depth * panel,
         moved=8 * panel * depth,
     )
-    def some(x, core_at, step):
-        pairs = [(i, i ^ step) for i in range(rows_n) if i % 2 == core_at]
-        return lax.ppermute(x, "rows", pairs)
-
-    y2 = [some(y3, 0, 2), some(y1, 1, 6)]
+    y2 = [along_y(y3[:mine], 1), along_y(y1[mine:], 3)]
     *y2_late, _ = lax.optimization_barrier((*y2, schur_part))
     by_far = [swap(schur_part, "far", far_n, k) for k in (1, 2, 3)]
     hi, lo = call(
         complete_kernel,
         (gathered, gathered),
         [SMEM] + [VMEM] * 6,
-        [me] + y2_late + [some(y2_late[0], 0, 1), some(y2_late[1], 1, 1), hi, lo],
+        [me] + y2_late + [core(x) for x in y2_late] + [hi, lo],
         moved=2 * panel * depth,
         aliases=((5, 0), (6, 1)),
     )
@@ -337,7 +332,6 @@
     schur_pieces = [schur_part] + [along_y(schur_part, k) for k in (1, 2, 3)]
     schur_pieces = schur_pieces + [core(x) for x in schur_pieces]
     a_got, b_got = swap(a_send, "far", far_n, 1), swap(b_send, "far", far_n, 3)
-    a_got, b_got, _ = lax.optimization_barrier((a_got, b_got, schur_part))
     block = jax.ShapeDtypeStruct(a_send.shape[1:], F32)
     a_next, b_next = call(middle_kernel, (block, block), [VMEM] * 4, [a_keep, a_got, b_keep, b_got], moved=2**20)
     a_last, b_last = swap(a_next, "far", far_n, 3), swap(b_next, "far", far_n, 1)

time: 110 us -> 99.2 us (0.902)
  waiting for transfers between devices: 25.2 us -> 18.9 us
  starting transfers between devices: 54.4 us -> 50.4 us
    ppermute x4 -> x0, starting transfers between devices: 10.3 us -> none  [some(): return lax.ppermute(x, 'rows', pairs)]
    ppermute x3, waiting for transfers between devices: 12.5 us -> 4.33 us  [move(): return lax.ppermute(x, ('rows', 'near'), pairs)]
    ppermute x23 -> x27, starting transfers between devices: 37.5 us -> 43.8 us  [swap(): return lax.ppermute(x, axis, [(i, i ^ step) for i in range(size)])]
    ppermute x23 -> x27, waiting for transfers between devices: 9.52 us -> 14.6 us  [swap(): return lax.ppermute(x, axis, [(i, i ^ step) for i in range(size)])]
    ppermute x4 -> x0, waiting for transfers between devices: 3.21 us -> none  [some(): return lax.ppermute(x, 'rows', pairs)]
  transfers between devices with their start and end apart: 30 -> 30, of which waited for: 10 -> 10; matrix products, arithmetic and copies ran while one was open for 0% -> 0% of each run, Pallas kernels for 24% -> 26%
where the time goes in v2:
time: 99.2 us; the launch traced here: 99.1 us
  starting transfers between devices  50.4 us (51%)
  Pallas kernels  27.1 us (27%)
  waiting for transfers between devices  18.9 us (19%)
  other arithmetic  1.13 us (1%)
    ppermute x27, starting transfers between devices, swap(): return lax.ppermute(x, axis, [(i, i ^ step) for i in range(size)])  43.8 us
    pallas_call x7, Pallas kernels, call(): pl.pallas_call(kernel, out_shape=out_shape, in_specs=in_specs, out_specs=...  27.1 us
    ppermute x27, waiting for transfers between devices, swap(): return lax.ppermute(x, axis, [(i, i ^ step) for i in range(size)])  14.6 us
    ppermute x3, starting transfers between devices, move(): return lax.ppermute(x, ('rows', 'near'), pairs)  6.56 us
    ppermute x3, waiting for transfers between devices, move(): return lax.ppermute(x, ('rows', 'near'), pairs)  4.33 us
  transfers between devices with their start and end apart: 30, of which 10 were waited for; matrix products, arithmetic and copies ran while one was open for 0% of the time, Pallas kernels for 26%

profile of v2, /device:TPU:1, one launch (start us, length us, event | category | flops | bytes accessed | tf_op | source)
XLA Modules:
  0.0 99.1 jit_solution(5812556266020918947)
XLA Ops:
  0.6 2.6 %collective-permute-start = (f32[32,1536]{1,0:T(8,128)}, f32[32,1536]{1,0:T(8,128)S(1)}, u32[]{:S(2)}, u32[]{:S(2)}) collective-permute-start(f32[32,1536]{1,0:T(8,128)} %param.5), channel_id=1, source_target_pairs={{0,128},{16,144},{32,160},{48,176},{64,192},{80,208},{96,224},{112... | collective-permute-start | bytes 589832 | tf_op jit(solution)/shard_map/ppermute | solution.py:266
  3.2 3.9 %collective-permute-done = f32[32,1536]{1,0:T(8,128)S(1)} collective-permute-done((f32[32,1536]{1,0:T(8,128)}, f32[32,1536]{1,0:T(8,128)S(1)}, u32[]{:S(2)}, u32[]{:S(2)}) %collective-permute-start) | collective-permute-done | bytes 196640 | tf_op jit(solution)/shard_map/ppermute | solution.py:266
  7.1 1.0 broadcast_select_fusion.1
  8.1 2.2 %collective-permute-start.3 = (f32[64,1536]{1,0:T(8,128)S(1)}, f32[64,1536]{1,0:T(8,128)S(1)}, u32[]{:S(2)}, u32[]{:S(2)}) collective-permute-start(f32[64,1536]{1,0:T(8,128)S(1)} %pad_maximum_fusion.refs_0_), channel_id=1, source_target_pairs={{0,32},{16,48},{32,0},{48,16},{64,96},{80,112},{96,64},{112,80},{1... | collective-permute-start | bytes 1179656 | tf_op jit(solution)/shard_map/ppermute | solution.py:266
  10.3 1.9 %collective-permute-start.1 = (f32[64,1536]{1,0:T(8,128)S(1)}, f32[64,1536]{1,0:T(8,128)S(1)}, u32[]{:S(2)}, u32[]{:S(2)}) collective-permute-start(f32[64,1536]{1,0:T(8,128)S(1)} %pad_maximum_fusion.refs_0_), channel_id=1, source_target_pairs={{0,96},{16,112},{32,64},{48,80},{64,32},{80,48},{96,0},{112,16},{1... | collective-permute-start | bytes 1179656 | tf_op jit(solution)/shard_map/ppermute | solution.py:266
  12.2 1.9 %collective-permute-start.5 = (f32[64,1536]{1,0:T(8,128)S(1)}, f32[64,1536]{1,0:T(8,128)S(1)}, u32[]{:S(2)}, u32[]{:S(2)}) collective-permute-start(f32[64,1536]{1,0:T(8,128)S(1)} %pad_maximum_fusion.refs_0_), channel_id=1, source_target_pairs={{0,16},{16,0},{32,48},{48,32},{64,80},{80,64},{96,112},{112,96},{1... | collective-permute-start | bytes 1179656 | tf_op jit(solution)/shard_map/ppermute | solution.py:266
  14.1 3.2 %collective-permute-done.3.refs_1_ = f32[64,1536]{1,0:T(8,128)S(1)} collective-permute-done((f32[64,1536]{1,0:T(8,128)S(1)}, f32[64,1536]{1,0:T(8,128)S(1)}, u32[]{:S(2)}, u32[]{:S(2)}) %collective-permute-start.3) | collective-permute-done | bytes 393248 | tf_op jit(solution)/shard_map/ppermute | solution.py:266
  17.3 3.0 %collective-permute-start.6 = (f32[64,1536]{1,0:T(8,128)S(1)}, f32[64,1536]{1,0:T(8,128)S(1)}, u32[]{:S(2)}, u32[]{:S(2)}) collective-permute-start(f32[64,1536]{1,0:T(8,128)S(1)} %collective-permute-done.3.refs_1_), channel_id=1, source_target_pairs={{0,16},{16,0},{32,48},{48,32},{64,80},{80,64},{96,112},{112,96},{1... | collective-permute-start | bytes 1179656 | tf_op jit(solution)/shard_map/ppermute | solution.py:266
  20.4 0.1 collective-permute-done.1.refs_2_
  20.5 2.6 %collective-permute-start.7 = (f32[64,1536]{1,0:T(8,128)S(1)}, f32[64,1536]{1,0:T(8,128)S(1)}, u32[]{:S(2)}, u32[]{:S(2)}) collective-permute-start(f32[64,1536]{1,0:T(8,128)S(1)} %collective-permute-done.1.refs_2_), channel_id=1, source_target_pairs={{0,16},{16,0},{32,48},{48,32},{64,80},{80,64},{96,112},{112,96},{1... | collective-permute-start | bytes 1179656 | tf_op jit(solution)/shard_map/ppermute | solution.py:266
  23.0 0.1 collective-permute-start.2
  23.2 2.0 %collective-permute-start.4 = (f32[32,1536]{1,0:T(8,128)S(1)}, f32[32,1536]{1,0:T(8,128)S(1)}, u32[]{:S(2)}, u32[]{:S(2)}) collective-permute-start(f32[32,1536]{1,0:T(8,128)S(1)} %slice.9), channel_id=1, source_target_pairs={{0,96},{16,112},{32,64},{48,80},{64,32},{80,48},{96,0},{112,16},{1... | collective-permute-start | bytes 589832 | tf_op jit(solution)/shard_map/ppermute | solution.py:266
  25.2 0.0 collective-permute-done.5.refs_3_
  25.2 0.0 collective-permute-done.6.refs_4_
  25.2 0.0 collective-permute-done.7.refs_5_
  25.2 2.1 %shard_map.59 = (f32[64,512]{1,0:T(8,128)S(1)}, bf16[512,1536]{1,0:T(8,128)(2,1)S(1)}, bf16[512,1536]{1,0:T(8,128)(2,1)S(1)}) custom-call(s32[1]{0:T(128)} %bitcast.3.me_ref, f32[64,1536]{1,0:T(8,128)S(1)} %pad_maximum_fusion.refs_0_, f32[64,1536]{1,0:T(8,128)S(1)} %collective-permute-done.3.refs_1_, f32[64,1536]{1,0:T(8,128)S(1)} %collective-permute-done.1.refs_2_, ...), custom_call_target="tpu_custom_call" | custom-call | flops 603979776 | bytes 6291456 | tf_op jit(solution)/shard_map/pallas_call | solution.py:30
  27.3 0.0 copy-start.1
  27.3 0.6 copy-done.1
  27.9 1.7 %collective-permute-done.2.refs_0_ = f32[32,1536]{1,0:T(8,128)S(1)} collective-permute-done((f32[32,1536]{1,0:T(8,128)S(1)}, f32[32,1536]{1,0:T(8,128)S(1)}, u32[]{:S(2)}, u32[]{:S(2)}) %collective-permute-start.2) | collective-permute-done | bytes 196640 | tf_op jit(solution)/shard_map/ppermute | solution.py:266
  29.7 1.3 %collective-permute-done.4.refs_1_ = f32[32,1536]{1,0:T(8,128)S(1)} collective-permute-done((f32[32,1536]{1,0:T(8,128)S(1)}, f32[32,1536]{1,0:T(8,128)S(1)}, u32[]{:S(2)}, u32[]{:S(2)}) %collective-permute-start.4) | collective-permute-done | bytes 196640 | tf_op jit(solution)/shard_map/ppermute | solution.py:266
  31.0 0.8 collective-permute-start.8
  31.8 0.0 collective-permute-start.9
  31.8 0.1 pad_add_fusion.at_ref
  31.9 1.2 %collective-permute-start.10 = (f32[64,512]{1,0:T(8,128)}, f32[64,512]{1,0:T(8,128)S(1)}, u32[]{:S(2)}, u32[]{:S(2)}) collective-permute-start(f32[64,512]{1,0:T(8,128)} %copy-done.1), channel_id=1, source_target_pairs={{0,1},{1,0},{2,3},{3,2},{4,5},{5,4},{6,7},{7,6},{8,9},{9,8},{10,11... | collective-permute-start | bytes 393224 | tf_op jit(solution)/shard_map/ppermute | solution.py:266
  33.1 2.5 %collective-permute-start.11 = (f32[64,512]{1,0:T(8,128)}, f32[64,512]{1,0:T(8,128)S(1)}, u32[]{:S(2)}, u32[]{:S(2)}) collective-permute-start(f32[64,512]{1,0:T(8,128)} %copy-done.1), channel_id=1, source_target_pairs={{0,2},{1,3},{2,0},{3,1},{4,6},{5,7},{6,4},{7,5},{8,10},{9,11},{10,... | collective-permute-start | bytes 393224 | tf_op jit(solution)/shard_map/ppermute | solution.py:266
  35.5 0.2 collective-permute-start.12
  35.7 0.0 collective-permute-done.8.refs_2_
  35.7 1.1 %shard_map.60 = (bf16[512,1536]{1,0:T(8,128)(2,1)S(1)}, bf16[512,1536]{1,0:T(8,128)(2,1)S(1)}) custom-call(s32[1]{0:T(128)} %bitcast.3.me_ref, f32[32,1536]{1,0:T(8,128)S(1)} %collective-permute-done.2.refs_0_, f32[32,1536]{1,0:T(8,128)S(1)} %collective-permute-done.4.refs_1_, ...), custom_call_target="tpu_custom_call", output_to_operand_aliasing={{0}: (5, {}), {1}: (6, {})} | custom-call | bytes 1572864 | tf_op jit(solution)/shard_map/pallas_call | solution.py:30
  36.9 0.0 copy-start.2
  36.9 7.8 %shard_map.61 = (f32[2,256,256]{2,1,0:T(8,128)S(1)}, f32[2,256,256]{2,1,0:T(8,128)S(1)}, f32[2,256,256]{2,1,0:T(8,128)S(1)}, f32[2,256,256]{2,1,0:T(8,128)S(1)}) custom-call(s32[2]{0:T(128)S(1)} %pad_add_fusion.at_ref, f32[4,4,64,1536]{3,2,1,0:T(8,128)} %bitcast.4, bf16[512,1536]{1,0:T(8,128)(2,1)S(1)} %get-tuple-element.31.hi_ref, ...), custom_call_target="tpu_custom_call" | custom-call | flops 7247757312 | bytes 6291456 | tf_op jit(solution)/shard_map/pallas_call | solution.py:30
  44.7 0.0 collective-permute-done.10
  44.7 0.0 collective-permute-done.12
  44.7 0.1 collective-permute-start.13
  44.8 2.6 %collective-permute-start.14 = (f32[2,256,256]{2,1,0:T(8,128)S(1)}, f32[2,256,256]{2,1,0:T(8,128)S(1)}, u32[]{:S(2)}, u32[]{:S(2)}) collective-permute-start(f32[2,256,256]{2,1,0:T(8,128)S(1)} %get-tuple-element.38), channel_id=1, source_target_pairs={{0,3},{1,2},{2,1},{3,0},{4,7},{5,6},{6,5},{7,4},{8,11},{9,10},{10,... | collective-permute-start | bytes 1572872 | tf_op jit(solution)/shard_map/ppermute | solution.py:266
  47.4 6.2 %collective-permute-start.20 = (f32[64,512]{1,0:T(8,128)S(1)}, f32[64,512]{1,0:T(8,128)S(1)}, u32[]{:S(2)}, u32[]{:S(2)}) collective-permute-start(f32[64,512]{1,0:T(8,128)S(1)} %add_add_fusion.1), channel_id=1, source_target_pairs={{136,0},{140,4},{128,8},{132,12},{152,16},{156,20},{144,24},{148,2... | collective-permute-start | bytes 393224 | tf_op jit(solution)/shard_map/ppermute | solution.py:283
  53.6 0.4 collective-permute-start.22
  54.0 2.9 %collective-permute-done.13.a_got = f32[2,256,256]{2,1,0:T(8,128)S(1)} collective-permute-done((f32[2,256,256]{2,1,0:T(8,128)S(1)}, f32[2,256,256]{2,1,0:T(8,128)S(1)}, u32[]{:S(2)}, u32[]{:S(2)}) %collective-permute-start.13) | collective-permute-done | bytes 524320 | tf_op jit(solution)/shard_map/ppermute | solution.py:266
  56.9 1.1 %collective-permute-done.14.b_got = f32[2,256,256]{2,1,0:T(8,128)S(1)} collective-permute-done((f32[2,256,256]{2,1,0:T(8,128)S(1)}, f32[2,256,256]{2,1,0:T(8,128)S(1)}, u32[]{:S(2)}, u32[]{:S(2)}) %collective-permute-start.14) | collective-permute-done | bytes 524320 | tf_op jit(solution)/shard_map/ppermute | solution.py:266
  58.0 0.1 shard_map.62
  58.1 2.7 %collective-permute-start.15 = (f32[256,256]{1,0:T(8,128)S(1)}, f32[256,256]{1,0:T(8,128)S(1)}, u32[]{:S(2)}, u32[]{:S(2)}) collective-permute-start(f32[256,256]{1,0:T(8,128)S(1)} %get-tuple-element.39), channel_id=1, source_target_pairs={{0,3},{1,2},{2,1},{3,0},{4,7},{5,6},{6,5},{7,4},{8,11},{9,10},{10,... | collective-permute-start | bytes 786440 | tf_op jit(solution)/shard_map/ppermute | solution.py:266
  60.8 0.0 collective-permute-done.20
  60.8 0.9 collective-permute-done.21
  61.7 3.5 %collective-permute-done.22 = f32[64,512]{1,0:T(8,128)S(1)} collective-permute-done((f32[64,512]{1,0:T(8,128)S(1)}, f32[64,512]{1,0:T(8,128)S(1)}, u32[]{:S(2)}, u32[]{:S(2)}) %collective-permute-start.22) | collective-permute-done | bytes 131104 | tf_op jit(solution)/shard_map/ppermute | solution.py:283
  65.2 0.3 collective-permute-start.23
  65.5 2.8 %collective-permute-start.24 = (f32[64,512]{1,0:T(8,128)S(1)}, f32[64,512]{1,0:T(8,128)S(1)}, u32[]{:S(2)}, u32[]{:S(2)}) collective-permute-start(f32[64,512]{1,0:T(8,128)S(1)} %add_add_fusion.refs_0_), channel_id=1, source_target_pairs={{0,64},{16,80},{32,96},{48,112},{64,0},{80,16},{96,32},{112,48},{1... | collective-permute-start | bytes 393224 | tf_op jit(solution)/shard_map/ppermute | solution.py:266
  68.4 0.8 collective-permute-start.25
  69.1 0.2 collective-permute-done.23.refs_1_
  69.3 3.3 %collective-permute-start.26 = (f32[64,512]{1,0:T(8,128)S(1)}, f32[64,512]{1,0:T(8,128)S(1)}, u32[]{:S(2)}, u32[]{:S(2)}) collective-permute-start(f32[64,512]{1,0:T(8,128)S(1)} %add_add_fusion.refs_0_), channel_id=1, source_target_pairs={{0,16},{16,0},{32,48},{48,32},{64,80},{80,64},{96,112},{112,96},{1... | collective-permute-start | bytes 393224 | tf_op jit(solution)/shard_map/ppermute | solution.py:266
  72.6 0.0 collective-permute-done.24.refs_2_
  72.6 3.1 %collective-permute-start.27 = (f32[64,512]{1,0:T(8,128)S(1)}, f32[64,512]{1,0:T(8,128)S(1)}, u32[]{:S(2)}, u32[]{:S(2)}) collective-permute-start(f32[64,512]{1,0:T(8,128)S(1)} %collective-permute-done.23.refs_1_), channel_id=1, source_target_pairs={{0,16},{16,0},{32,48},{48,32},{64,80},{80,64},{96,112},{112,96},{1... | collective-permute-start | bytes 393224 | tf_op jit(solution)/shard_map/ppermute | solution.py:266
  75.7 0.0 collective-permute-done.25.refs_3_
  75.7 1.5 %collective-permute-start.28 = (f32[64,512]{1,0:T(8,128)S(1)}, f32[64,512]{1,0:T(8,128)S(1)}, u32[]{:S(2)}, u32[]{:S(2)}) collective-permute-start(f32[64,512]{1,0:T(8,128)S(1)} %collective-permute-done.24.refs_2_), channel_id=1, source_target_pairs={{0,16},{16,0},{32,48},{48,32},{64,80},{80,64},{96,112},{112,96},{1... | collective-permute-start | bytes 393224 | tf_op jit(solution)/shard_map/ppermute | solution.py:266
  77.2 0.0 collective-permute-done.15.a_last
  77.2 0.0 collective-permute-start.29
  77.2 0.0 collective-permute-done.16.b_last
  77.2 0.1 shard_map.63
  77.3 1.0 %collective-permute-start.17 = (f32[64,512]{1,0:T(8,128)S(1)}, f32[64,512]{1,0:T(8,128)S(1)}, u32[]{:S(2)}, u32[]{:S(2)}) collective-permute-start(f32[64,512]{1,0:T(8,128)S(1)} %get-tuple-element.42), channel_id=1, source_target_pairs={{0,4},{4,0},{8,12},{12,8},{1,5},{5,1},{9,13},{13,9},{2,6},{6,2},{1... | collective-permute-start | bytes 393224 | tf_op jit(solution)/shard_map/ppermute | solution.py:266
  78.3 0.0 collective-permute-done.26.refs_4_
  78.3 3.9 %collective-permute-start.18 = (f32[64,512]{1,0:T(8,128)S(1)}, f32[64,512]{1,0:T(8,128)S(1)}, u32[]{:S(2)}, u32[]{:S(2)}) collective-permute-start(f32[64,512]{1,0:T(8,128)S(1)} %get-tuple-element.43), channel_id=1, source_target_pairs={{0,8},{4,12},{8,0},{12,4},{1,9},{5,13},{9,1},{13,5},{2,10},{6,14},... | collective-permute-start | bytes 393224 | tf_op jit(solution)/shard_map/ppermute | solution.py:266
  82.3 0.0 collective-permute-done.27.refs_5_
  82.3 0.8 collective-permute-start.19
  83.1 0.0 collective-permute-done.28.refs_6_
  83.1 14.7 %shard_map.64 = (f32[512,512]{1,0:T(8,128)}, f32[512,512]{1,0:T(8,128)S(1)}) custom-call(s32[1]{0:T(128)} %bitcast.3.me_ref, f32[512,512]{1,0:T(8,128)S(1)} %copy-done.3, f32[64,512]{1,0:T(8,128)S(1)} %add_add_fusion.refs_0_, f32[64,512]{1,0:T(8,128)S(1)} %collective-permute-done.23.refs_1_, f32[64,512]{1,0:T(8,128)S(1)} %collective-permute-done.24.refs_2_, ...), custom_call_target="tpu_custom_call" | custom-call | flops 16106127360 | bytes 4194304 | tf_op jit(solution)/shard_map/pallas_call | solution.py:30
  97.8 1.3 %shard_map.65 = f32[64,512]{1,0:T(8,128)} custom-call(f32[64,512]{1,0:T(8,128)S(1)} %copy-done, f32[64,512]{1,0:T(8,128)S(1)} %get-tuple-element.41.p0, f32[64,512]{1,0:T(8,128)S(1)} %collective-permute-done.17.p1, f32[64,512]{1,0:T(8,128)S(1)} %collective-permute-done.18.p2, f32[64,512]{1,0:T(8,128)S(1)} %collective-permute-done.19.p3, ...), custom_call_target="tpu_custom_call" | custom-call | flops 100663296 | bytes 2097152 | tf_op jit(solution)/shard_map/pallas_call | solution.py:30
  (18 shorter events, 0.2 us)
Async XLA Ops:
  0.6 6.4 %collective-permute-start = (f32[32,1536]{1,0:T(8,128)}, f32[32,1536]{1,0:T(8,128)S(1)}, u32[]{:S(2)}, u32[]{:S(2)}) collective-permute-start(f32[32,1536]{1,0:T(8,128)} %param.5), channel_id=1, source_target_pairs={{0,128},{16,144},{32,160},{48,176},{64,192},{80,208},{96,224},{112... | collective-permute-start | bytes 589832 | tf_op jit(solution)/shard_map/ppermute | solution.py:266
  8.1 9.3 %collective-permute-start.3 = (f32[64,1536]{1,0:T(8,128)S(1)}, f32[64,1536]{1,0:T(8,128)S(1)}, u32[]{:S(2)}, u32[]{:S(2)}) collective-permute-start(f32[64,1536]{1,0:T(8,128)S(1)} %pad_maximum_fusion.refs_0_), channel_id=1, source_target_pairs={{0,32},{16,48},{32,0},{48,16},{64,96},{80,112},{96,64},{112,80},{1... | collective-permute-start | bytes 1179656 | tf_op jit(solution)/shard_map/ppermute | solution.py:266
  10.3 10.2 %collective-permute-start.1 = (f32[64,1536]{1,0:T(8,128)S(1)}, f32[64,1536]{1,0:T(8,128)S(1)}, u32[]{:S(2)}, u32[]{:S(2)}) collective-permute-start(f32[64,1536]{1,0:T(8,128)S(1)} %pad_maximum_fusion.refs_0_), channel_id=1, source_target_pairs={{0,96},{16,112},{32,64},{48,80},{64,32},{80,48},{96,0},{112,16},{1... | collective-permute-start | bytes 1179656 | tf_op jit(solution)/shard_map/ppermute | solution.py:266
  12.2 13.0 %collective-permute-start.5 = (f32[64,1536]{1,0:T(8,128)S(1)}, f32[64,1536]{1,0:T(8,128)S(1)}, u32[]{:S(2)}, u32[]{:S(2)}) collective-permute-start(f32[64,1536]{1,0:T(8,128)S(1)} %pad_maximum_fusion.refs_0_), channel_id=1, source_target_pairs={{0,16},{16,0},{32,48},{48,32},{64,80},{80,64},{96,112},{112,96},{1... | collective-permute-start | bytes 1179656 | tf_op jit(solution)/shard_map/ppermute | solution.py:266
  17.3 7.8 %collective-permute-start.6 = (f32[64,1536]{1,0:T(8,128)S(1)}, f32[64,1536]{1,0:T(8,128)S(1)}, u32[]{:S(2)}, u32[]{:S(2)}) collective-permute-start(f32[64,1536]{1,0:T(8,128)S(1)} %collective-permute-done.3.refs_1_), channel_id=1, source_target_pairs={{0,16},{16,0},{32,48},{48,32},{64,80},{80,64},{96,112},{112,96},{1... | collective-permute-start | bytes 1179656 | tf_op jit(solution)/shard_map/ppermute | solution.py:266
  20.5 4.7 %collective-permute-start.7 = (f32[64,1536]{1,0:T(8,128)S(1)}, f32[64,1536]{1,0:T(8,128)S(1)}, u32[]{:S(2)}, u32[]{:S(2)}) collective-permute-start(f32[64,1536]{1,0:T(8,128)S(1)} %collective-permute-done.1.refs_2_), channel_id=1, source_target_pairs={{0,16},{16,0},{32,48},{48,32},{64,80},{80,64},{96,112},{112,96},{1... | collective-permute-start | bytes 1179656 | tf_op jit(solution)/shard_map/ppermute | solution.py:266
  23.0 6.6 %collective-permute-start.2 = (f32[32,1536]{1,0:T(8,128)S(1)}, f32[32,1536]{1,0:T(8,128)S(1)}, u32[]{:S(2)}, u32[]{:S(2)}) collective-permute-start(f32[32,1536]{1,0:T(8,128)S(1)} %slice.8), channel_id=1, source_target_pairs={{0,32},{16,48},{32,0},{48,16},{64,96},{80,112},{96,64},{112,80},{1... | collective-permute-start | bytes 589832 | tf_op jit(solution)/shard_map/ppermute | solution.py:266
  23.2 7.8 %collective-permute-start.4 = (f32[32,1536]{1,0:T(8,128)S(1)}, f32[32,1536]{1,0:T(8,128)S(1)}, u32[]{:S(2)}, u32[]{:S(2)}) collective-permute-start(f32[32,1536]{1,0:T(8,128)S(1)} %slice.9), channel_id=1, source_target_pairs={{0,96},{16,112},{32,64},{48,80},{64,32},{80,48},{96,0},{112,16},{1... | collective-permute-start | bytes 589832 | tf_op jit(solution)/shard_map/ppermute | solution.py:266
  27.3 0.7 copy-start.1
  31.0 4.7 %collective-permute-start.8 = (f32[32,1536]{1,0:T(8,128)S(1)}, f32[32,1536]{1,0:T(8,128)}, u32[]{:S(2)}, u32[]{:S(2)}) collective-permute-start(f32[32,1536]{1,0:T(8,128)S(1)} %collective-permute-done.2.refs_0_), channel_id=1, source_target_pairs={{0,16},{16,0},{32,48},{48,32},{64,80},{80,64},{96,112},{112,96},{1... | collective-permute-start | bytes 589832 | tf_op jit(solution)/shard_map/ppermute | solution.py:266
  31.8 4.0 %collective-permute-start.9 = (f32[32,1536]{1,0:T(8,128)S(1)}, f32[32,1536]{1,0:T(8,128)}, u32[]{:S(2)}, u32[]{:S(2)}) collective-permute-start(f32[32,1536]{1,0:T(8,128)S(1)} %collective-permute-done.4.refs_1_), channel_id=1, source_target_pairs={{0,16},{16,0},{32,48},{48,32},{64,80},{80,64},{96,112},{112,96},{1... | collective-permute-start | bytes 589832 | tf_op jit(solution)/shard_map/ppermute | solution.py:266
  31.9 12.8 %collective-permute-start.10 = (f32[64,512]{1,0:T(8,128)}, f32[64,512]{1,0:T(8,128)S(1)}, u32[]{:S(2)}, u32[]{:S(2)}) collective-permute-start(f32[64,512]{1,0:T(8,128)} %copy-done.1), channel_id=1, source_target_pairs={{0,1},{1,0},{2,3},{3,2},{4,5},{5,4},{6,7},{7,6},{8,9},{9,8},{10,11... | collective-permute-start | bytes 393224 | tf_op jit(solution)/shard_map/ppermute | solution.py:266
  33.1 11.6 %collective-permute-start.11 = (f32[64,512]{1,0:T(8,128)}, f32[64,512]{1,0:T(8,128)S(1)}, u32[]{:S(2)}, u32[]{:S(2)}) collective-permute-start(f32[64,512]{1,0:T(8,128)} %copy-done.1), channel_id=1, source_target_pairs={{0,2},{1,3},{2,0},{3,1},{4,6},{5,7},{6,4},{7,5},{8,10},{9,11},{10,... | collective-permute-start | bytes 393224 | tf_op jit(solution)/shard_map/ppermute | solution.py:266
  35.5 9.2 %collective-permute-start.12 = (f32[64,512]{1,0:T(8,128)}, f32[64,512]{1,0:T(8,128)S(1)}, u32[]{:S(2)}, u32[]{:S(2)}) collective-permute-start(f32[64,512]{1,0:T(8,128)} %copy-done.1), channel_id=1, source_target_pairs={{0,3},{1,2},{2,1},{3,0},{4,7},{5,6},{6,5},{7,4},{8,11},{9,10},{10,... | collective-permute-start | bytes 393224 | tf_op jit(solution)/shard_map/ppermute | solution.py:266
  36.9 10.5 %copy-start.2 = (f32[64,512]{1,0:T(8,128)S(1)}, f32[64,512]{1,0:T(8,128)}, u32[]{:S(2)}) copy-start(f32[64,512]{1,0:T(8,128)} %copy-done.1) | copy-start | bytes 393220
  44.7 12.2 %collective-permute-start.13 = (f32[2,256,256]{2,1,0:T(8,128)S(1)}, f32[2,256,256]{2,1,0:T(8,128)S(1)}, u32[]{:S(2)}, u32[]{:S(2)}) collective-permute-start(f32[2,256,256]{2,1,0:T(8,128)S(1)} %get-tuple-element.36), channel_id=1, source_target_pairs={{0,1},{1,0},{2,3},{3,2},{4,5},{5,4},{6,7},{7,6},{8,9},{9,8},{10,11... | collective-permute-start | bytes 1572872 | tf_op jit(solution)/shard_map/ppermute | solution.py:266
  44.8 13.2 %collective-permute-start.14 = (f32[2,256,256]{2,1,0:T(8,128)S(1)}, f32[2,256,256]{2,1,0:T(8,128)S(1)}, u32[]{:S(2)}, u32[]{:S(2)}) collective-permute-start(f32[2,256,256]{2,1,0:T(8,128)S(1)} %get-tuple-element.38), channel_id=1, source_target_pairs={{0,3},{1,2},{2,1},{3,0},{4,7},{5,6},{6,5},{7,4},{8,11},{9,10},{10,... | collective-permute-start | bytes 1572872 | tf_op jit(solution)/shard_map/ppermute | solution.py:266
  47.4 13.4 %collective-permute-start.20 = (f32[64,512]{1,0:T(8,128)S(1)}, f32[64,512]{1,0:T(8,128)S(1)}, u32[]{:S(2)}, u32[]{:S(2)}) collective-permute-start(f32[64,512]{1,0:T(8,128)S(1)} %add_add_fusion.1), channel_id=1, source_target_pairs={{136,0},{140,4},{128,8},{132,12},{152,16},{156,20},{144,24},{148,2... | collective-permute-start | bytes 393224 | tf_op jit(solution)/shard_map/ppermute | solution.py:283
  53.6 8.1 %collective-permute-start.21 = (f32[64,512]{1,0:T(8,128)S(1)}, f32[64,512]{1,0:T(8,128)S(1)}, u32[]{:S(2)}, u32[]{:S(2)}) collective-permute-start(f32[64,512]{1,0:T(8,128)S(1)} %add_add_fusion.1), channel_id=1, source_target_pairs={{140,0},{128,4},{132,8},{136,12},{156,16},{144,20},{148,24},{152,2... | collective-permute-start | bytes 393224 | tf_op jit(solution)/shard_map/ppermute | solution.py:283
  53.6 11.6 %collective-permute-start.22 = (f32[64,512]{1,0:T(8,128)S(1)}, f32[64,512]{1,0:T(8,128)S(1)}, u32[]{:S(2)}, u32[]{:S(2)}) collective-permute-start(f32[64,512]{1,0:T(8,128)S(1)} %add_add_fusion.1), channel_id=1, source_target_pairs={{4,0},{8,4},{12,8},{0,12},{20,16},{24,20},{28,24},{16,28},{36,32},... | collective-permute-start | bytes 393224 | tf_op jit(solution)/shard_map/ppermute | solution.py:283
  58.1 19.1 %collective-permute-start.15 = (f32[256,256]{1,0:T(8,128)S(1)}, f32[256,256]{1,0:T(8,128)S(1)}, u32[]{:S(2)}, u32[]{:S(2)}) collective-permute-start(f32[256,256]{1,0:T(8,128)S(1)} %get-tuple-element.39), channel_id=1, source_target_pairs={{0,3},{1,2},{2,1},{3,0},{4,7},{5,6},{6,5},{7,4},{8,11},{9,10},{10,... | collective-permute-start | bytes 786440 | tf_op jit(solution)/shard_map/ppermute | solution.py:266
  60.8 22.3 %copy-start.3 = (f32[512,512]{1,0:T(8,128)S(1)}, f32[512,512]{1,0:T(8,128)}, u32[]{:S(2)}) copy-start(f32[512,512]{1,0:T(8,128)} %diag_ref.1) | copy-start | bytes 3145732
  60.8 16.4 %collective-permute-start.16 = (f32[256,256]{1,0:T(8,128)S(1)}, f32[256,256]{1,0:T(8,128)S(1)}, u32[]{:S(2)}, u32[]{:S(2)}) collective-permute-start(f32[256,256]{1,0:T(8,128)S(1)} %get-tuple-element.40), channel_id=1, source_target_pairs={{0,1},{1,0},{2,3},{3,2},{4,5},{5,4},{6,7},{7,6},{8,9},{9,8},{10,11... | collective-permute-start | bytes 786440 | tf_op jit(solution)/shard_map/ppermute | solution.py:266
  65.2 4.1 %collective-permute-start.23 = (f32[64,512]{1,0:T(8,128)S(1)}, f32[64,512]{1,0:T(8,128)S(1)}, u32[]{:S(2)}, u32[]{:S(2)}) collective-permute-start(f32[64,512]{1,0:T(8,128)S(1)} %add_add_fusion.refs_0_), channel_id=1, source_target_pairs={{0,32},{16,48},{32,0},{48,16},{64,96},{80,112},{96,64},{112,80},{1... | collective-permute-start | bytes 393224 | tf_op jit(solution)/shard_map/ppermute | solution.py:266
  65.5 7.1 %collective-permute-start.24 = (f32[64,512]{1,0:T(8,128)S(1)}, f32[64,512]{1,0:T(8,128)S(1)}, u32[]{:S(2)}, u32[]{:S(2)}) collective-permute-start(f32[64,512]{1,0:T(8,128)S(1)} %add_add_fusion.refs_0_), channel_id=1, source_target_pairs={{0,64},{16,80},{32,96},{48,112},{64,0},{80,16},{96,32},{112,48},{1... | collective-permute-start | bytes 393224 | tf_op jit(solution)/shard_map/ppermute | solution.py:266
  68.4 7.4 %collective-permute-start.25 = (f32[64,512]{1,0:T(8,128)S(1)}, f32[64,512]{1,0:T(8,128)S(1)}, u32[]{:S(2)}, u32[]{:S(2)}) collective-permute-start(f32[64,512]{1,0:T(8,128)S(1)} %add_add_fusion.refs_0_), channel_id=1, source_target_pairs={{0,96},{16,112},{32,64},{48,80},{64,32},{80,48},{96,0},{112,16},{1... | collective-permute-start | bytes 393224 | tf_op jit(solution)/shard_map/ppermute | solution.py:266
  69.3 9.0 %collective-permute-start.26 = (f32[64,512]{1,0:T(8,128)S(1)}, f32[64,512]{1,0:T(8,128)S(1)}, u32[]{:S(2)}, u32[]{:S(2)}) collective-permute-start(f32[64,512]{1,0:T(8,128)S(1)} %add_add_fusion.refs_0_), channel_id=1, source_target_pairs={{0,16},{16,0},{32,48},{48,32},{64,80},{80,64},{96,112},{112,96},{1... | collective-permute-start | bytes 393224 | tf_op jit(solution)/shard_map/ppermute | solution.py:266
  72.6 9.6 %collective-permute-start.27 = (f32[64,512]{1,0:T(8,128)S(1)}, f32[64,512]{1,0:T(8,128)S(1)}, u32[]{:S(2)}, u32[]{:S(2)}) collective-permute-start(f32[64,512]{1,0:T(8,128)S(1)} %collective-permute-done.23.refs_1_), channel_id=1, source_target_pairs={{0,16},{16,0},{32,48},{48,32},{64,80},{80,64},{96,112},{112,96},{1... | collective-permute-start | bytes 393224 | tf_op jit(solution)/shard_map/ppermute | solution.py:266
  75.7 7.3 %collective-permute-start.28 = (f32[64,512]{1,0:T(8,128)S(1)}, f32[64,512]{1,0:T(8,128)S(1)}, u32[]{:S(2)}, u32[]{:S(2)}) collective-permute-start(f32[64,512]{1,0:T(8,128)S(1)} %collective-permute-done.24.refs_2_), channel_id=1, source_target_pairs={{0,16},{16,0},{32,48},{48,32},{64,80},{80,64},{96,112},{112,96},{1... | collective-permute-start | bytes 393224 | tf_op jit(solution)/shard_map/ppermute | solution.py:266
  77.2 5.9 %collective-permute-start.29 = (f32[64,512]{1,0:T(8,128)S(1)}, f32[64,512]{1,0:T(8,128)S(1)}, u32[]{:S(2)}, u32[]{:S(2)}) collective-permute-start(f32[64,512]{1,0:T(8,128)S(1)} %collective-permute-done.25.refs_3_), channel_id=1, source_target_pairs={{0,16},{16,0},{32,48},{48,32},{64,80},{80,64},{96,112},{112,96},{1... | collective-permute-start | bytes 393224 | tf_op jit(solution)/shard_map/ppermute | solution.py:266
  77.3 20.5 %collective-permute-start.17 = (f32[64,512]{1,0:T(8,128)S(1)}, f32[64,512]{1,0:T(8,128)S(1)}, u32[]{:S(2)}, u32[]{:S(2)}) collective-permute-start(f32[64,512]{1,0:T(8,128)S(1)} %get-tuple-element.42), channel_id=1, source_target_pairs={{0,4},{4,0},{8,12},{12,8},{1,5},{5,1},{9,13},{13,9},{2,6},{6,2},{1... | collective-permute-start | bytes 393224 | tf_op jit(solution)/shard_map/ppermute | solution.py:266
  78.3 19.4 %collective-permute-start.18 = (f32[64,512]{1,0:T(8,128)S(1)}, f32[64,512]{1,0:T(8,128)S(1)}, u32[]{:S(2)}, u32[]{:S(2)}) collective-permute-start(f32[64,512]{1,0:T(8,128)S(1)} %get-tuple-element.43), channel_id=1, source_target_pairs={{0,8},{4,12},{8,0},{12,4},{1,9},{5,13},{9,1},{13,5},{2,10},{6,14},... | collective-permute-start | bytes 393224 | tf_op jit(solution)/shard_map/ppermute | solution.py:266
  82.3 15.5 %copy-start = (f32[64,512]{1,0:T(8,128)S(1)}, f32[64,512]{1,0:T(8,128)}, u32[]{:S(2)}) copy-start(f32[64,512]{1,0:T(8,128)} %below_ref.1) | copy-start | bytes 393220
  82.3 15.5 %collective-permute-start.19 = (f32[64,512]{1,0:T(8,128)S(1)}, f32[64,512]{1,0:T(8,128)S(1)}, u32[]{:S(2)}, u32[]{:S(2)}) collective-permute-start(f32[64,512]{1,0:T(8,128)S(1)} %get-tuple-element.44), channel_id=1, source_target_pairs={{0,12},{4,8},{8,4},{12,0},{1,13},{5,9},{9,5},{13,1},{2,14},{6,10},... | collective-permute-start | bytes 393224 | tf_op jit(solution)/shard_map/ppermute | solution.py:266

commit v3 on v2

--- a/solution.py
+++ b/solution.py
@@ -46,6 +46,13 @@
 
 def slot_of(shape, size):
     return lax.rem(lax.broadcasted_iota(jnp.int32, shape, 1) // (2 * size), 4)
+
+
+def join_kernel(me_ref, mine_ref, other_ref, out_ref):
+    size = mine_ref.shape[0]
+    z = me_ref[0] // 8
+    out_ref[pl.ds(pl.multiple_of(z * size, size), size), :] = mine_ref[...]
+    out_ref[pl.ds(pl.multiple_of((1 - z) * size, size), size), :] = other_ref[...]
 
 
 def schur_kernel(me_ref, *refs):
@@ -78,31 +85,51 @@
             hi_ref[at, :], lo_ref[at, :] = split(pieces[core_step * 2 + z][...])
 
 
-def long_dot(rows, hi, lo):
-    left_hi, left_lo = split(rows)
+def split_kernel(x_ref, hi_ref, lo_ref):
+    hi_ref[...], lo_ref[...] = split(x_ref[...])
+
+
+def split_rows(x, block):
+    rows, depth = x.shape
+    spec = pl.BlockSpec((block, depth), lambda i: (i, 0))
+    return pl.pallas_call(
+        split_kernel,
+        out_shape=(jax.ShapeDtypeStruct(x.shape, BF16),) * 2,
+        grid=(rows // block,),
+        in_specs=[spec],
+        out_specs=(spec, spec),
+        cost_estimate=pl.CostEstimate(flops=2 * x.size, bytes_accessed=8 * x.size, transcendentals=0),
+        compiler_params=pltpu.CompilerParams(vmem_limit_bytes=56 * 2**20),
+    )(x)
+
+
+def long_dot(left_hi, left_lo, hi, lo):
     left = jnp.concatenate([left_hi, left_lo, left_hi], 1)
     right = jnp.concatenate([lo, hi, hi], 1)
     return lax.dot_general(left, right, NT, preferred_element_type=F32)
 
 
-def product_kernel(at_ref, below_ref, hi_ref, lo_ref, a_send, b_send, a_keep, b_keep, held, sems):
+def product_kernel(at_ref, below_hi, below_lo, hi_ref, lo_ref, a_send, b_send, a_keep, b_keep, held_hi, held_lo, sems):
     near, far = at_ref[0], at_ref[1]
-    near_n, _, share, _ = below_ref.shape
+    near_n, _, share, _ = below_hi.shape
     half = a_send.shape[2]
     groups = ((1, 2), (3, 0))
     copies = {}
     for k in (1, 2, 3, 0):
         for j in range(near_n):
-            to = held.at[k, pl.ds(j * share, share)]
-            copies[k, j] = pltpu.make_async_copy(below_ref.at[near ^ j, far ^ k], to, sems.at[k, j])
-            copies[k, j].start()
+            for i, (source, held) in enumerate(((below_hi, held_hi), (below_lo, held_lo))):
+                to = held.at[k, pl.ds(j * share, share)]
+                copies[k, j, i] = pltpu.make_async_copy(source.at[near ^ j, far ^ k], to, sems.at[i, k, j])
+                copies[k, j, i].start()
     places = {1: ((a_send, 0), (b_keep, 1)), 2: ((a_send, 1), (b_send, 1)),
               3: ((a_keep, 1), (b_send, 0)), 0: ((a_keep, 0), (b_keep, 0))}
     for group in groups:
         for k in group:
             for j in range(near_n):
-                copies[k, j].wait()
-        out = long_dot(jnp.concatenate([held[k] for k in group], 0), hi_ref[...], lo_ref[...])
+                for i in range(2):
+                    copies[k, j, i].wait()
+        left = [jnp.concatenate([held[k] for k in group], 0) for held in (held_hi, held_lo)]
+        out = long_dot(*left, hi_ref[...], lo_ref[...])
         size = out.shape[0] // 2
         for i, k in enumerate(group):
             (a, at_a), (b, at_b) = places[k]
@@ -111,15 +138,15 @@
 
 
 def products(at, below, hi, lo):
-    near_n, far_n, share, depth = below.shape
+    near_n, far_n, share, depth = below[0].shape
     panel = hi.shape[0]
     rows = near_n * share
     return call(
         product_kernel,
         (jax.ShapeDtypeStruct((2, rows, panel // 2), F32),) * 4,
-        [SMEM, pl.BlockSpec(memory_space=pl.ANY), VMEM, VMEM],
-        [at, below, hi, lo],
-        scratch=[pltpu.VMEM((far_n, rows, depth), F32), pltpu.SemaphoreType.DMA((far_n, near_n))],
+        [SMEM] + [pl.BlockSpec(memory_space=pl.ANY)] * 2 + [VMEM] * 2,
+        [at, *below, hi, lo],
+        scratch=[pltpu.VMEM((far_n, rows, depth), BF16)] * 2 + [pltpu.SemaphoreType.DMA((2, far_n, near_n))],
         flops=9 * far_n * rows * depth * panel,
         moved=6 * 2**20,
         vmem=PRODUCT_VMEM,
@@ -299,8 +326,16 @@
     core = lambda x: swap(x, "rows", rows_n, 1)
     along_y = lambda x, k: swap(x, "rows", rows_n, 2 * k)
     other_z = swap(history_rows, "rows", rows_n, 8)
-    low = place < rows_n // 2
-    pair = jnp.concatenate([jnp.where(low, history_rows, other_z), jnp.where(low, other_z, history_rows)], 0)
+    below_parts = split_rows(history_below, 2 * share)
+    other_z, *below_parts = lax.optimization_barrier((other_z, *below_parts))
+    pair = call(
+        join_kernel,
+        jax.ShapeDtypeStruct((2 * mine, depth), F32),
+        [SMEM] + [VMEM] * 2,
+        [me, history_rows, other_z],
+        moved=16 * mine * depth,
+        vmem=4,
+    )
     y1, y3 = along_y(pair, 1), along_y(pair, 3)
     close = [pair, y1, y3]
     close_other = [core(x) for x in close]
@@ -324,7 +359,7 @@
         moved=2 * panel * depth,
         aliases=((5, 0), (6, 1)),
     )
-    below = history_below.reshape(near_n, far_n, share, depth)
+    below = [x.reshape(near_n, far_n, share, depth) for x in below_parts]
     a_send, b_send, a_keep, b_keep = products(at, below, hi, lo)
     *by_far, a_send, b_send = lax.optimization_barrier((*by_far, a_send, b_send))
     schur_part = tree(schur_part, *by_far)

time: 99.2 us -> 103 us (1.038)
  Pallas kernels: 27.1 us -> 37.7 us
  waiting for transfers between devices: 18.9 us -> 13.3 us
    pallas_call x0 -> x1, Pallas kernels: none -> 7.88 us  [split_rows(): pl.pallas_call(split_kernel, out_shape=(jax.ShapeDtypeStruct(x.shape, BF1...]
    ppermute x3, waiting for transfers between devices: 4.33 us -> 1.03 us  [move(): return lax.ppermute(x, ('rows', 'near'), pairs)]
    pallas_call x7 -> x8, Pallas kernels: 27.1 us -> 29.8 us  [call(): pl.pallas_call(kernel, out_shape=out_shape, in_specs=in_specs, out_specs=...]
    ppermute x27, waiting for transfers between devices: 14.6 us -> 12.3 us  [swap(): return lax.ppermute(x, axis, [(i, i ^ step) for i in range(size)])]
    ppermute x27, starting transfers between devices: 43.8 us -> 42.8 us  [swap(): return lax.ppermute(x, axis, [(i, i ^ step) for i in range(size)])]
  transfers between devices with their start and end apart: 30 -> 30, of which waited for: 10 -> 8; matrix products, arithmetic and copies ran while one was open for 0% -> 0% of each run, Pallas kernels for 26% -> 35%
where the time goes in v3:
time: 103 us
  starting transfers between devices  49.7 us (48%)
  Pallas kernels  37.7 us (37%)
  waiting for transfers between devices  13.3 us (13%)
  local copies, waits for them, and re-layouts  1.48 us (1%)
    ppermute x27, starting transfers between devices, swap(): return lax.ppermute(x, axis, [(i, i ^ step) for i in range(size)])  42.8 us
    pallas_call x8, Pallas kernels, call(): pl.pallas_call(kernel, out_shape=out_shape, in_specs=in_specs, out_specs=...  29.8 us
    ppermute x27, waiting for transfers between devices, swap(): return lax.ppermute(x, axis, [(i, i ^ step) for i in range(size)])  12.3 us
    pallas_call x1, Pallas kernels, split_rows(): pl.pallas_call(split_kernel, out_shape=(jax.ShapeDtypeStruct(x.shape, BF1...  7.88 us
    ppermute x3, starting transfers between devices, move(): return lax.ppermute(x, ('rows', 'near'), pairs)  6.92 us
  transfers between devices with their start and end apart: 30, of which 8 were waited for; matrix products, arithmetic and copies ran while one was open for 0% of the time, Pallas kernels for 35%

profile of v3, /device:TPU:1, one launch (start us, length us, event | category | flops | bytes accessed | tf_op | source)
XLA Modules:
  0.0 103.1 jit_solution(14991831613547995140)
XLA Ops:
  0.6 2.6 %collective-permute-start = (f32[32,1536]{1,0:T(8,128)}, f32[32,1536]{1,0:T(8,128)S(1)}, u32[]{:S(2)}, u32[]{:S(2)}) collective-permute-start(f32[32,1536]{1,0:T(8,128)} %mine_ref.1), channel_id=1, source_target_pairs={{0,128},{16,144},{32,160},{48,176},{64,192},{80,208},{96,224},{112... | collective-permute-start | bytes 589832 | tf_op jit(solution)/shard_map/ppermute | solution.py:293
  3.2 7.9 %shard_map.59 = (bf16[1024,1536]{1,0:T(8,128)(2,1)}, bf16[1024,1536]{1,0:T(8,128)(2,1)}) custom-call(f32[1024,1536]{1,0:T(8,128)} %x_ref.1), custom_call_target="tpu_custom_call" | custom-call | flops 3145728 | bytes 12582912 | tf_op jit(solution)/shard_map/pallas_call | solution.py:95
  11.1 0.0 collective-permute-done.other_ref
  11.1 1.4 %collective-permute-start.3 = (f32[64,1536]{1,0:T(8,128)S(1)}, f32[64,1536]{1,0:T(8,128)S(1)}, u32[]{:S(2)}, u32[]{:S(2)}) collective-permute-start(f32[64,1536]{1,0:T(8,128)S(1)} %shard_map.60.refs_0_), channel_id=1, source_target_pairs={{0,32},{16,48},{32,0},{48,16},{64,96},{80,112},{96,64},{112,80},{1... | collective-permute-start | bytes 1179656 | tf_op jit(solution)/shard_map/ppermute | solution.py:293
  12.5 1.9 %collective-permute-start.1 = (f32[64,1536]{1,0:T(8,128)S(1)}, f32[64,1536]{1,0:T(8,128)S(1)}, u32[]{:S(2)}, u32[]{:S(2)}) collective-permute-start(f32[64,1536]{1,0:T(8,128)S(1)} %shard_map.60.refs_0_), channel_id=1, source_target_pairs={{0,96},{16,112},{32,64},{48,80},{64,32},{80,48},{96,0},{112,16},{1... | collective-permute-start | bytes 1179656 | tf_op jit(solution)/shard_map/ppermute | solution.py:293
  14.4 1.5 %collective-permute-start.5 = (f32[64,1536]{1,0:T(8,128)S(1)}, f32[64,1536]{1,0:T(8,128)S(1)}, u32[]{:S(2)}, u32[]{:S(2)}) collective-permute-start(f32[64,1536]{1,0:T(8,128)S(1)} %shard_map.60.refs_0_), channel_id=1, source_target_pairs={{0,16},{16,0},{32,48},{48,32},{64,80},{80,64},{96,112},{112,96},{1... | collective-permute-start | bytes 1179656 | tf_op jit(solution)/shard_map/ppermute | solution.py:293
  15.9 5.0 %collective-permute-done.3.refs_1_ = f32[64,1536]{1,0:T(8,128)S(1)} collective-permute-done((f32[64,1536]{1,0:T(8,128)S(1)}, f32[64,1536]{1,0:T(8,128)S(1)}, u32[]{:S(2)}, u32[]{:S(2)}) %collective-permute-start.3) | collective-permute-done | bytes 393248 | tf_op jit(solution)/shard_map/ppermute | solution.py:293
  20.9 1.9 %collective-permute-start.6 = (f32[64,1536]{1,0:T(8,128)S(1)}, f32[64,1536]{1,0:T(8,128)S(1)}, u32[]{:S(2)}, u32[]{:S(2)}) collective-permute-start(f32[64,1536]{1,0:T(8,128)S(1)} %collective-permute-done.3.refs_1_), channel_id=1, source_target_pairs={{0,16},{16,0},{32,48},{48,32},{64,80},{80,64},{96,112},{112,96},{1... | collective-permute-start | bytes 1179656 | tf_op jit(solution)/shard_map/ppermute | solution.py:293
  22.7 0.3 collective-permute-done.1.refs_2_
  23.1 2.2 %collective-permute-start.7 = (f32[64,1536]{1,0:T(8,128)S(1)}, f32[64,1536]{1,0:T(8,128)S(1)}, u32[]{:S(2)}, u32[]{:S(2)}) collective-permute-start(f32[64,1536]{1,0:T(8,128)S(1)} %collective-permute-done.1.refs_2_), channel_id=1, source_target_pairs={{0,16},{16,0},{32,48},{48,32},{64,80},{80,64},{96,112},{112,96},{1... | collective-permute-start | bytes 1179656 | tf_op jit(solution)/shard_map/ppermute | solution.py:293
  25.3 0.1 collective-permute-start.2
  25.4 2.0 %collective-permute-start.4 = (f32[32,1536]{1,0:T(8,128)S(1)}, f32[32,1536]{1,0:T(8,128)S(1)}, u32[]{:S(2)}, u32[]{:S(2)}) collective-permute-start(f32[32,1536]{1,0:T(8,128)S(1)} %slice.9), channel_id=1, source_target_pairs={{0,96},{16,112},{32,64},{48,80},{64,32},{80,48},{96,0},{112,16},{1... | collective-permute-start | bytes 589832 | tf_op jit(solution)/shard_map/ppermute | solution.py:293
  27.4 0.0 collective-permute-done.5.refs_3_
  27.4 0.0 collective-permute-done.6.refs_4_
  27.4 0.0 collective-permute-done.7.refs_5_
  27.4 2.1 %shard_map.61 = (f32[64,512]{1,0:T(8,128)S(1)}, bf16[512,1536]{1,0:T(8,128)(2,1)S(1)}, bf16[512,1536]{1,0:T(8,128)(2,1)S(1)}) custom-call(s32[1]{0:T(128)} %bitcast.4.me_ref, f32[64,1536]{1,0:T(8,128)S(1)} %shard_map.60.refs_0_, f32[64,1536]{1,0:T(8,128)S(1)} %collective-permute-done.3.refs_1_, f32[64,1536]{1,0:T(8,128)S(1)} %collective-permute-done.1.refs_2_, ...), custom_call_target="tpu_custom_call" | custom-call | flops 603979776 | bytes 6291456 | tf_op jit(solution)/shard_map/pallas_call | solution.py:30
  29.5 0.0 copy-start.2
  29.5 0.6 copy-done.2
  30.2 1.7 %collective-permute-done.2.refs_0_ = f32[32,1536]{1,0:T(8,128)S(1)} collective-permute-done((f32[32,1536]{1,0:T(8,128)S(1)}, f32[32,1536]{1,0:T(8,128)S(1)}, u32[]{:S(2)}, u32[]{:S(2)}) %collective-permute-start.2) | collective-permute-done | bytes 196640 | tf_op jit(solution)/shard_map/ppermute | solution.py:293
  31.9 1.3 %collective-permute-done.4.refs_1_ = f32[32,1536]{1,0:T(8,128)S(1)} collective-permute-done((f32[32,1536]{1,0:T(8,128)S(1)}, f32[32,1536]{1,0:T(8,128)S(1)}, u32[]{:S(2)}, u32[]{:S(2)}) %collective-permute-start.4) | collective-permute-done | bytes 196640 | tf_op jit(solution)/shard_map/ppermute | solution.py:293
  33.2 0.8 collective-permute-start.8
  34.0 0.0 collective-permute-start.9
  34.0 0.1 pad_add_fusion.at_ref
  34.1 1.2 %collective-permute-start.10 = (f32[64,512]{1,0:T(8,128)}, f32[64,512]{1,0:T(8,128)S(1)}, u32[]{:S(2)}, u32[]{:S(2)}) collective-permute-start(f32[64,512]{1,0:T(8,128)} %copy-done.2), channel_id=1, source_target_pairs={{0,1},{1,0},{2,3},{3,2},{4,5},{5,4},{6,7},{7,6},{8,9},{9,8},{10,11... | collective-permute-start | bytes 393224 | tf_op jit(solution)/shard_map/ppermute | solution.py:293
  35.3 2.5 %collective-permute-start.11 = (f32[64,512]{1,0:T(8,128)}, f32[64,512]{1,0:T(8,128)S(1)}, u32[]{:S(2)}, u32[]{:S(2)}) collective-permute-start(f32[64,512]{1,0:T(8,128)} %copy-done.2), channel_id=1, source_target_pairs={{0,2},{1,3},{2,0},{3,1},{4,6},{5,7},{6,4},{7,5},{8,10},{9,11},{10,... | collective-permute-start | bytes 393224 | tf_op jit(solution)/shard_map/ppermute | solution.py:293
  37.8 0.2 collective-permute-start.12
  38.0 0.0 collective-permute-done.8.refs_2_
  38.0 1.3 %shard_map.62 = (bf16[512,1536]{1,0:T(8,128)(2,1)S(1)}, bf16[512,1536]{1,0:T(8,128)(2,1)S(1)}) custom-call(s32[1]{0:T(128)} %bitcast.4.me_ref, f32[32,1536]{1,0:T(8,128)S(1)} %collective-permute-done.2.refs_0_, f32[32,1536]{1,0:T(8,128)S(1)} %collective-permute-done.4.refs_1_, ...), custom_call_target="tpu_custom_call", output_to_operand_aliasing={{0}: (5, {}), {1}: (6, {})} | custom-call | bytes 1572864 | tf_op jit(solution)/shard_map/pallas_call | solution.py:30
  39.3 0.8 copy-done.4
  40.1 10.2 %shard_map.63 = (f32[2,256,256]{2,1,0:T(8,128)S(1)}, f32[2,256,256]{2,1,0:T(8,128)S(1)}, f32[2,256,256]{2,1,0:T(8,128)S(1)}, f32[2,256,256]{2,1,0:T(8,128)S(1)}) custom-call(s32[2]{0:T(128)S(1)} %pad_add_fusion.at_ref, bf16[4,4,64,1536]{3,2,1,0:T(8,128)(2,1)S(1)} %bitcast.5, bf16[4,4,64,1536]{3,2,1,0:T(8,128)(2,1)} %bitcast.6, ...), custom_call_target="tpu_custom_call" | custom-call | flops 7247757312 | bytes 6291456 | tf_op jit(solution)/shard_map/pallas_call | solution.py:30
  50.3 0.0 collective-permute-done.11
  50.3 0.0 collective-permute-done.12
  50.3 0.3 collective-permute-start.13
  50.6 2.6 %collective-permute-start.14 = (f32[2,256,256]{2,1,0:T(8,128)S(1)}, f32[2,256,256]{2,1,0:T(8,128)S(1)}, u32[]{:S(2)}, u32[]{:S(2)}) collective-permute-start(f32[2,256,256]{2,1,0:T(8,128)S(1)} %get-tuple-element.48), channel_id=1, source_target_pairs={{0,3},{1,2},{2,1},{3,0},{4,7},{5,6},{6,5},{7,4},{8,11},{9,10},{10,... | collective-permute-start | bytes 1572872 | tf_op jit(solution)/shard_map/ppermute | solution.py:293
  53.2 4.8 %collective-permute-start.21 = (f32[64,512]{1,0:T(8,128)S(1)}, f32[64,512]{1,0:T(8,128)S(1)}, u32[]{:S(2)}, u32[]{:S(2)}) collective-permute-start(f32[64,512]{1,0:T(8,128)S(1)} %add_add_fusion.1), channel_id=1, source_target_pairs={{140,0},{128,4},{132,8},{136,12},{156,16},{144,20},{148,24},{152,2... | collective-permute-start | bytes 393224 | tf_op jit(solution)/shard_map/ppermute | solution.py:310
  57.9 1.2 %collective-permute-start.22 = (f32[64,512]{1,0:T(8,128)S(1)}, f32[64,512]{1,0:T(8,128)S(1)}, u32[]{:S(2)}, u32[]{:S(2)}) collective-permute-start(f32[64,512]{1,0:T(8,128)S(1)} %add_add_fusion.1), channel_id=1, source_target_pairs={{4,0},{8,4},{12,8},{0,12},{20,16},{24,20},{28,24},{16,28},{36,32},... | collective-permute-start | bytes 393224 | tf_op jit(solution)/shard_map/ppermute | solution.py:310
  59.1 1.0 collective-permute-start.20
  60.1 2.5 %collective-permute-done.13.a_got = f32[2,256,256]{2,1,0:T(8,128)S(1)} collective-permute-done((f32[2,256,256]{2,1,0:T(8,128)S(1)}, f32[2,256,256]{2,1,0:T(8,128)S(1)}, u32[]{:S(2)}, u32[]{:S(2)}) %collective-permute-start.13) | collective-permute-done | bytes 524320 | tf_op jit(solution)/shard_map/ppermute | solution.py:293
  62.6 1.1 %collective-permute-done.14.b_got = f32[2,256,256]{2,1,0:T(8,128)S(1)} collective-permute-done((f32[2,256,256]{2,1,0:T(8,128)S(1)}, f32[2,256,256]{2,1,0:T(8,128)S(1)}, u32[]{:S(2)}, u32[]{:S(2)}) %collective-permute-start.14) | collective-permute-done | bytes 524320 | tf_op jit(solution)/shard_map/ppermute | solution.py:293
  63.8 0.1 shard_map.64
  63.8 2.7 %collective-permute-start.15 = (f32[256,256]{1,0:T(8,128)S(1)}, f32[256,256]{1,0:T(8,128)S(1)}, u32[]{:S(2)}, u32[]{:S(2)}) collective-permute-start(f32[256,256]{1,0:T(8,128)S(1)} %get-tuple-element.49), channel_id=1, source_target_pairs={{0,3},{1,2},{2,1},{3,0},{4,7},{5,6},{6,5},{7,4},{8,11},{9,10},{10,... | collective-permute-start | bytes 786440 | tf_op jit(solution)/shard_map/ppermute | solution.py:293
  66.6 0.0 collective-permute-start.16
  66.6 0.0 collective-permute-done.21
  66.6 1.0 collective-permute-done.20
  67.7 0.3 collective-permute-start.23
  68.0 2.9 %collective-permute-start.24 = (f32[64,512]{1,0:T(8,128)S(1)}, f32[64,512]{1,0:T(8,128)S(1)}, u32[]{:S(2)}, u32[]{:S(2)}) collective-permute-start(f32[64,512]{1,0:T(8,128)S(1)} %add_add_fusion.refs_0_), channel_id=1, source_target_pairs={{0,64},{16,80},{32,96},{48,112},{64,0},{80,16},{96,32},{112,48},{1... | collective-permute-start | bytes 393224 | tf_op jit(solution)/shard_map/ppermute | solution.py:293
  70.9 0.8 collective-permute-start.25
  71.6 0.3 collective-permute-done.23.refs_1_
  71.9 4.0 %collective-permute-start.26 = (f32[64,512]{1,0:T(8,128)S(1)}, f32[64,512]{1,0:T(8,128)S(1)}, u32[]{:S(2)}, u32[]{:S(2)}) collective-permute-start(f32[64,512]{1,0:T(8,128)S(1)} %add_add_fusion.refs_0_), channel_id=1, source_target_pairs={{0,16},{16,0},{32,48},{48,32},{64,80},{80,64},{96,112},{112,96},{1... | collective-permute-start | bytes 393224 | tf_op jit(solution)/shard_map/ppermute | solution.py:293
  75.8 0.0 collective-permute-done.24.refs_2_
  75.9 3.0 %collective-permute-start.27 = (f32[64,512]{1,0:T(8,128)S(1)}, f32[64,512]{1,0:T(8,128)S(1)}, u32[]{:S(2)}, u32[]{:S(2)}) collective-permute-start(f32[64,512]{1,0:T(8,128)S(1)} %collective-permute-done.23.refs_1_), channel_id=1, source_target_pairs={{0,16},{16,0},{32,48},{48,32},{64,80},{80,64},{96,112},{112,96},{1... | collective-permute-start | bytes 393224 | tf_op jit(solution)/shard_map/ppermute | solution.py:293
  78.9 1.8 %collective-permute-start.28 = (f32[64,512]{1,0:T(8,128)S(1)}, f32[64,512]{1,0:T(8,128)S(1)}, u32[]{:S(2)}, u32[]{:S(2)}) collective-permute-start(f32[64,512]{1,0:T(8,128)S(1)} %collective-permute-done.24.refs_2_), channel_id=1, source_target_pairs={{0,16},{16,0},{32,48},{48,32},{64,80},{80,64},{96,112},{112,96},{1... | collective-permute-start | bytes 393224 | tf_op jit(solution)/shard_map/ppermute | solution.py:293
  80.7 0.0 collective-permute-start.29
  80.7 0.0 collective-permute-done.16.b_last
  80.7 0.1 shard_map.65
  80.8 2.2 %collective-permute-start.17 = (f32[64,512]{1,0:T(8,128)S(1)}, f32[64,512]{1,0:T(8,128)S(1)}, u32[]{:S(2)}, u32[]{:S(2)}) collective-permute-start(f32[64,512]{1,0:T(8,128)S(1)} %get-tuple-element.52), channel_id=1, source_target_pairs={{0,4},{4,0},{8,12},{12,8},{1,5},{5,1},{9,13},{13,9},{2,6},{6,2},{1... | collective-permute-start | bytes 393224 | tf_op jit(solution)/shard_map/ppermute | solution.py:293
  83.1 4.0 %collective-permute-start.18 = (f32[64,512]{1,0:T(8,128)S(1)}, f32[64,512]{1,0:T(8,128)S(1)}, u32[]{:S(2)}, u32[]{:S(2)}) collective-permute-start(f32[64,512]{1,0:T(8,128)S(1)} %get-tuple-element.53), channel_id=1, source_target_pairs={{0,8},{4,12},{8,0},{12,4},{1,9},{5,13},{9,1},{13,5},{2,10},{6,14},... | collective-permute-start | bytes 393224 | tf_op jit(solution)/shard_map/ppermute | solution.py:293
  87.1 0.0 collective-permute-start.19
  87.1 0.0 collective-permute-done.29.refs_7_
  87.1 14.7 %shard_map.66 = (f32[512,512]{1,0:T(8,128)}, f32[512,512]{1,0:T(8,128)S(1)}) custom-call(s32[1]{0:T(128)} %bitcast.4.me_ref, f32[512,512]{1,0:T(8,128)S(1)} %copy-done.5, f32[64,512]{1,0:T(8,128)S(1)} %add_add_fusion.refs_0_, f32[64,512]{1,0:T(8,128)S(1)} %collective-permute-done.23.refs_1_, f32[64,512]{1,0:T(8,128)S(1)} %collective-permute-done.24.refs_2_, ...), custom_call_target="tpu_custom_call" | custom-call | flops 16106127360 | bytes 4194304 | tf_op jit(solution)/shard_map/pallas_call | solution.py:30
  101.8 0.0 collective-permute-done.17.p1
  101.8 0.0 collective-permute-done.18.p2
  101.8 0.0 collective-permute-done.19.p3
  101.8 1.3 %shard_map.67 = f32[64,512]{1,0:T(8,128)} custom-call(f32[64,512]{1,0:T(8,128)S(1)} %copy-done.1, f32[64,512]{1,0:T(8,128)S(1)} %get-tuple-element.51.p0, f32[64,512]{1,0:T(8,128)S(1)} %collective-permute-done.17.p1, f32[64,512]{1,0:T(8,128)S(1)} %collective-permute-done.18.p2, f32[64,512]{1,0:T(8,128)S(1)} %collective-permute-done.19.p3, ...), custom_call_target="tpu_custom_call" | custom-call | flops 100663296 | bytes 2097152 | tf_op jit(solution)/shard_map/pallas_call | solution.py:30
  (22 shorter events, 0.2 us)
Async XLA Ops:
  0.6 10.4 %collective-permute-start = (f32[32,1536]{1,0:T(8,128)}, f32[32,1536]{1,0:T(8,128)S(1)}, u32[]{:S(2)}, u32[]{:S(2)}) collective-permute-start(f32[32,1536]{1,0:T(8,128)} %mine_ref.1), channel_id=1, source_target_pairs={{0,128},{16,144},{32,160},{48,176},{64,192},{80,208},{96,224},{112... | collective-permute-start | bytes 589832 | tf_op jit(solution)/shard_map/ppermute | solution.py:293
  3.2 7.9 %copy-start = (f32[32,1536]{1,0:T(8,128)S(1)}, f32[32,1536]{1,0:T(8,128)}, u32[]{:S(2)}) copy-start(f32[32,1536]{1,0:T(8,128)} %mine_ref.1) | copy-start | bytes 589828
  11.1 9.8 %collective-permute-start.3 = (f32[64,1536]{1,0:T(8,128)S(1)}, f32[64,1536]{1,0:T(8,128)S(1)}, u32[]{:S(2)}, u32[]{:S(2)}) collective-permute-start(f32[64,1536]{1,0:T(8,128)S(1)} %shard_map.60.refs_0_), channel_id=1, source_target_pairs={{0,32},{16,48},{32,0},{48,16},{64,96},{80,112},{96,64},{112,80},{1... | collective-permute-start | bytes 1179656 | tf_op jit(solution)/shard_map/ppermute | solution.py:293
  12.5 10.6 %collective-permute-start.1 = (f32[64,1536]{1,0:T(8,128)S(1)}, f32[64,1536]{1,0:T(8,128)S(1)}, u32[]{:S(2)}, u32[]{:S(2)}) collective-permute-start(f32[64,1536]{1,0:T(8,128)S(1)} %shard_map.60.refs_0_), channel_id=1, source_target_pairs={{0,96},{16,112},{32,64},{48,80},{64,32},{80,48},{96,0},{112,16},{1... | collective-permute-start | bytes 1179656 | tf_op jit(solution)/shard_map/ppermute | solution.py:293
  14.4 13.0 %collective-permute-start.5 = (f32[64,1536]{1,0:T(8,128)S(1)}, f32[64,1536]{1,0:T(8,128)S(1)}, u32[]{:S(2)}, u32[]{:S(2)}) collective-permute-start(f32[64,1536]{1,0:T(8,128)S(1)} %shard_map.60.refs_0_), channel_id=1, source_target_pairs={{0,16},{16,0},{32,48},{48,32},{64,80},{80,64},{96,112},{112,96},{1... | collective-permute-start | bytes 1179656 | tf_op jit(solution)/shard_map/ppermute | solution.py:293
  20.9 6.5 %collective-permute-start.6 = (f32[64,1536]{1,0:T(8,128)S(1)}, f32[64,1536]{1,0:T(8,128)S(1)}, u32[]{:S(2)}, u32[]{:S(2)}) collective-permute-start(f32[64,1536]{1,0:T(8,128)S(1)} %collective-permute-done.3.refs_1_), channel_id=1, source_target_pairs={{0,16},{16,0},{32,48},{48,32},{64,80},{80,64},{96,112},{112,96},{1... | collective-permute-start | bytes 1179656 | tf_op jit(solution)/shard_map/ppermute | solution.py:293
  23.1 4.3 %collective-permute-start.7 = (f32[64,1536]{1,0:T(8,128)S(1)}, f32[64,1536]{1,0:T(8,128)S(1)}, u32[]{:S(2)}, u32[]{:S(2)}) collective-permute-start(f32[64,1536]{1,0:T(8,128)S(1)} %collective-permute-done.1.refs_2_), channel_id=1, source_target_pairs={{0,16},{16,0},{32,48},{48,32},{64,80},{80,64},{96,112},{112,96},{1... | collective-permute-start | bytes 1179656 | tf_op jit(solution)/shard_map/ppermute | solution.py:293
  25.3 6.6 %collective-permute-start.2 = (f32[32,1536]{1,0:T(8,128)S(1)}, f32[32,1536]{1,0:T(8,128)S(1)}, u32[]{:S(2)}, u32[]{:S(2)}) collective-permute-start(f32[32,1536]{1,0:T(8,128)S(1)} %slice.8), channel_id=1, source_target_pairs={{0,32},{16,48},{32,0},{48,16},{64,96},{80,112},{96,64},{112,80},{1... | collective-permute-start | bytes 589832 | tf_op jit(solution)/shard_map/ppermute | solution.py:293
  25.4 7.8 %collective-permute-start.4 = (f32[32,1536]{1,0:T(8,128)S(1)}, f32[32,1536]{1,0:T(8,128)S(1)}, u32[]{:S(2)}, u32[]{:S(2)}) collective-permute-start(f32[32,1536]{1,0:T(8,128)S(1)} %slice.9), channel_id=1, source_target_pairs={{0,96},{16,112},{32,64},{48,80},{64,32},{80,48},{96,0},{112,16},{1... | collective-permute-start | bytes 589832 | tf_op jit(solution)/shard_map/ppermute | solution.py:293
  29.5 0.7 copy-start.2
  33.2 4.7 %collective-permute-start.8 = (f32[32,1536]{1,0:T(8,128)S(1)}, f32[32,1536]{1,0:T(8,128)}, u32[]{:S(2)}, u32[]{:S(2)}) collective-permute-start(f32[32,1536]{1,0:T(8,128)S(1)} %collective-permute-done.2.refs_0_), channel_id=1, source_target_pairs={{0,16},{16,0},{32,48},{48,32},{64,80},{80,64},{96,112},{112,96},{1... | collective-permute-start | bytes 589832 | tf_op jit(solution)/shard_map/ppermute | solution.py:293
  34.0 4.0 %collective-permute-start.9 = (f32[32,1536]{1,0:T(8,128)S(1)}, f32[32,1536]{1,0:T(8,128)}, u32[]{:S(2)}, u32[]{:S(2)}) collective-permute-start(f32[32,1536]{1,0:T(8,128)S(1)} %collective-permute-done.4.refs_1_), channel_id=1, source_target_pairs={{0,16},{16,0},{32,48},{48,32},{64,80},{80,64},{96,112},{112,96},{1... | collective-permute-start | bytes 589832 | tf_op jit(solution)/shard_map/ppermute | solution.py:293
  34.1 16.2 %collective-permute-start.10 = (f32[64,512]{1,0:T(8,128)}, f32[64,512]{1,0:T(8,128)S(1)}, u32[]{:S(2)}, u32[]{:S(2)}) collective-permute-start(f32[64,512]{1,0:T(8,128)} %copy-done.2), channel_id=1, source_target_pairs={{0,1},{1,0},{2,3},{3,2},{4,5},{5,4},{6,7},{7,6},{8,9},{9,8},{10,11... | collective-permute-start | bytes 393224 | tf_op jit(solution)/shard_map/ppermute | solution.py:293
  35.3 15.0 %collective-permute-start.11 = (f32[64,512]{1,0:T(8,128)}, f32[64,512]{1,0:T(8,128)S(1)}, u32[]{:S(2)}, u32[]{:S(2)}) collective-permute-start(f32[64,512]{1,0:T(8,128)} %copy-done.2), channel_id=1, source_target_pairs={{0,2},{1,3},{2,0},{3,1},{4,6},{5,7},{6,4},{7,5},{8,10},{9,11},{10,... | collective-permute-start | bytes 393224 | tf_op jit(solution)/shard_map/ppermute | solution.py:293
  37.8 12.5 %collective-permute-start.12 = (f32[64,512]{1,0:T(8,128)}, f32[64,512]{1,0:T(8,128)S(1)}, u32[]{:S(2)}, u32[]{:S(2)}) collective-permute-start(f32[64,512]{1,0:T(8,128)} %copy-done.2), channel_id=1, source_target_pairs={{0,3},{1,2},{2,1},{3,0},{4,7},{5,6},{6,5},{7,4},{8,11},{9,10},{10,... | collective-permute-start | bytes 393224 | tf_op jit(solution)/shard_map/ppermute | solution.py:293
  38.0 2.1 %copy-start.4 = (bf16[1024,1536]{1,0:T(8,128)(2,1)S(1)}, bf16[1024,1536]{1,0:T(8,128)(2,1)}, u32[]{:S(2)}) copy-start(bf16[1024,1536]{1,0:T(8,128)(2,1)} %get-tuple-element.33) | copy-start | bytes 9437188
  40.0 13.1 %copy-start.3 = (f32[64,512]{1,0:T(8,128)S(1)}, f32[64,512]{1,0:T(8,128)}, u32[]{:S(2)}) copy-start(f32[64,512]{1,0:T(8,128)} %copy-done.2) | copy-start | bytes 393220
  50.3 12.3 %collective-permute-start.13 = (f32[2,256,256]{2,1,0:T(8,128)S(1)}, f32[2,256,256]{2,1,0:T(8,128)S(1)}, u32[]{:S(2)}, u32[]{:S(2)}) collective-permute-start(f32[2,256,256]{2,1,0:T(8,128)S(1)} %get-tuple-element.46), channel_id=1, source_target_pairs={{0,1},{1,0},{2,3},{3,2},{4,5},{5,4},{6,7},{7,6},{8,9},{9,8},{10,11... | collective-permute-start | bytes 1572872 | tf_op jit(solution)/shard_map/ppermute | solution.py:293
  50.6 13.2 %collective-permute-start.14 = (f32[2,256,256]{2,1,0:T(8,128)S(1)}, f32[2,256,256]{2,1,0:T(8,128)S(1)}, u32[]{:S(2)}, u32[]{:S(2)}) collective-permute-start(f32[2,256,256]{2,1,0:T(8,128)S(1)} %get-tuple-element.48), channel_id=1, source_target_pairs={{0,3},{1,2},{2,1},{3,0},{4,7},{5,6},{6,5},{7,4},{8,11},{9,10},{10,... | collective-permute-start | bytes 1572872 | tf_op jit(solution)/shard_map/ppermute | solution.py:293
  53.2 13.4 %collective-permute-start.21 = (f32[64,512]{1,0:T(8,128)S(1)}, f32[64,512]{1,0:T(8,128)S(1)}, u32[]{:S(2)}, u32[]{:S(2)}) collective-permute-start(f32[64,512]{1,0:T(8,128)S(1)} %add_add_fusion.1), channel_id=1, source_target_pairs={{140,0},{128,4},{132,8},{136,12},{156,16},{144,20},{148,24},{152,2... | collective-permute-start | bytes 393224 | tf_op jit(solution)/shard_map/ppermute | solution.py:310
  57.9 8.7 %collective-permute-start.22 = (f32[64,512]{1,0:T(8,128)S(1)}, f32[64,512]{1,0:T(8,128)S(1)}, u32[]{:S(2)}, u32[]{:S(2)}) collective-permute-start(f32[64,512]{1,0:T(8,128)S(1)} %add_add_fusion.1), channel_id=1, source_target_pairs={{4,0},{8,4},{12,8},{0,12},{20,16},{24,20},{28,24},{16,28},{36,32},... | collective-permute-start | bytes 393224 | tf_op jit(solution)/shard_map/ppermute | solution.py:310
  59.1 8.5 %collective-permute-start.20 = (f32[64,512]{1,0:T(8,128)S(1)}, f32[64,512]{1,0:T(8,128)S(1)}, u32[]{:S(2)}, u32[]{:S(2)}) collective-permute-start(f32[64,512]{1,0:T(8,128)S(1)} %add_add_fusion.1), channel_id=1, source_target_pairs={{136,0},{140,4},{128,8},{132,12},{152,16},{156,20},{144,24},{148,2... | collective-permute-start | bytes 393224 | tf_op jit(solution)/shard_map/ppermute | solution.py:310
  63.8 16.9 %collective-permute-start.15 = (f32[256,256]{1,0:T(8,128)S(1)}, f32[256,256]{1,0:T(8,128)S(1)}, u32[]{:S(2)}, u32[]{:S(2)}) collective-permute-start(f32[256,256]{1,0:T(8,128)S(1)} %get-tuple-element.49), channel_id=1, source_target_pairs={{0,3},{1,2},{2,1},{3,0},{4,7},{5,6},{6,5},{7,4},{8,11},{9,10},{10,... | collective-permute-start | bytes 786440 | tf_op jit(solution)/shard_map/ppermute | solution.py:293
  66.6 20.5 %copy-start.5 = (f32[512,512]{1,0:T(8,128)S(1)}, f32[512,512]{1,0:T(8,128)}, u32[]{:S(2)}) copy-start(f32[512,512]{1,0:T(8,128)} %diag_ref.1) | copy-start | bytes 3145732
  66.6 14.1 %collective-permute-start.16 = (f32[256,256]{1,0:T(8,128)S(1)}, f32[256,256]{1,0:T(8,128)S(1)}, u32[]{:S(2)}, u32[]{:S(2)}) collective-permute-start(f32[256,256]{1,0:T(8,128)S(1)} %get-tuple-element.50), channel_id=1, source_target_pairs={{0,1},{1,0},{2,3},{3,2},{4,5},{5,4},{6,7},{7,6},{8,9},{9,8},{10,11... | collective-permute-start | bytes 786440 | tf_op jit(solution)/shard_map/ppermute | solution.py:293
  67.7 4.2 %collective-permute-start.23 = (f32[64,512]{1,0:T(8,128)S(1)}, f32[64,512]{1,0:T(8,128)S(1)}, u32[]{:S(2)}, u32[]{:S(2)}) collective-permute-start(f32[64,512]{1,0:T(8,128)S(1)} %add_add_fusion.refs_0_), channel_id=1, source_target_pairs={{0,32},{16,48},{32,0},{48,16},{64,96},{80,112},{96,64},{112,80},{1... | collective-permute-start | bytes 393224 | tf_op jit(solution)/shard_map/ppermute | solution.py:293
  68.0 7.9 %collective-permute-start.24 = (f32[64,512]{1,0:T(8,128)S(1)}, f32[64,512]{1,0:T(8,128)S(1)}, u32[]{:S(2)}, u32[]{:S(2)}) collective-permute-start(f32[64,512]{1,0:T(8,128)S(1)} %add_add_fusion.refs_0_), channel_id=1, source_target_pairs={{0,64},{16,80},{32,96},{48,112},{64,0},{80,16},{96,32},{112,48},{1... | collective-permute-start | bytes 393224 | tf_op jit(solution)/shard_map/ppermute | solution.py:293
  70.9 8.0 %collective-permute-start.25 = (f32[64,512]{1,0:T(8,128)S(1)}, f32[64,512]{1,0:T(8,128)S(1)}, u32[]{:S(2)}, u32[]{:S(2)}) collective-permute-start(f32[64,512]{1,0:T(8,128)S(1)} %add_add_fusion.refs_0_), channel_id=1, source_target_pairs={{0,96},{16,112},{32,64},{48,80},{64,32},{80,48},{96,0},{112,16},{1... | collective-permute-start | bytes 393224 | tf_op jit(solution)/shard_map/ppermute | solution.py:293
  71.9 11.2 %collective-permute-start.26 = (f32[64,512]{1,0:T(8,128)S(1)}, f32[64,512]{1,0:T(8,128)S(1)}, u32[]{:S(2)}, u32[]{:S(2)}) collective-permute-start(f32[64,512]{1,0:T(8,128)S(1)} %add_add_fusion.refs_0_), channel_id=1, source_target_pairs={{0,16},{16,0},{32,48},{48,32},{64,80},{80,64},{96,112},{112,96},{1... | collective-permute-start | bytes 393224 | tf_op jit(solution)/shard_map/ppermute | solution.py:293
  75.9 11.2 %collective-permute-start.27 = (f32[64,512]{1,0:T(8,128)S(1)}, f32[64,512]{1,0:T(8,128)S(1)}, u32[]{:S(2)}, u32[]{:S(2)}) collective-permute-start(f32[64,512]{1,0:T(8,128)S(1)} %collective-permute-done.23.refs_1_), channel_id=1, source_target_pairs={{0,16},{16,0},{32,48},{48,32},{64,80},{80,64},{96,112},{112,96},{1... | collective-permute-start | bytes 393224 | tf_op jit(solution)/shard_map/ppermute | solution.py:293
  78.9 8.2 %collective-permute-start.28 = (f32[64,512]{1,0:T(8,128)S(1)}, f32[64,512]{1,0:T(8,128)S(1)}, u32[]{:S(2)}, u32[]{:S(2)}) collective-permute-start(f32[64,512]{1,0:T(8,128)S(1)} %collective-permute-done.24.refs_2_), channel_id=1, source_target_pairs={{0,16},{16,0},{32,48},{48,32},{64,80},{80,64},{96,112},{112,96},{1... | collective-permute-start | bytes 393224 | tf_op jit(solution)/shard_map/ppermute | solution.py:293
  80.7 6.4 %collective-permute-start.29 = (f32[64,512]{1,0:T(8,128)S(1)}, f32[64,512]{1,0:T(8,128)S(1)}, u32[]{:S(2)}, u32[]{:S(2)}) collective-permute-start(f32[64,512]{1,0:T(8,128)S(1)} %collective-permute-done.25.refs_3_), channel_id=1, source_target_pairs={{0,16},{16,0},{32,48},{48,32},{64,80},{80,64},{96,112},{112,96},{1... | collective-permute-start | bytes 393224 | tf_op jit(solution)/shard_map/ppermute | solution.py:293
  80.8 21.0 %collective-permute-start.17 = (f32[64,512]{1,0:T(8,128)S(1)}, f32[64,512]{1,0:T(8,128)S(1)}, u32[]{:S(2)}, u32[]{:S(2)}) collective-permute-start(f32[64,512]{1,0:T(8,128)S(1)} %get-tuple-element.52), channel_id=1, source_target_pairs={{0,4},{4,0},{8,12},{12,8},{1,5},{5,1},{9,13},{13,9},{2,6},{6,2},{1... | collective-permute-start | bytes 393224 | tf_op jit(solution)/shard_map/ppermute | solution.py:293
  83.1 18.8 %collective-permute-start.18 = (f32[64,512]{1,0:T(8,128)S(1)}, f32[64,512]{1,0:T(8,128)S(1)}, u32[]{:S(2)}, u32[]{:S(2)}) collective-permute-start(f32[64,512]{1,0:T(8,128)S(1)} %get-tuple-element.53), channel_id=1, source_target_pairs={{0,8},{4,12},{8,0},{12,4},{1,9},{5,13},{9,1},{13,5},{2,10},{6,14},... | collective-permute-start | bytes 393224 | tf_op jit(solution)/shard_map/ppermute | solution.py:293
  87.1 14.8 %copy-start.1 = (f32[64,512]{1,0:T(8,128)S(1)}, f32[64,512]{1,0:T(8,128)}, u32[]{:S(2)}) copy-start(f32[64,512]{1,0:T(8,128)} %below_ref.1) | copy-start | bytes 393220
  87.1 14.7 %collective-permute-start.19 = (f32[64,512]{1,0:T(8,128)S(1)}, f32[64,512]{1,0:T(8,128)S(1)}, u32[]{:S(2)}, u32[]{:S(2)}) collective-permute-start(f32[64,512]{1,0:T(8,128)S(1)} %get-tuple-element.54), channel_id=1, source_target_pairs={{0,12},{4,8},{8,4},{12,0},{1,13},{5,9},{9,5},{13,1},{2,14},{6,10},... | collective-permute-start | bytes 393224 | tf_op jit(solution)/shard_map/ppermute | solution.py:293

commit v4 on v2

--- a/solution.py
+++ b/solution.py
@@ -46,6 +46,13 @@
 
 def slot_of(shape, size):
     return lax.rem(lax.broadcasted_iota(jnp.int32, shape, 1) // (2 * size), 4)
+
+
+def join_kernel(me_ref, mine_ref, other_ref, out_ref):
+    size = mine_ref.shape[0]
+    z = me_ref[0] // 8
+    out_ref[pl.ds(pl.multiple_of(z * size, size), size), :] = mine_ref[...]
+    out_ref[pl.ds(pl.multiple_of((1 - z) * size, size), size), :] = other_ref[...]
 
 
 def schur_kernel(me_ref, *refs):
@@ -299,8 +306,14 @@
     core = lambda x: swap(x, "rows", rows_n, 1)
     along_y = lambda x, k: swap(x, "rows", rows_n, 2 * k)
     other_z = swap(history_rows, "rows", rows_n, 8)
-    low = place < rows_n // 2
-    pair = jnp.concatenate([jnp.where(low, history_rows, other_z), jnp.where(low, other_z, history_rows)], 0)
+    pair = call(
+        join_kernel,
+        jax.ShapeDtypeStruct((2 * mine, depth), F32),
+        [SMEM] + [VMEM] * 2,
+        [me, history_rows, other_z],
+        moved=16 * mine * depth,
+        vmem=4,
+    )
     y1, y3 = along_y(pair, 1), along_y(pair, 3)
     close = [pair, y1, y3]
     close_other = [core(x) for x in close]

time: 99.2 us -> 99.2 us (level)
    pallas_call x7 -> x8, Pallas kernels: 27.1 us -> 27.2 us  [call(): pl.pallas_call(kernel, out_shape=out_shape, in_specs=in_specs, out_specs=...]
where the time goes in v4:
time: 99.2 us; the launch traced here: 99 us
  starting transfers between devices  50.4 us (51%)
  Pallas kernels  27.2 us (27%)
  waiting for transfers between devices  18.9 us (19%)
  local copies, waits for them, and re-layouts  1.62 us (2%)
    ppermute x27, starting transfers between devices, swap(): return lax.ppermute(x, axis, [(i, i ^ step) for i in range(size)])  43.8 us
    pallas_call x8, Pallas kernels, call(): pl.pallas_call(kernel, out_shape=out_shape, in_specs=in_specs, out_specs=...  27.2 us
    ppermute x27, waiting for transfers between devices, swap(): return lax.ppermute(x, axis, [(i, i ^ step) for i in range(size)])  14.6 us
    ppermute x3, starting transfers between devices, move(): return lax.ppermute(x, ('rows', 'near'), pairs)  6.58 us
    ppermute x3, waiting for transfers between devices, move(): return lax.ppermute(x, ('rows', 'near'), pairs)  4.34 us
  transfers between devices with their start and end apart: 30, of which 10 were waited for; matrix products, arithmetic and copies ran while one was open for 0% of the time, Pallas kernels for 26%

profile of v4, /device:TPU:1, one launch (start us, length us, event | category | flops | bytes accessed | tf_op | source)
XLA Modules:
  0.0 99.0 jit_solution(7069931255000680296)
XLA Ops:
  0.6 2.6 %collective-permute-start = (f32[32,1536]{1,0:T(8,128)}, f32[32,1536]{1,0:T(8,128)S(1)}, u32[]{:S(2)}, u32[]{:S(2)}) collective-permute-start(f32[32,1536]{1,0:T(8,128)} %mine_ref.1), channel_id=1, source_target_pairs={{0,128},{16,144},{32,160},{48,176},{64,192},{80,208},{96,224},{112... | collective-permute-start | bytes 589832 | tf_op jit(solution)/shard_map/ppermute | solution.py:273
  3.2 3.9 %collective-permute-done.other_ref = f32[32,1536]{1,0:T(8,128)S(1)} collective-permute-done((f32[32,1536]{1,0:T(8,128)}, f32[32,1536]{1,0:T(8,128)S(1)}, u32[]{:S(2)}, u32[]{:S(2)}) %collective-permute-start) | collective-permute-done | bytes 196640 | tf_op jit(solution)/shard_map/ppermute | solution.py:273
  7.1 0.9 copy-done
  8.0 2.2 %collective-permute-start.3 = (f32[64,1536]{1,0:T(8,128)S(1)}, f32[64,1536]{1,0:T(8,128)S(1)}, u32[]{:S(2)}, u32[]{:S(2)}) collective-permute-start(f32[64,1536]{1,0:T(8,128)S(1)} %shard_map.59.refs_0_), channel_id=1, source_target_pairs={{0,32},{16,48},{32,0},{48,16},{64,96},{80,112},{96,64},{112,80},{1... | collective-permute-start | bytes 1179656 | tf_op jit(solution)/shard_map/ppermute | solution.py:273
  10.3 1.9 %collective-permute-start.1 = (f32[64,1536]{1,0:T(8,128)S(1)}, f32[64,1536]{1,0:T(8,128)S(1)}, u32[]{:S(2)}, u32[]{:S(2)}) collective-permute-start(f32[64,1536]{1,0:T(8,128)S(1)} %shard_map.59.refs_0_), channel_id=1, source_target_pairs={{0,96},{16,112},{32,64},{48,80},{64,32},{80,48},{96,0},{112,16},{1... | collective-permute-start | bytes 1179656 | tf_op jit(solution)/shard_map/ppermute | solution.py:273
  12.2 1.9 %collective-permute-start.5 = (f32[64,1536]{1,0:T(8,128)S(1)}, f32[64,1536]{1,0:T(8,128)S(1)}, u32[]{:S(2)}, u32[]{:S(2)}) collective-permute-start(f32[64,1536]{1,0:T(8,128)S(1)} %shard_map.59.refs_0_), channel_id=1, source_target_pairs={{0,16},{16,0},{32,48},{48,32},{64,80},{80,64},{96,112},{112,96},{1... | collective-permute-start | bytes 1179656 | tf_op jit(solution)/shard_map/ppermute | solution.py:273
  14.1 3.2 %collective-permute-done.3.refs_1_ = f32[64,1536]{1,0:T(8,128)S(1)} collective-permute-done((f32[64,1536]{1,0:T(8,128)S(1)}, f32[64,1536]{1,0:T(8,128)S(1)}, u32[]{:S(2)}, u32[]{:S(2)}) %collective-permute-start.3) | collective-permute-done | bytes 393248 | tf_op jit(solution)/shard_map/ppermute | solution.py:273
  17.3 3.0 %collective-permute-start.6 = (f32[64,1536]{1,0:T(8,128)S(1)}, f32[64,1536]{1,0:T(8,128)S(1)}, u32[]{:S(2)}, u32[]{:S(2)}) collective-permute-start(f32[64,1536]{1,0:T(8,128)S(1)} %collective-permute-done.3.refs_1_), channel_id=1, source_target_pairs={{0,16},{16,0},{32,48},{48,32},{64,80},{80,64},{96,112},{112,96},{1... | collective-permute-start | bytes 1179656 | tf_op jit(solution)/shard_map/ppermute | solution.py:273
  20.3 0.1 collective-permute-done.1.refs_2_
  20.4 2.6 %collective-permute-start.7 = (f32[64,1536]{1,0:T(8,128)S(1)}, f32[64,1536]{1,0:T(8,128)S(1)}, u32[]{:S(2)}, u32[]{:S(2)}) collective-permute-start(f32[64,1536]{1,0:T(8,128)S(1)} %collective-permute-done.1.refs_2_), channel_id=1, source_target_pairs={{0,16},{16,0},{32,48},{48,32},{64,80},{80,64},{96,112},{112,96},{1... | collective-permute-start | bytes 1179656 | tf_op jit(solution)/shard_map/ppermute | solution.py:273
  23.0 0.1 collective-permute-start.2
  23.1 2.0 %collective-permute-start.4 = (f32[32,1536]{1,0:T(8,128)S(1)}, f32[32,1536]{1,0:T(8,128)S(1)}, u32[]{:S(2)}, u32[]{:S(2)}) collective-permute-start(f32[32,1536]{1,0:T(8,128)S(1)} %slice.9), channel_id=1, source_target_pairs={{0,96},{16,112},{32,64},{48,80},{64,32},{80,48},{96,0},{112,16},{1... | collective-permute-start | bytes 589832 | tf_op jit(solution)/shard_map/ppermute | solution.py:273
  25.1 0.0 collective-permute-done.5.refs_3_
  25.1 0.0 collective-permute-done.6.refs_4_
  25.1 0.0 collective-permute-done.7.refs_5_
  25.1 2.1 %shard_map.60 = (f32[64,512]{1,0:T(8,128)S(1)}, bf16[512,1536]{1,0:T(8,128)(2,1)S(1)}, bf16[512,1536]{1,0:T(8,128)(2,1)S(1)}) custom-call(s32[1]{0:T(128)} %bitcast.3.me_ref, f32[64,1536]{1,0:T(8,128)S(1)} %shard_map.59.refs_0_, f32[64,1536]{1,0:T(8,128)S(1)} %collective-permute-done.3.refs_1_, f32[64,1536]{1,0:T(8,128)S(1)} %collective-permute-done.1.refs_2_, ...), custom_call_target="tpu_custom_call" | custom-call | flops 603979776 | bytes 6291456 | tf_op jit(solution)/shard_map/pallas_call | solution.py:30
  27.3 0.0 copy-start.2
  27.3 0.6 copy-done.2
  27.9 1.7 %collective-permute-done.2.refs_0_ = f32[32,1536]{1,0:T(8,128)S(1)} collective-permute-done((f32[32,1536]{1,0:T(8,128)S(1)}, f32[32,1536]{1,0:T(8,128)S(1)}, u32[]{:S(2)}, u32[]{:S(2)}) %collective-permute-start.2) | collective-permute-done | bytes 196640 | tf_op jit(solution)/shard_map/ppermute | solution.py:273
  29.6 1.3 %collective-permute-done.4.refs_1_ = f32[32,1536]{1,0:T(8,128)S(1)} collective-permute-done((f32[32,1536]{1,0:T(8,128)S(1)}, f32[32,1536]{1,0:T(8,128)S(1)}, u32[]{:S(2)}, u32[]{:S(2)}) %collective-permute-start.4) | collective-permute-done | bytes 196640 | tf_op jit(solution)/shard_map/ppermute | solution.py:273
  31.0 0.8 collective-permute-start.8
  31.7 0.0 collective-permute-start.9
  31.8 0.1 pad_add_fusion.at_ref
  31.8 1.2 %collective-permute-start.10 = (f32[64,512]{1,0:T(8,128)}, f32[64,512]{1,0:T(8,128)S(1)}, u32[]{:S(2)}, u32[]{:S(2)}) collective-permute-start(f32[64,512]{1,0:T(8,128)} %copy-done.2), channel_id=1, source_target_pairs={{0,1},{1,0},{2,3},{3,2},{4,5},{5,4},{6,7},{7,6},{8,9},{9,8},{10,11... | collective-permute-start | bytes 393224 | tf_op jit(solution)/shard_map/ppermute | solution.py:273
  33.1 2.5 %collective-permute-start.11 = (f32[64,512]{1,0:T(8,128)}, f32[64,512]{1,0:T(8,128)S(1)}, u32[]{:S(2)}, u32[]{:S(2)}) collective-permute-start(f32[64,512]{1,0:T(8,128)} %copy-done.2), channel_id=1, source_target_pairs={{0,2},{1,3},{2,0},{3,1},{4,6},{5,7},{6,4},{7,5},{8,10},{9,11},{10,... | collective-permute-start | bytes 393224 | tf_op jit(solution)/shard_map/ppermute | solution.py:273
  35.5 0.2 collective-permute-start.12
  35.7 0.0 collective-permute-done.8.refs_2_
  35.7 0.0 collective-permute-done.9.refs_3_
  35.7 1.1 %shard_map.61 = (bf16[512,1536]{1,0:T(8,128)(2,1)S(1)}, bf16[512,1536]{1,0:T(8,128)(2,1)S(1)}) custom-call(s32[1]{0:T(128)} %bitcast.3.me_ref, f32[32,1536]{1,0:T(8,128)S(1)} %collective-permute-done.2.refs_0_, f32[32,1536]{1,0:T(8,128)S(1)} %collective-permute-done.4.refs_1_, ...), custom_call_target="tpu_custom_call", output_to_operand_aliasing={{0}: (5, {}), {1}: (6, {})} | custom-call | bytes 1572864 | tf_op jit(solution)/shard_map/pallas_call | solution.py:30
  36.9 0.0 copy-start.3
  36.9 7.8 %shard_map.62 = (f32[2,256,256]{2,1,0:T(8,128)S(1)}, f32[2,256,256]{2,1,0:T(8,128)S(1)}, f32[2,256,256]{2,1,0:T(8,128)S(1)}, f32[2,256,256]{2,1,0:T(8,128)S(1)}) custom-call(s32[2]{0:T(128)S(1)} %pad_add_fusion.at_ref, f32[4,4,64,1536]{3,2,1,0:T(8,128)} %bitcast.4, bf16[512,1536]{1,0:T(8,128)(2,1)S(1)} %get-tuple-element.31.hi_ref, ...), custom_call_target="tpu_custom_call" | custom-call | flops 7247757312 | bytes 6291456 | tf_op jit(solution)/shard_map/pallas_call | solution.py:30
  44.7 0.0 collective-permute-done.10
  44.7 0.0 collective-permute-done.11
  44.7 0.0 collective-permute-done.12
  44.7 0.1 collective-permute-start.13
  44.8 2.6 %collective-permute-start.14 = (f32[2,256,256]{2,1,0:T(8,128)S(1)}, f32[2,256,256]{2,1,0:T(8,128)S(1)}, u32[]{:S(2)}, u32[]{:S(2)}) collective-permute-start(f32[2,256,256]{2,1,0:T(8,128)S(1)} %get-tuple-element.38), channel_id=1, source_target_pairs={{0,3},{1,2},{2,1},{3,0},{4,7},{5,6},{6,5},{7,4},{8,11},{9,10},{10,... | collective-permute-start | bytes 1572872 | tf_op jit(solution)/shard_map/ppermute | solution.py:273
  47.4 6.2 %collective-permute-start.20 = (f32[64,512]{1,0:T(8,128)S(1)}, f32[64,512]{1,0:T(8,128)S(1)}, u32[]{:S(2)}, u32[]{:S(2)}) collective-permute-start(f32[64,512]{1,0:T(8,128)S(1)} %add_add_fusion.1), channel_id=1, source_target_pairs={{136,0},{140,4},{128,8},{132,12},{152,16},{156,20},{144,24},{148,2... | collective-permute-start | bytes 393224 | tf_op jit(solution)/shard_map/ppermute | solution.py:290
  53.6 0.4 collective-permute-start.22
  54.0 2.9 %collective-permute-done.13.a_got = f32[2,256,256]{2,1,0:T(8,128)S(1)} collective-permute-done((f32[2,256,256]{2,1,0:T(8,128)S(1)}, f32[2,256,256]{2,1,0:T(8,128)S(1)}, u32[]{:S(2)}, u32[]{:S(2)}) %collective-permute-start.13) | collective-permute-done | bytes 524320 | tf_op jit(solution)/shard_map/ppermute | solution.py:273
  56.8 1.1 %collective-permute-done.14.b_got = f32[2,256,256]{2,1,0:T(8,128)S(1)} collective-permute-done((f32[2,256,256]{2,1,0:T(8,128)S(1)}, f32[2,256,256]{2,1,0:T(8,128)S(1)}, u32[]{:S(2)}, u32[]{:S(2)}) %collective-permute-start.14) | collective-permute-done | bytes 524320 | tf_op jit(solution)/shard_map/ppermute | solution.py:273
  58.0 0.1 shard_map.63
  58.0 2.7 %collective-permute-start.15 = (f32[256,256]{1,0:T(8,128)S(1)}, f32[256,256]{1,0:T(8,128)S(1)}, u32[]{:S(2)}, u32[]{:S(2)}) collective-permute-start(f32[256,256]{1,0:T(8,128)S(1)} %get-tuple-element.39), channel_id=1, source_target_pairs={{0,3},{1,2},{2,1},{3,0},{4,7},{5,6},{6,5},{7,4},{8,11},{9,10},{10,... | collective-permute-start | bytes 786440 | tf_op jit(solution)/shard_map/ppermute | solution.py:273
  60.8 0.0 collective-permute-start.16
  60.8 0.0 collective-permute-done.20
  60.8 0.8 collective-permute-done.21
  61.6 3.5 %collective-permute-done.22 = f32[64,512]{1,0:T(8,128)S(1)} collective-permute-done((f32[64,512]{1,0:T(8,128)S(1)}, f32[64,512]{1,0:T(8,128)S(1)}, u32[]{:S(2)}, u32[]{:S(2)}) %collective-permute-start.22) | collective-permute-done | bytes 131104 | tf_op jit(solution)/shard_map/ppermute | solution.py:290
  65.2 0.3 collective-permute-start.23
  65.5 2.8 %collective-permute-start.24 = (f32[64,512]{1,0:T(8,128)S(1)}, f32[64,512]{1,0:T(8,128)S(1)}, u32[]{:S(2)}, u32[]{:S(2)}) collective-permute-start(f32[64,512]{1,0:T(8,128)S(1)} %add_add_fusion.refs_0_), channel_id=1, source_target_pairs={{0,64},{16,80},{32,96},{48,112},{64,0},{80,16},{96,32},{112,48},{1... | collective-permute-start | bytes 393224 | tf_op jit(solution)/shard_map/ppermute | solution.py:273
  68.3 0.8 collective-permute-start.25
  69.1 0.2 collective-permute-done.23.refs_1_
  69.3 3.3 %collective-permute-start.26 = (f32[64,512]{1,0:T(8,128)S(1)}, f32[64,512]{1,0:T(8,128)S(1)}, u32[]{:S(2)}, u32[]{:S(2)}) collective-permute-start(f32[64,512]{1,0:T(8,128)S(1)} %add_add_fusion.refs_0_), channel_id=1, source_target_pairs={{0,16},{16,0},{32,48},{48,32},{64,80},{80,64},{96,112},{112,96},{1... | collective-permute-start | bytes 393224 | tf_op jit(solution)/shard_map/ppermute | solution.py:273
  72.6 0.0 collective-permute-done.24.refs_2_
  72.6 3.1 %collective-permute-start.27 = (f32[64,512]{1,0:T(8,128)S(1)}, f32[64,512]{1,0:T(8,128)S(1)}, u32[]{:S(2)}, u32[]{:S(2)}) collective-permute-start(f32[64,512]{1,0:T(8,128)S(1)} %collective-permute-done.23.refs_1_), channel_id=1, source_target_pairs={{0,16},{16,0},{32,48},{48,32},{64,80},{80,64},{96,112},{112,96},{1... | collective-permute-start | bytes 393224 | tf_op jit(solution)/shard_map/ppermute | solution.py:273
  75.7 1.5 %collective-permute-start.28 = (f32[64,512]{1,0:T(8,128)S(1)}, f32[64,512]{1,0:T(8,128)S(1)}, u32[]{:S(2)}, u32[]{:S(2)}) collective-permute-start(f32[64,512]{1,0:T(8,128)S(1)} %collective-permute-done.24.refs_2_), channel_id=1, source_target_pairs={{0,16},{16,0},{32,48},{48,32},{64,80},{80,64},{96,112},{112,96},{1... | collective-permute-start | bytes 393224 | tf_op jit(solution)/shard_map/ppermute | solution.py:273
  77.2 0.0 collective-permute-start.29
  77.2 0.0 collective-permute-done.16.b_last
  77.2 0.1 shard_map.64
  77.3 1.0 %collective-permute-start.17 = (f32[64,512]{1,0:T(8,128)S(1)}, f32[64,512]{1,0:T(8,128)S(1)}, u32[]{:S(2)}, u32[]{:S(2)}) collective-permute-start(f32[64,512]{1,0:T(8,128)S(1)} %get-tuple-element.42), channel_id=1, source_target_pairs={{0,4},{4,0},{8,12},{12,8},{1,5},{5,1},{9,13},{13,9},{2,6},{6,2},{1... | collective-permute-start | bytes 393224 | tf_op jit(solution)/shard_map/ppermute | solution.py:273
  78.3 4.0 %collective-permute-start.18 = (f32[64,512]{1,0:T(8,128)S(1)}, f32[64,512]{1,0:T(8,128)S(1)}, u32[]{:S(2)}, u32[]{:S(2)}) collective-permute-start(f32[64,512]{1,0:T(8,128)S(1)} %get-tuple-element.43), channel_id=1, source_target_pairs={{0,8},{4,12},{8,0},{12,4},{1,9},{5,13},{9,1},{13,5},{2,10},{6,14},... | collective-permute-start | bytes 393224 | tf_op jit(solution)/shard_map/ppermute | solution.py:273
  82.3 0.8 collective-permute-start.19
  83.1 14.7 %shard_map.65 = (f32[512,512]{1,0:T(8,128)}, f32[512,512]{1,0:T(8,128)S(1)}) custom-call(s32[1]{0:T(128)} %bitcast.3.me_ref, f32[512,512]{1,0:T(8,128)S(1)} %copy-done.4, f32[64,512]{1,0:T(8,128)S(1)} %add_add_fusion.refs_0_, f32[64,512]{1,0:T(8,128)S(1)} %collective-permute-done.23.refs_1_, f32[64,512]{1,0:T(8,128)S(1)} %collective-permute-done.24.refs_2_, ...), custom_call_target="tpu_custom_call" | custom-call | flops 16106127360 | bytes 4194304 | tf_op jit(solution)/shard_map/pallas_call | solution.py:30
  97.8 0.0 collective-permute-done.17.p1
  97.8 0.0 collective-permute-done.18.p2
  97.8 1.3 %shard_map.66 = f32[64,512]{1,0:T(8,128)} custom-call(f32[64,512]{1,0:T(8,128)S(1)} %copy-done.1, f32[64,512]{1,0:T(8,128)S(1)} %get-tuple-element.41.p0, f32[64,512]{1,0:T(8,128)S(1)} %collective-permute-done.17.p1, f32[64,512]{1,0:T(8,128)S(1)} %collective-permute-done.18.p2, f32[64,512]{1,0:T(8,128)S(1)} %collective-permute-done.19.p3, ...), custom_call_target="tpu_custom_call" | custom-call | flops 100663296 | bytes 2097152 | tf_op jit(solution)/shard_map/pallas_call | solution.py:30
  (19 shorter events, 0.2 us)
Async XLA Ops:
  0.6 6.4 %collective-permute-start = (f32[32,1536]{1,0:T(8,128)}, f32[32,1536]{1,0:T(8,128)S(1)}, u32[]{:S(2)}, u32[]{:S(2)}) collective-permute-start(f32[32,1536]{1,0:T(8,128)} %mine_ref.1), channel_id=1, source_target_pairs={{0,128},{16,144},{32,160},{48,176},{64,192},{80,208},{96,224},{112... | collective-permute-start | bytes 589832 | tf_op jit(solution)/shard_map/ppermute | solution.py:273
  7.1 0.9 copy-start
  8.0 9.3 %collective-permute-start.3 = (f32[64,1536]{1,0:T(8,128)S(1)}, f32[64,1536]{1,0:T(8,128)S(1)}, u32[]{:S(2)}, u32[]{:S(2)}) collective-permute-start(f32[64,1536]{1,0:T(8,128)S(1)} %shard_map.59.refs_0_), channel_id=1, source_target_pairs={{0,32},{16,48},{32,0},{48,16},{64,96},{80,112},{96,64},{112,80},{1... | collective-permute-start | bytes 1179656 | tf_op jit(solution)/shard_map/ppermute | solution.py:273
  10.3 10.2 %collective-permute-start.1 = (f32[64,1536]{1,0:T(8,128)S(1)}, f32[64,1536]{1,0:T(8,128)S(1)}, u32[]{:S(2)}, u32[]{:S(2)}) collective-permute-start(f32[64,1536]{1,0:T(8,128)S(1)} %shard_map.59.refs_0_), channel_id=1, source_target_pairs={{0,96},{16,112},{32,64},{48,80},{64,32},{80,48},{96,0},{112,16},{1... | collective-permute-start | bytes 1179656 | tf_op jit(solution)/shard_map/ppermute | solution.py:273
  12.2 13.0 %collective-permute-start.5 = (f32[64,1536]{1,0:T(8,128)S(1)}, f32[64,1536]{1,0:T(8,128)S(1)}, u32[]{:S(2)}, u32[]{:S(2)}) collective-permute-start(f32[64,1536]{1,0:T(8,128)S(1)} %shard_map.59.refs_0_), channel_id=1, source_target_pairs={{0,16},{16,0},{32,48},{48,32},{64,80},{80,64},{96,112},{112,96},{1... | collective-permute-start | bytes 1179656 | tf_op jit(solution)/shard_map/ppermute | solution.py:273
  17.3 7.8 %collective-permute-start.6 = (f32[64,1536]{1,0:T(8,128)S(1)}, f32[64,1536]{1,0:T(8,128)S(1)}, u32[]{:S(2)}, u32[]{:S(2)}) collective-permute-start(f32[64,1536]{1,0:T(8,128)S(1)} %collective-permute-done.3.refs_1_), channel_id=1, source_target_pairs={{0,16},{16,0},{32,48},{48,32},{64,80},{80,64},{96,112},{112,96},{1... | collective-permute-start | bytes 1179656 | tf_op jit(solution)/shard_map/ppermute | solution.py:273
  20.4 4.7 %collective-permute-start.7 = (f32[64,1536]{1,0:T(8,128)S(1)}, f32[64,1536]{1,0:T(8,128)S(1)}, u32[]{:S(2)}, u32[]{:S(2)}) collective-permute-start(f32[64,1536]{1,0:T(8,128)S(1)} %collective-permute-done.1.refs_2_), channel_id=1, source_target_pairs={{0,16},{16,0},{32,48},{48,32},{64,80},{80,64},{96,112},{112,96},{1... | collective-permute-start | bytes 1179656 | tf_op jit(solution)/shard_map/ppermute | solution.py:273
  23.0 6.6 %collective-permute-start.2 = (f32[32,1536]{1,0:T(8,128)S(1)}, f32[32,1536]{1,0:T(8,128)S(1)}, u32[]{:S(2)}, u32[]{:S(2)}) collective-permute-start(f32[32,1536]{1,0:T(8,128)S(1)} %slice.8), channel_id=1, source_target_pairs={{0,32},{16,48},{32,0},{48,16},{64,96},{80,112},{96,64},{112,80},{1... | collective-permute-start | bytes 589832 | tf_op jit(solution)/shard_map/ppermute | solution.py:273
  23.1 7.8 %collective-permute-start.4 = (f32[32,1536]{1,0:T(8,128)S(1)}, f32[32,1536]{1,0:T(8,128)S(1)}, u32[]{:S(2)}, u32[]{:S(2)}) collective-permute-start(f32[32,1536]{1,0:T(8,128)S(1)} %slice.9), channel_id=1, source_target_pairs={{0,96},{16,112},{32,64},{48,80},{64,32},{80,48},{96,0},{112,16},{1... | collective-permute-start | bytes 589832 | tf_op jit(solution)/shard_map/ppermute | solution.py:273
  27.3 0.7 copy-start.2
  31.0 4.7 %collective-permute-start.8 = (f32[32,1536]{1,0:T(8,128)S(1)}, f32[32,1536]{1,0:T(8,128)}, u32[]{:S(2)}, u32[]{:S(2)}) collective-permute-start(f32[32,1536]{1,0:T(8,128)S(1)} %collective-permute-done.2.refs_0_), channel_id=1, source_target_pairs={{0,16},{16,0},{32,48},{48,32},{64,80},{80,64},{96,112},{112,96},{1... | collective-permute-start | bytes 589832 | tf_op jit(solution)/shard_map/ppermute | solution.py:273
  31.7 4.0 %collective-permute-start.9 = (f32[32,1536]{1,0:T(8,128)S(1)}, f32[32,1536]{1,0:T(8,128)}, u32[]{:S(2)}, u32[]{:S(2)}) collective-permute-start(f32[32,1536]{1,0:T(8,128)S(1)} %collective-permute-done.4.refs_1_), channel_id=1, source_target_pairs={{0,16},{16,0},{32,48},{48,32},{64,80},{80,64},{96,112},{112,96},{1... | collective-permute-start | bytes 589832 | tf_op jit(solution)/shard_map/ppermute | solution.py:273
  31.8 12.8 %collective-permute-start.10 = (f32[64,512]{1,0:T(8,128)}, f32[64,512]{1,0:T(8,128)S(1)}, u32[]{:S(2)}, u32[]{:S(2)}) collective-permute-start(f32[64,512]{1,0:T(8,128)} %copy-done.2), channel_id=1, source_target_pairs={{0,1},{1,0},{2,3},{3,2},{4,5},{5,4},{6,7},{7,6},{8,9},{9,8},{10,11... | collective-permute-start | bytes 393224 | tf_op jit(solution)/shard_map/ppermute | solution.py:273
  33.1 11.6 %collective-permute-start.11 = (f32[64,512]{1,0:T(8,128)}, f32[64,512]{1,0:T(8,128)S(1)}, u32[]{:S(2)}, u32[]{:S(2)}) collective-permute-start(f32[64,512]{1,0:T(8,128)} %copy-done.2), channel_id=1, source_target_pairs={{0,2},{1,3},{2,0},{3,1},{4,6},{5,7},{6,4},{7,5},{8,10},{9,11},{10,... | collective-permute-start | bytes 393224 | tf_op jit(solution)/shard_map/ppermute | solution.py:273
  35.5 9.2 %collective-permute-start.12 = (f32[64,512]{1,0:T(8,128)}, f32[64,512]{1,0:T(8,128)S(1)}, u32[]{:S(2)}, u32[]{:S(2)}) collective-permute-start(f32[64,512]{1,0:T(8,128)} %copy-done.2), channel_id=1, source_target_pairs={{0,3},{1,2},{2,1},{3,0},{4,7},{5,6},{6,5},{7,4},{8,11},{9,10},{10,... | collective-permute-start | bytes 393224 | tf_op jit(solution)/shard_map/ppermute | solution.py:273
  36.9 10.5 %copy-start.3 = (f32[64,512]{1,0:T(8,128)S(1)}, f32[64,512]{1,0:T(8,128)}, u32[]{:S(2)}) copy-start(f32[64,512]{1,0:T(8,128)} %copy-done.2) | copy-start | bytes 393220
  44.7 12.2 %collective-permute-start.13 = (f32[2,256,256]{2,1,0:T(8,128)S(1)}, f32[2,256,256]{2,1,0:T(8,128)S(1)}, u32[]{:S(2)}, u32[]{:S(2)}) collective-permute-start(f32[2,256,256]{2,1,0:T(8,128)S(1)} %get-tuple-element.36), channel_id=1, source_target_pairs={{0,1},{1,0},{2,3},{3,2},{4,5},{5,4},{6,7},{7,6},{8,9},{9,8},{10,11... | collective-permute-start | bytes 1572872 | tf_op jit(solution)/shard_map/ppermute | solution.py:273
  44.8 13.2 %collective-permute-start.14 = (f32[2,256,256]{2,1,0:T(8,128)S(1)}, f32[2,256,256]{2,1,0:T(8,128)S(1)}, u32[]{:S(2)}, u32[]{:S(2)}) collective-permute-start(f32[2,256,256]{2,1,0:T(8,128)S(1)} %get-tuple-element.38), channel_id=1, source_target_pairs={{0,3},{1,2},{2,1},{3,0},{4,7},{5,6},{6,5},{7,4},{8,11},{9,10},{10,... | collective-permute-start | bytes 1572872 | tf_op jit(solution)/shard_map/ppermute | solution.py:273
  47.4 13.4 %collective-permute-start.20 = (f32[64,512]{1,0:T(8,128)S(1)}, f32[64,512]{1,0:T(8,128)S(1)}, u32[]{:S(2)}, u32[]{:S(2)}) collective-permute-start(f32[64,512]{1,0:T(8,128)S(1)} %add_add_fusion.1), channel_id=1, source_target_pairs={{136,0},{140,4},{128,8},{132,12},{152,16},{156,20},{144,24},{148,2... | collective-permute-start | bytes 393224 | tf_op jit(solution)/shard_map/ppermute | solution.py:290
  53.6 8.0 %collective-permute-start.21 = (f32[64,512]{1,0:T(8,128)S(1)}, f32[64,512]{1,0:T(8,128)S(1)}, u32[]{:S(2)}, u32[]{:S(2)}) collective-permute-start(f32[64,512]{1,0:T(8,128)S(1)} %add_add_fusion.1), channel_id=1, source_target_pairs={{140,0},{128,4},{132,8},{136,12},{156,16},{144,20},{148,24},{152,2... | collective-permute-start | bytes 393224 | tf_op jit(solution)/shard_map/ppermute | solution.py:290
  53.6 11.5 %collective-permute-start.22 = (f32[64,512]{1,0:T(8,128)S(1)}, f32[64,512]{1,0:T(8,128)S(1)}, u32[]{:S(2)}, u32[]{:S(2)}) collective-permute-start(f32[64,512]{1,0:T(8,128)S(1)} %add_add_fusion.1), channel_id=1, source_target_pairs={{4,0},{8,4},{12,8},{0,12},{20,16},{24,20},{28,24},{16,28},{36,32},... | collective-permute-start | bytes 393224 | tf_op jit(solution)/shard_map/ppermute | solution.py:290
  58.0 19.2 %collective-permute-start.15 = (f32[256,256]{1,0:T(8,128)S(1)}, f32[256,256]{1,0:T(8,128)S(1)}, u32[]{:S(2)}, u32[]{:S(2)}) collective-permute-start(f32[256,256]{1,0:T(8,128)S(1)} %get-tuple-element.39), channel_id=1, source_target_pairs={{0,3},{1,2},{2,1},{3,0},{4,7},{5,6},{6,5},{7,4},{8,11},{9,10},{10,... | collective-permute-start | bytes 786440 | tf_op jit(solution)/shard_map/ppermute | solution.py:273
  60.8 22.3 %copy-start.4 = (f32[512,512]{1,0:T(8,128)S(1)}, f32[512,512]{1,0:T(8,128)}, u32[]{:S(2)}) copy-start(f32[512,512]{1,0:T(8,128)} %diag_ref.1) | copy-start | bytes 3145732
  60.8 16.4 %collective-permute-start.16 = (f32[256,256]{1,0:T(8,128)S(1)}, f32[256,256]{1,0:T(8,128)S(1)}, u32[]{:S(2)}, u32[]{:S(2)}) collective-permute-start(f32[256,256]{1,0:T(8,128)S(1)} %get-tuple-element.40), channel_id=1, source_target_pairs={{0,1},{1,0},{2,3},{3,2},{4,5},{5,4},{6,7},{7,6},{8,9},{9,8},{10,11... | collective-permute-start | bytes 786440 | tf_op jit(solution)/shard_map/ppermute | solution.py:273
  65.2 4.1 %collective-permute-start.23 = (f32[64,512]{1,0:T(8,128)S(1)}, f32[64,512]{1,0:T(8,128)S(1)}, u32[]{:S(2)}, u32[]{:S(2)}) collective-permute-start(f32[64,512]{1,0:T(8,128)S(1)} %add_add_fusion.refs_0_), channel_id=1, source_target_pairs={{0,32},{16,48},{32,0},{48,16},{64,96},{80,112},{96,64},{112,80},{1... | collective-permute-start | bytes 393224 | tf_op jit(solution)/shard_map/ppermute | solution.py:273
  65.5 7.1 %collective-permute-start.24 = (f32[64,512]{1,0:T(8,128)S(1)}, f32[64,512]{1,0:T(8,128)S(1)}, u32[]{:S(2)}, u32[]{:S(2)}) collective-permute-start(f32[64,512]{1,0:T(8,128)S(1)} %add_add_fusion.refs_0_), channel_id=1, source_target_pairs={{0,64},{16,80},{32,96},{48,112},{64,0},{80,16},{96,32},{112,48},{1... | collective-permute-start | bytes 393224 | tf_op jit(solution)/shard_map/ppermute | solution.py:273
  68.3 7.4 %collective-permute-start.25 = (f32[64,512]{1,0:T(8,128)S(1)}, f32[64,512]{1,0:T(8,128)S(1)}, u32[]{:S(2)}, u32[]{:S(2)}) collective-permute-start(f32[64,512]{1,0:T(8,128)S(1)} %add_add_fusion.refs_0_), channel_id=1, source_target_pairs={{0,96},{16,112},{32,64},{48,80},{64,32},{80,48},{96,0},{112,16},{1... | collective-permute-start | bytes 393224 | tf_op jit(solution)/shard_map/ppermute | solution.py:273
  69.3 9.0 %collective-permute-start.26 = (f32[64,512]{1,0:T(8,128)S(1)}, f32[64,512]{1,0:T(8,128)S(1)}, u32[]{:S(2)}, u32[]{:S(2)}) collective-permute-start(f32[64,512]{1,0:T(8,128)S(1)} %add_add_fusion.refs_0_), channel_id=1, source_target_pairs={{0,16},{16,0},{32,48},{48,32},{64,80},{80,64},{96,112},{112,96},{1... | collective-permute-start | bytes 393224 | tf_op jit(solution)/shard_map/ppermute | solution.py:273
  72.6 9.6 %collective-permute-start.27 = (f32[64,512]{1,0:T(8,128)S(1)}, f32[64,512]{1,0:T(8,128)S(1)}, u32[]{:S(2)}, u32[]{:S(2)}) collective-permute-start(f32[64,512]{1,0:T(8,128)S(1)} %collective-permute-done.23.refs_1_), channel_id=1, source_target_pairs={{0,16},{16,0},{32,48},{48,32},{64,80},{80,64},{96,112},{112,96},{1... | collective-permute-start | bytes 393224 | tf_op jit(solution)/shard_map/ppermute | solution.py:273
  75.7 7.3 %collective-permute-start.28 = (f32[64,512]{1,0:T(8,128)S(1)}, f32[64,512]{1,0:T(8,128)S(1)}, u32[]{:S(2)}, u32[]{:S(2)}) collective-permute-start(f32[64,512]{1,0:T(8,128)S(1)} %collective-permute-done.24.refs_2_), channel_id=1, source_target_pairs={{0,16},{16,0},{32,48},{48,32},{64,80},{80,64},{96,112},{112,96},{1... | collective-permute-start | bytes 393224 | tf_op jit(solution)/shard_map/ppermute | solution.py:273
  77.2 5.9 %collective-permute-start.29 = (f32[64,512]{1,0:T(8,128)S(1)}, f32[64,512]{1,0:T(8,128)S(1)}, u32[]{:S(2)}, u32[]{:S(2)}) collective-permute-start(f32[64,512]{1,0:T(8,128)S(1)} %collective-permute-done.25.refs_3_), channel_id=1, source_target_pairs={{0,16},{16,0},{32,48},{48,32},{64,80},{80,64},{96,112},{112,96},{1... | collective-permute-start | bytes 393224 | tf_op jit(solution)/shard_map/ppermute | solution.py:273
  77.3 20.5 %collective-permute-start.17 = (f32[64,512]{1,0:T(8,128)S(1)}, f32[64,512]{1,0:T(8,128)S(1)}, u32[]{:S(2)}, u32[]{:S(2)}) collective-permute-start(f32[64,512]{1,0:T(8,128)S(1)} %get-tuple-element.42), channel_id=1, source_target_pairs={{0,4},{4,0},{8,12},{12,8},{1,5},{5,1},{9,13},{13,9},{2,6},{6,2},{1... | collective-permute-start | bytes 393224 | tf_op jit(solution)/shard_map/ppermute | solution.py:273
  78.3 19.5 %collective-permute-start.18 = (f32[64,512]{1,0:T(8,128)S(1)}, f32[64,512]{1,0:T(8,128)S(1)}, u32[]{:S(2)}, u32[]{:S(2)}) collective-permute-start(f32[64,512]{1,0:T(8,128)S(1)} %get-tuple-element.43), channel_id=1, source_target_pairs={{0,8},{4,12},{8,0},{12,4},{1,9},{5,13},{9,1},{13,5},{2,10},{6,14},... | collective-permute-start | bytes 393224 | tf_op jit(solution)/shard_map/ppermute | solution.py:273
  82.3 15.5 %copy-start.1 = (f32[64,512]{1,0:T(8,128)S(1)}, f32[64,512]{1,0:T(8,128)}, u32[]{:S(2)}) copy-start(f32[64,512]{1,0:T(8,128)} %below_ref.1) | copy-start | bytes 393220
  82.3 15.5 %collective-permute-start.19 = (f32[64,512]{1,0:T(8,128)S(1)}, f32[64,512]{1,0:T(8,128)S(1)}, u32[]{:S(2)}, u32[]{:S(2)}) collective-permute-start(f32[64,512]{1,0:T(8,128)S(1)} %get-tuple-element.44), channel_id=1, source_target_pairs={{0,12},{4,8},{8,4},{12,0},{1,13},{5,9},{9,5},{13,1},{2,14},{6,10},... | collective-permute-start | bytes 393224 | tf_op jit(solution)/shard_map/ppermute | solution.py:273
